TPU v7x, 512 devices: a whole 4x8x8 slice. The times are simulated.
512 devices in a mesh: ctx: 64 (over z, x, core), head: 8 (over y).
Axes of the slice: x: 4, y: 8, z: 8, core: 2. Of those that a mesh axis runs over, the one named last changes fastest.
Arguments:
- query_rows: bfloat16 [8192, 2048], P('ctx', 'head'), may hold values from -120 to 120
- key_rows: bfloat16 [8192, 2048], P('ctx', 'head'), may hold values from -4 to 4
- value_rows: bfloat16 [8192, 2048], P('ctx', 'head'), may hold values from -6 to 6
- reflect_dirs: bfloat16 [8192, 2048], P('ctx', 'head'), may hold values from -6 to 6
- reflect_rates: float32 [16, 8192], P('head', 'ctx'), may hold values from 0.02 to 1.98
- norm_gain: float32 [2048], P('head'), may hold values from 0.5 to 1.5
- doc_lengths: int32 [32], replicated, may hold values from 1 to 512, 8192 in all
- out_cotangent: bfloat16 [8192, 2048], P('ctx', 'head'), may hold values from -6 to 6
Outputs:
- normed_out: bfloat16 [8192, 2048], P('ctx', 'head')
- grad_query: bfloat16 [8192, 2048], P('ctx', 'head')
- grad_key: bfloat16 [8192, 2048], P('ctx', 'head')
- grad_value: bfloat16 [8192, 2048], P('ctx', 'head')
- grad_reflect: bfloat16 [8192, 2048], P('ctx', 'head')
- grad_rate: float32 [16, 8192], P('head', 'ctx')
- grad_gain: float32 [2048], P('head')
Inputs may be any that keep to these rules, and one draw needn't show every extreme that they name: `doc_lengths`: every document has at most 512 tokens and one has exactly that many; the lengths sum to 8192.
All inputs are finite; a program needn't handle non-finite values.
Results may differ from a plain program's by a relative error of at most 0.018.
Values may be sent and summed in bfloat16 or wider, within the bound.
No kernel may reach another device: no remote copies, remote signals or barrier semaphores. Data moves between devices by JAX's collectives and lax.ppermute only.
A program may use at most 128 MiB of HBM per device.

v0:
```python
import jax
import jax.numpy as jnp
from jax import lax
from jax.sharding import PartitionSpec as P

DH = 128
WIN = 4


NEG_FILL = -1e30
EPSILON = 1e-06


def passed_along(value, axis, steps):
    count = lax.axis_size(axis)
    first, last = (max(0, -steps), min(count, count - steps))
    return lax.ppermute(value, axis, [(source, source + steps) for source in range(first, last)])


def exact_dot(left, right):
    return jnp.dot(left, right, precision=lax.Precision.HIGHEST)


def exact_sum(form, left, right):
    return jnp.einsum(form, left, right, precision=lax.Precision.HIGHEST)


def unit_lower_inverse(matrix):
    length_rows = matrix.shape[0]
    padded_size = 1 << (length_rows - 1).bit_length()
    full = jnp.eye(padded_size, dtype=jnp.float32) + (
        matrix - jnp.eye(length_rows, dtype=jnp.float32)
    )
    inverse_blocks = jnp.ones((padded_size, 1, 1), jnp.float32)
    block_width = 1
    while block_width < padded_size:
        groups = padded_size // (2 * block_width)
        diagonal_blocks = jnp.einsum(
            "aibj,ab->aij",
            full.reshape(groups, 2 * block_width, groups, 2 * block_width),
            jnp.eye(groups, dtype=jnp.float32),
            precision=lax.Precision.HIGHEST,
        )
        paired = inverse_blocks.reshape(groups, 2, block_width, block_width)
        first_inverse = paired[:, 0]
        second_inverse = paired[:, 1]
        coupling = diagonal_blocks[:, block_width:, :block_width]
        corner_block = -exact_sum(
            "aij,ajk->aik", second_inverse, exact_sum("aij,ajk->aik", coupling, first_inverse)
        )
        upper_rows = jnp.concatenate([first_inverse, jnp.zeros_like(first_inverse)], axis=2)
        lower_rows = jnp.concatenate([corner_block, second_inverse], axis=2)
        inverse_blocks = jnp.concatenate([upper_rows, lower_rows], axis=1)
        block_width = 2 * block_width
    return inverse_blocks[0]


def shard_prepare(query_block, key_block, mixer_block, rate_block):
    query_float = query_block.astype(jnp.float32)
    key_float = key_block.astype(jnp.float32)
    mixer_float = mixer_block.astype(jnp.float32)
    direction = mixer_float * lax.rsqrt(
        jnp.sum(mixer_float * mixer_float, axis=1, keepdims=True) + EPSILON
    )
    length = direction.shape[0]
    identity = jnp.eye(length, dtype=jnp.float32)
    gram_rates = rate_block[:, None] * exact_dot(direction, direction.T)
    lower_mat = identity + jnp.tril(gram_rates, -1)
    upper_mat = identity + jnp.triu(gram_rates, 1)
    lower_inverse = unit_lower_inverse(lower_mat)
    upper_inverse = unit_lower_inverse(upper_mat.T).T
    key_coef = exact_dot(
        lower_inverse, jnp.tril(rate_block[:, None] * exact_dot(direction, key_float.T), -1)
    )
    query_dir = exact_dot(query_float, direction.T)
    intra_raw = jnp.tril(
        exact_dot(query_float, key_float.T) - exact_dot(jnp.tril(query_dir), key_coef)
    )
    key_end = key_float - exact_dot(key_coef.T, direction)
    query_coef = exact_dot(upper_inverse, jnp.triu(rate_block[:, None] * query_dir.T))
    query_frame = query_float - exact_dot(query_coef.T, direction)
    applied = exact_dot(lower_inverse, rate_block[:, None] * direction)
    transform = jnp.eye(direction.shape[1], dtype=jnp.float32) - exact_dot(direction.T, applied)
    return (intra_raw, query_frame, key_end, transform)


def document_of(positions, doc_ends):
    return jnp.sum((doc_ends[None, :] <= positions[:, None]).astype(jnp.int32), axis=1)


def per_device(
    query_rows,
    key_rows,
    value_rows,
    reflect_dirs,
    reflect_rates,
    norm_gain,
    doc_lengths,
    out_cotangent,
):
    row_count = query_rows.shape[0]
    head_count = query_rows.shape[1] // DH
    features = head_count * DH * lax.axis_size("head")
    score_scale = DH ** (-0.5)

    def split_heads(tensor):
        return tensor.reshape(row_count, head_count, DH).transpose(1, 0, 2)

    def join_heads(tensor):
        return tensor.transpose(1, 0, 2).reshape(row_count, head_count * DH)

    prepared, prepare_back = jax.vjp(
        jax.vmap(shard_prepare),
        split_heads(query_rows),
        split_heads(key_rows),
        split_heads(reflect_dirs),
        reflect_rates,
    )
    intra_raw, query_frame, key_end, transform = prepared
    first_token = lax.axis_index("ctx") * row_count
    query_pos = first_token + jnp.arange(row_count, dtype=jnp.int32)
    doc_ends = jnp.cumsum(doc_lengths)
    query_doc = document_of(query_pos, doc_ends)
    seen_masks = [
        (query_pos[:, None] >= query_pos[None, :]) & (query_doc[:, None] == query_doc[None, :])
    ]
    value_list = [split_heads(value_rows)]
    for offset in range(1, WIN + 1):
        key_pos = query_pos - offset * row_count
        seen_masks.append(
            (key_pos[None, :] >= 0)
            & (query_doc[:, None] == document_of(key_pos, doc_ends)[None, :])
        )
        value_list.append(split_heads(passed_along(value_rows, "ctx", offset)))
    left_ops = []
    right_ops = []
    outgoing = key_end
    for offset in range(1, WIN + 1):
        received = passed_along(outgoing, "ctx", 1)
        left_ops.append(query_frame)
        right_ops.append(received)
        if offset < WIN:
            outgoing = exact_sum("htd,hed->hte", received, transform)
    score_list = []
    for position in range(WIN + 1):
        if position == 0:
            raw_scores = intra_raw
        else:
            raw_scores = exact_sum("htd,hud->htu", left_ops[position - 1], right_ops[position - 1])
        score_list.append(jnp.where(seen_masks[position][None], raw_scores * score_scale, NEG_FILL))
    row_max = jnp.full((head_count, row_count), NEG_FILL, jnp.float32)
    for position in range(WIN + 1):
        row_max = jnp.maximum(row_max, jnp.max(score_list[position], axis=2))
    weight_list = []
    prob_total = jnp.zeros((head_count, row_count), jnp.float32)
    numerator = jnp.zeros((head_count, row_count, DH), jnp.float32)
    for position in range(WIN + 1):
        exp_weights = jnp.where(
            seen_masks[position][None], jnp.exp(score_list[position] - row_max[:, :, None]), 0.0
        )
        weight_list.append(exp_weights)
        prob_total = prob_total + jnp.sum(exp_weights, axis=2)
        numerator = numerator + jnp.einsum(
            "htu,hud->htd",
            exp_weights.astype(jnp.bfloat16),
            value_list[position],
            preferred_element_type=jnp.float32,
        )
    attended_heads = numerator / prob_total[:, :, None]
    attended = join_heads(attended_heads)
    square = lax.psum(jnp.sum(attended * attended, axis=1), "head")
    inverse_rms = lax.rsqrt(square / features + EPSILON)
    normed_out = (attended * inverse_rms[:, None] * norm_gain[None, :]).astype(jnp.bfloat16)
    cotangent = out_cotangent.astype(jnp.float32)
    weighted = cotangent * norm_gain[None, :]
    inner_sum = lax.psum(jnp.sum(weighted * attended, axis=1), "head")
    grad_att = (
        weighted * inverse_rms[:, None]
        - attended * (inverse_rms**3 * inner_sum / features)[:, None]
    )
    grad_gain = lax.psum(jnp.sum(cotangent * attended * inverse_rms[:, None], axis=0), "ctx")
    grad_heads = split_heads(grad_att)
    grad_scaled = (grad_heads / prob_total[:, :, None]).astype(jnp.bfloat16)
    row_delta = jnp.sum(grad_heads * attended_heads, axis=2) / prob_total
    value_grads = []
    left_grads = []
    right_grads = []
    intra_grad = None
    for position in range(WIN + 1):
        exp_weights = weight_list[position]
        value_grads.append(
            jnp.einsum(
                "htu,htd->hud",
                exp_weights.astype(jnp.bfloat16),
                grad_scaled,
                preferred_element_type=jnp.float32,
            )
        )
        through = jnp.einsum(
            "htd,hud->htu", grad_scaled, value_list[position], preferred_element_type=jnp.float32
        )
        score_grad = exp_weights * (through - row_delta[:, :, None]) * score_scale
        if position == 0:
            intra_grad = score_grad
        else:
            left_grads.append(exact_sum("htu,hud->htd", score_grad, right_ops[position - 1]))
            right_grads.append(exact_sum("htu,htd->hud", score_grad, left_ops[position - 1]))
    value_far = jnp.zeros_like(value_grads[0])
    frame_grad = left_grads[0]
    for slot_index in range(1, WIN):
        frame_grad = frame_grad + left_grads[slot_index]
    carried = jnp.zeros_like(key_end)
    trans_grad = jnp.zeros_like(transform)
    for offset in range(WIN, 0, -1):
        grad_recv = right_grads[offset - 1] + exact_sum("hte,hed->htd", carried, transform)
        trans_grad = trans_grad + exact_sum("hte,htd->hed", carried, right_ops[offset - 1])
        carried = passed_along(grad_recv.astype(jnp.bfloat16), "ctx", -1).astype(grad_recv.dtype)
    for offset in range(1, WIN + 1):
        value_far = value_far + passed_along(
            value_grads[offset].astype(jnp.bfloat16), "ctx", -offset
        ).astype(jnp.float32)
    query_grad, key_in_grad, mixer_grad, rate_grad = prepare_back(
        (intra_grad, frame_grad, carried, trans_grad)
    )
    grad_value = join_heads(value_grads[0] + value_far).astype(jnp.bfloat16)
    return (
        normed_out,
        join_heads(query_grad),
        join_heads(key_in_grad),
        grad_value,
        join_heads(mixer_grad),
        rate_grad,
        grad_gain,
    )


def solution(mesh):
    return jax.shard_map(
        per_device,
        mesh=mesh,
        in_specs=(
            P("ctx", "head"),
            P("ctx", "head"),
            P("ctx", "head"),
            P("ctx", "head"),
            P("head", "ctx"),
            P("head"),
            P(),
            P("ctx", "head"),
        ),
        out_specs=(
            P("ctx", "head"),
            P("ctx", "head"),
            P("ctx", "head"),
            P("ctx", "head"),
            P("ctx", "head"),
            P("head", "ctx"),
            P("head"),
        ),
        check_vma=False,
    )
```

profile of v0, /device:TPU:199, one launch (start us, length us, event | category | flops | bytes accessed | tf_op | source)
XLA Modules:
  0.0 504.3 jit_solution(18141806317304957531)
XLA Ops:
  0.6 5.1 %collective-permute-start.5 = (bf16[128,256]{1,0:T(8,128)(2,1)}, bf16[128,256]{1,0:T(8,128)(2,1)}, u32[]{:S(2)}, u32[]{:S(2)}) collective-permute-start(bf16[128,256]{1,0:T(8,128)(2,1)} %param.10), channel_id=1, source_target_pairs={{0,16},{8,24},{16,32},{24,40},{32,48},{40,56},{48,64},{56,72},{64,... | collective-permute-start | bytes 196616 | tf_op jit(solution)/shard_map/ppermute | solution.py:17
  5.8 4.0 collective-permute-start.4
  9.7 3.8 collective-permute-start.7
  27.9 6.2 %reshape.694 = f32[2,32,4,32,4]{4,3,2,1,0:T(8,128)} reshape(f32[2,128,128]{2,1,0:T(8,128)S(1)} %subtract_add_fusion) | data formatting | bytes 262144 | tf_op jit(solution)/shard_map/jvp(vmap())/reshape | solution.py:40
  34.2 9.8 %reshape.692 = f32[2,64,2,64,2]{4,3,2,1,0:T(8,128)} reshape(f32[2,128,128]{2,1,0:T(8,128)S(1)} %subtract_add_fusion) | data formatting | bytes 262144 | tf_op jit(solution)/shard_map/jvp(vmap())/reshape | solution.py:40
  55.6 3.7 fusion.6
  62.3 9.9 %reshape.707 = f32[2,64,2,64,2]{4,3,2,1,0:T(8,128)} reshape(f32[2,128,128]{2,1,0:T(8,128)S(1)} %get-tuple-element.67) | data formatting | bytes 262144 | tf_op jit(solution)/shard_map/jvp(vmap())/reshape | solution.py:40
  72.3 6.2 %fusion = f32[64,1,2,2,2]{4,1,3,2,0:T(1,128)S(1)} fusion(f32[2,64,2,64,2]{4,3,2,1,0:T(8,128)} %reshape.707, pred[64,64,1,1,1]{1,0,2,3,4:T(32,128)(4,1)S(1)} %copy-done.44), kind=kOutput, calls=%fused_computation | convolution fusion | flops 393216 | bytes 137216 | tf_op jit(solution)/shard_map/jvp(vmap(aibj,ab->aij))/dot_general | solution.py:38
  88.1 3.4 collective-permute-start
  100.8 6.1 %reshape.709 = f32[2,32,4,32,4]{4,3,2,1,0:T(8,128)} reshape(f32[2,128,128]{2,1,0:T(8,128)S(1)} %get-tuple-element.67) | data formatting | bytes 262144 | tf_op jit(solution)/shard_map/jvp(vmap())/reshape | solution.py:40
  144.9 7.8 %collective-permute-start.2 = (f32[2,128,128]{2,1,0:T(8,128)S(1)}, f32[2,128,128]{2,1,0:T(8,128)S(1)}, u32[]{:S(2)}, u32[]{:S(2)}) collective-permute-start(f32[2,128,128]{2,1,0:T(8,128)S(1)} %fusion.373), channel_id=1, source_target_pairs={{0,8},{8,16},{16,24},{24,32},{32,40},{40,48},{48,56},{56,64},{64,7... | collective-permute-start | bytes 393224 | tf_op jit(solution)/shard_map/ppermute | solution.py:17
  155.1 7.7 %collective-permute-start.3 = (f32[2,128,128]{2,1,0:T(8,128)S(1)}, f32[2,128,128]{2,1,0:T(8,128)S(1)}, u32[]{:S(2)}, u32[]{:S(2)}) collective-permute-start(f32[2,128,128]{2,1,0:T(8,128)S(1)} %fusion.374), channel_id=1, source_target_pairs={{0,8},{8,16},{16,24},{24,32},{32,40},{40,48},{48,56},{56,64},{64,7... | collective-permute-start | bytes 393224 | tf_op jit(solution)/shard_map/ppermute | solution.py:17
  169.1 13.8 %psum.21 = f32[128]{0:T(128)S(1)} all-reduce(f32[128]{0:T(128)S(1)} %get-tuple-element.65), channel_id=1, replica_groups=mesh['ctx'=64,'head'=8] {'head'}, use_global_device_ids=true, to_apply=%region_18.19 | all-reduce | flops 128 | bytes 1024 | tf_op jit(solution)/shard_map/psum | solution.py:171
  185.5 11.2 %psum.22 = f32[128]{0:T(128)S(1)} all-reduce(f32[128]{0:T(128)S(1)} %get-tuple-element.52), channel_id=1, replica_groups=mesh['ctx'=64,'head'=8] {'head'}, use_global_device_ids=true, to_apply=%region_20.21 | all-reduce | flops 128 | bytes 1024 | tf_op jit(solution)/shard_map/psum | solution.py:176
  230.4 132.3 %psum.23 = f32[256]{0:T(256)} all-reduce(f32[256]{0:T(256)S(1)} %copy-done.142), channel_id=1, replica_groups=mesh['ctx'=64,'head'=8] {'ctx'}, use_global_device_ids=true, to_apply=%region_28.29 | all-reduce | flops 256 | bytes 2048 | tf_op jit(solution)/shard_map/psum | solution.py:181
  392.2 4.4 collective-permute-done.9
  399.1 6.7 %collective-permute-done.10 = bf16[2,128,128]{2,1,0:T(8,128)(2,1)S(1)} collective-permute-done((bf16[2,128,128]{2,1,0:T(8,128)(2,1)S(1)}, bf16[2,128,128]{2,1,0:T(8,128)(2,1)S(1)}, u32[]{:S(2)}, u32[]{:S(2)}) %collective-permute-start.10) | collective-permute-done | bytes 65568 | tf_op jit(solution)/shard_map/ppermute | solution.py:17
  413.2 4.4 collective-permute-done.11
  456.1 5.3 %multiply_bitcast_fusion.3 = (f32[2,32,4,32,4]{4,3,2,1,0:T(8,128)}, f32[2,32,4,32,4]{4,3,2,1,0:T(8,128)}) fusion(f32[32,32]{1,0:T(8,128)S(1)} %copy-done.131, f32[32,2,4,4]{3,2,0,1:T(4,128)S(1)} %copy-done.84, f32[32,2,4,4]{3,2,0,1:T(4,128)} %pad.162), kind=kLoop, calls=%fused_computation.11 | loop fusion | flops 65536 | bytes 274432 | tf_op jit(solution)/shard_map/transpose(jvp(vmap(aibj,ab->aij)))/transpose | solution.py:38
  461.4 4.9 reshape.741
  466.3 4.9 reshape.754
  471.9 7.1 %multiply_bitcast_fusion.1 = (f32[2,64,2,64,2]{4,3,2,1,0:T(8,128)}, f32[2,64,2,64,2]{4,3,2,1,0:T(8,128)}) fusion(f32[64,64]{1,0:T(8,128)S(1)} %copy-done.130, f32[64,2,2,2]{3,2,0,1:T(2,128)S(1)} %copy-done.83, f32[64,2,2,2]{3,2,0,1:T(2,128)S(1)} %copy-done.85), kind=kLoop, calls=%fused_computation.5 | loop fusion | flops 65536 | bytes 282624 | tf_op jit(solution)/shard_map/transpose(jvp(vmap(aibj,ab->aij)))/transpose | solution.py:38
  479.0 6.9 %reshape.743 = f32[2,128,128]{2,1,0:T(8,128)S(1)} reshape(f32[2,64,2,64,2]{4,3,2,1,0:T(8,128)} %get-tuple-element.101) | data formatting | bytes 262144 | tf_op jit(solution)/shard_map/transpose(jvp(vmap()))/reshape | solution.py:40
  486.1 7.3 %reshape.756 = f32[2,128,128]{2,1,0:T(8,128)S(1)} reshape(f32[2,64,2,64,2]{4,3,2,1,0:T(8,128)} %get-tuple-element.102) | data formatting | bytes 262144 | tf_op jit(solution)/shard_map/transpose(jvp(vmap()))/reshape | solution.py:40
  (677 shorter events, 216.8 us)
Async XLA Ops:
  0.6 134.7 %collective-permute-start.5 = (bf16[128,256]{1,0:T(8,128)(2,1)}, bf16[128,256]{1,0:T(8,128)(2,1)}, u32[]{:S(2)}, u32[]{:S(2)}) collective-permute-start(bf16[128,256]{1,0:T(8,128)(2,1)} %param.10), channel_id=1, source_target_pairs={{0,16},{8,24},{16,32},{24,40},{32,48},{40,56},{48,64},{56,72},{64,... | collective-permute-start | bytes 196616 | tf_op jit(solution)/shard_map/ppermute | solution.py:17
  5.8 130.5 %collective-permute-start.4 = (bf16[128,256]{1,0:T(8,128)(2,1)}, bf16[128,256]{1,0:T(8,128)(2,1)}, u32[]{:S(2)}, u32[]{:S(2)}) collective-permute-start(bf16[128,256]{1,0:T(8,128)(2,1)} %param.10), channel_id=1, source_target_pairs={{0,8},{8,16},{16,24},{24,32},{32,40},{40,48},{48,56},{56,64},{64,7... | collective-permute-start | bytes 196616 | tf_op jit(solution)/shard_map/ppermute | solution.py:17
  9.7 127.6 %collective-permute-start.7 = (bf16[128,256]{1,0:T(8,128)(2,1)}, bf16[128,256]{1,0:T(8,128)(2,1)}, u32[]{:S(2)}, u32[]{:S(2)}) collective-permute-start(bf16[128,256]{1,0:T(8,128)(2,1)} %param.10), channel_id=1, source_target_pairs={{0,32},{8,40},{16,48},{24,56},{32,64},{40,72},{48,80},{56,88},{64,... | collective-permute-start | bytes 196616 | tf_op jit(solution)/shard_map/ppermute | solution.py:17
  13.5 124.8 %collective-permute-start.6 = (bf16[128,256]{1,0:T(8,128)(2,1)}, bf16[128,256]{1,0:T(8,128)(2,1)}, u32[]{:S(2)}, u32[]{:S(2)}) collective-permute-start(bf16[128,256]{1,0:T(8,128)(2,1)} %param.10), channel_id=1, source_target_pairs={{0,24},{8,32},{16,40},{24,48},{32,56},{40,64},{48,72},{56,80},{64,... | collective-permute-start | bytes 196616 | tf_op jit(solution)/shard_map/ppermute | solution.py:17
  88.1 51.2 %collective-permute-start = (f32[2,128,128]{2,1,0:T(8,128)}, f32[2,128,128]{2,1,0:T(8,128)}, u32[]{:S(2)}, u32[]{:S(2)}) collective-permute-start(f32[2,128,128]{2,1,0:T(8,128)} %convolution_subtract_fusion.7), channel_id=1, source_target_pairs={{0,8},{8,16},{16,24},{24,32},{32,40},{40,48},{48,56},{56,64},{64,7... | collective-permute-start | bytes 393224 | tf_op jit(solution)/shard_map/ppermute | solution.py:17
  133.4 63.3 %copy-start.82 = (pred[128,128]{0,1:T(8,128)(4,1)}, pred[128,128]{0,1:T(8,128)(4,1)S(1)}, u32[]{:S(2)}) copy-start(pred[128,128]{0,1:T(8,128)(4,1)S(1)} %get-tuple-element.126) | copy-start | bytes 49156
  140.6 4.0 collective-permute-start.1
  144.9 9.8 %collective-permute-start.2 = (f32[2,128,128]{2,1,0:T(8,128)S(1)}, f32[2,128,128]{2,1,0:T(8,128)S(1)}, u32[]{:S(2)}, u32[]{:S(2)}) collective-permute-start(f32[2,128,128]{2,1,0:T(8,128)S(1)} %fusion.373), channel_id=1, source_target_pairs={{0,8},{8,16},{16,24},{24,32},{32,40},{40,48},{48,56},{56,64},{64,7... | collective-permute-start | bytes 393224 | tf_op jit(solution)/shard_map/ppermute | solution.py:17
  155.1 9.6 %collective-permute-start.3 = (f32[2,128,128]{2,1,0:T(8,128)S(1)}, f32[2,128,128]{2,1,0:T(8,128)S(1)}, u32[]{:S(2)}, u32[]{:S(2)}) collective-permute-start(f32[2,128,128]{2,1,0:T(8,128)S(1)} %fusion.374), channel_id=1, source_target_pairs={{0,8},{8,16},{16,24},{24,32},{32,40},{40,48},{48,56},{56,64},{64,7... | collective-permute-start | bytes 393224 | tf_op jit(solution)/shard_map/ppermute | solution.py:17
  217.3 153.1 %copy-start.46 = (pred[128,128]{0,1:T(8,128)(4,1)S(1)}, pred[128,128]{0,1:T(8,128)(4,1)}, u32[]{:S(2)}) copy-start(pred[128,128]{0,1:T(8,128)(4,1)} %iota_compare_fusion.11) | copy-start | bytes 49156
  218.4 152.5 %copy-start.94 = (f32[2,128,128]{2,1,0:T(8,128)S(1)}, f32[2,128,128]{2,1,0:T(8,128)}, u32[]{:S(2)}) copy-start(f32[2,128,128]{2,1,0:T(8,128)} %fusion.381) | copy-start | bytes 393220
  223.2 156.8 %copy-start.67 = (f32[2,32,1,2,2]{4,3,1,0,2:T(2,128)S(1)}, f32[2,32,1,2,2]{4,3,1,0,2:T(2,128)}, u32[]{:S(2)}) copy-start(f32[2,32,1,2,2]{4,3,1,0,2:T(2,128)} %copy-done.66) | copy-start | bytes 3076
  226.1 158.9 %copy-start.74 = (f32[2,64,64]{2,1,0:T(8,128)S(1)}, f32[2,64,64]{2,1,0:T(8,128)}, u32[]{:S(2)}) copy-start(f32[2,64,64]{2,1,0:T(8,128)} %copy-done.73) | copy-start | bytes 98308
  226.2 159.9 %copy-start.88 = (f32[2,128,128]{2,1,0:T(8,128)S(1)}, f32[2,128,128]{2,1,0:T(8,128)}, u32[]{:S(2)}) copy-start(f32[2,128,128]{2,1,0:T(8,128)} %fusion.380) | copy-start | bytes 393220
  226.6 149.3 %copy-start.126 = (f32[2,2,32,32]{3,2,0,1:T(8,128)S(1)}, f32[2,2,32,32]{3,2,0,1:T(8,128)}, u32[]{:S(2)}) copy-start(f32[2,2,32,32]{3,2,0,1:T(8,128)} %convolution_bitcast_fusion.13) | copy-start | bytes 49156
  228.3 168.3 %copy-start.87 = (f32[2,128,128]{2,1,0:T(8,128)S(1)}, f32[2,128,128]{2,1,0:T(8,128)}, u32[]{:S(2)}) copy-start(f32[2,128,128]{2,1,0:T(8,128)} %fusion.379) | copy-start | bytes 393220
  362.7 26.4 %collective-permute-start.12 = (bf16[2,128,128]{1,2,0:T(8,128)(2,1)}, bf16[2,128,128]{1,2,0:T(8,128)(2,1)}, u32[]{:S(2)}, u32[]{:S(2)}) collective-permute-start(bf16[2,128,128]{1,2,0:T(8,128)(2,1)} %convolution_convert_fusion.3), channel_id=1, source_target_pairs={{8,0},{16,8},{24,16},{32,24},{40,32},{48,40},{56,48},{64,56},{72,6... | collective-permute-start | bytes 196616 | tf_op jit(solution)/shard_map/ppermute | solution.py:17
  364.7 24.5 %collective-permute-start.15 = (bf16[2,128,128]{1,2,0:T(8,128)(2,1)}, bf16[2,128,128]{1,2,0:T(8,128)(2,1)}, u32[]{:S(2)}, u32[]{:S(2)}) collective-permute-start(bf16[2,128,128]{1,2,0:T(8,128)(2,1)} %convolution_convert_fusion), channel_id=1, source_target_pairs={{32,0},{40,8},{48,16},{56,24},{64,32},{72,40},{80,48},{88,56},{96,... | collective-permute-start | bytes 196616 | tf_op jit(solution)/shard_map/ppermute | solution.py:17
  366.6 22.6 %collective-permute-start.14 = (bf16[2,128,128]{1,2,0:T(8,128)(2,1)}, bf16[2,128,128]{1,2,0:T(8,128)(2,1)}, u32[]{:S(2)}, u32[]{:S(2)}) collective-permute-start(bf16[2,128,128]{1,2,0:T(8,128)(2,1)} %convolution_convert_fusion.1), channel_id=1, source_target_pairs={{24,0},{32,8},{40,16},{48,24},{56,32},{64,40},{72,48},{80,56},{88,... | collective-permute-start | bytes 196616 | tf_op jit(solution)/shard_map/ppermute | solution.py:17
  368.5 20.7 %collective-permute-start.13 = (bf16[2,128,128]{1,2,0:T(8,128)(2,1)}, bf16[2,128,128]{1,2,0:T(8,128)(2,1)}, u32[]{:S(2)}, u32[]{:S(2)}) collective-permute-start(bf16[2,128,128]{1,2,0:T(8,128)(2,1)} %convolution_convert_fusion.2), channel_id=1, source_target_pairs={{16,0},{24,8},{32,16},{40,24},{48,32},{56,40},{64,48},{72,56},{80,... | collective-permute-start | bytes 196616 | tf_op jit(solution)/shard_map/ppermute | solution.py:17
  371.8 14.2 %collective-permute-start.8 = (bf16[2,128,128]{2,1,0:T(8,128)(2,1)}, bf16[2,128,128]{2,1,0:T(8,128)(2,1)}, u32[]{:S(2)}, u32[]{:S(2)}) collective-permute-start(bf16[2,128,128]{2,1,0:T(8,128)(2,1)} %fusion.41), channel_id=1, source_target_pairs={{8,0},{16,8},{24,16},{32,24},{40,32},{48,40},{56,48},{64,56},{72,6... | collective-permute-start | bytes 196616 | tf_op jit(solution)/shard_map/ppermute | solution.py:17
  387.1 9.6 %collective-permute-start.9 = (bf16[2,128,128]{2,1,0:T(8,128)(2,1)S(1)}, bf16[2,128,128]{2,1,0:T(8,128)(2,1)S(1)}, u32[]{:S(2)}, u32[]{:S(2)}) collective-permute-start(bf16[2,128,128]{2,1,0:T(8,128)(2,1)S(1)} %fusion.44), channel_id=1, source_target_pairs={{8,0},{16,8},{24,16},{32,24},{40,32},{48,40},{56,48},{64,56},{72,6... | collective-permute-start | bytes 196616 | tf_op jit(solution)/shard_map/ppermute | solution.py:17
  396.9 8.9 %collective-permute-start.10 = (bf16[2,128,128]{2,1,0:T(8,128)(2,1)S(1)}, bf16[2,128,128]{2,1,0:T(8,128)(2,1)S(1)}, u32[]{:S(2)}, u32[]{:S(2)}) collective-permute-start(bf16[2,128,128]{2,1,0:T(8,128)(2,1)S(1)} %fusion.45), channel_id=1, source_target_pairs={{8,0},{16,8},{24,16},{32,24},{40,32},{48,40},{56,48},{64,56},{72,6... | collective-permute-start | bytes 196616 | tf_op jit(solution)/shard_map/ppermute | solution.py:17
  408.6 9.0 %collective-permute-start.11 = (bf16[2,128,128]{2,1,0:T(8,128)(2,1)S(1)}, bf16[2,128,128]{2,1,0:T(8,128)(2,1)S(1)}, u32[]{:S(2)}, u32[]{:S(2)}) collective-permute-start(bf16[2,128,128]{2,1,0:T(8,128)(2,1)S(1)} %fusion.46), channel_id=1, source_target_pairs={{8,0},{16,8},{24,16},{32,24},{40,32},{48,40},{56,48},{64,56},{72,6... | collective-permute-start | bytes 196616 | tf_op jit(solution)/shard_map/ppermute | solution.py:17
  (145 other events, 1851.5 us)
where the time goes:
time: 509 us; the launch traced here: 504 us
  blocking collectives  157 us (31%)
  matrix products  116 us (23%)
  local copies, waits for them, and re-layouts  114 us (22%)
  starting transfers between devices  52.8 us (10%)
  other arithmetic  39.7 us (8%)
  waiting for transfers between devices  19.2 us (4%)
    psum x1, blocking collectives, per_device(): lax.psum(jnp.sum(cotangent * attended * inverse_rms[:, None], axis=0), 'c...  132 us
    reshape x30, local copies, waits for them, and re-layouts, unit_lower_inverse(): full.reshape(groups, 2 * block_width, groups, 2 * block_width)  75.9 us
    ppermute x16, starting transfers between devices, passed_along(): lax.ppermute(value, axis, [(source, source + steps) for source in range(f...  52.8 us
    dot_general x95, matrix products, exact_sum(): return jnp.einsum(form, left, right, precision=lax.Precision.HIGHEST)  49.8 us
    dot_general x12, matrix products, unit_lower_inverse(): jnp.einsum('aibj,ab->aij', full.reshape(groups, 2 * block_width, groups,...  27.3 us
    dot_general x33, matrix products, exact_dot(): return jnp.dot(left, right, precision=lax.Precision.HIGHEST)  24.9 us
    ppermute x16, waiting for transfers between devices, passed_along(): lax.ppermute(value, axis, [(source, source + steps) for source in range(f...  19.2 us
    transpose x6, other arithmetic, unit_lower_inverse(): jnp.einsum('aibj,ab->aij', full.reshape(groups, 2 * block_width, groups,...  18.4 us
  transfers between devices with their start and end apart: 16, of which 6 were waited for; matrix products, arithmetic and copies ran while one was open for 27% of the time, Pallas kernels for 0%

commit v1 on v0

v1 whole, which is shorter than its diff:
```python
import functools

import jax
import jax.numpy as jnp
from jax import lax
from jax.experimental import pallas as pl
from jax.experimental.pallas import tpu as pltpu
from jax.sharding import PartitionSpec as P

DH = 128
WIN = 4
NEG_FILL = -1e30
EPSILON = 1e-06
F32 = jnp.float32
BF16 = jnp.bfloat16
VMEM_LIMIT = 48 * 1024 * 1024


def mm(left, right, form="nn"):
    lhs = 0 if form[0] == "t" else 1
    rhs = 1 if form[1] == "t" else 0
    return lax.dot_general(
        left.astype(BF16), right.astype(BF16), (((lhs,), (rhs,)), ((), ())), preferred_element_type=F32
    )


def split(value):
    high = value.astype(BF16)
    low = (value - high.astype(F32)).astype(BF16)
    return high, low


def mm3(left, right):
    lh, ll = split(left)
    rh, rl = split(right)
    return mm(lh, rh) + (mm(lh, rl) + mm(ll, rh))


def grids(size):
    rows = lax.broadcasted_iota(jnp.int32, (size, size), 0)
    cols = lax.broadcasted_iota(jnp.int32, (size, size), 1)
    return rows, cols


def to_col(row, eye):
    return jnp.sum(jnp.where(eye, row, 0.0), axis=1, keepdims=True)


def to_row(col, eye):
    return jnp.sum(jnp.where(eye, col, 0.0), axis=0, keepdims=True)


def unit_lower_inverses(strict_list):
    size = strict_list[0].shape[0]
    rows, cols = grids(size)
    width = 1
    inverses = None
    while width < size:
        row_block = rows // width
        coupling = (row_block - cols // width == 1) & (row_block % 2 == 1)
        parts = [jnp.where(coupling, strict, 0.0) for strict in strict_list]
        if inverses is None:
            inverses = [jnp.where(rows == cols, 1.0, 0.0) - part for part in parts]
        else:
            halves = [mm3(part, inverse) for part, inverse in zip(parts, inverses)]
            inverses = [inverse - mm3(inverse, half) for inverse, half in zip(inverses, halves)]
        width = 2 * width
    return inverses


def shard_scales(dirs, rate_row, eye):
    gram = mm(dirs, dirs, "nt")
    square = jnp.where(eye, gram, 0.0)
    norm_row = lax.rsqrt(jnp.sum(square, axis=0, keepdims=True) + EPSILON)
    norm_col = lax.rsqrt(jnp.sum(square, axis=1, keepdims=True) + EPSILON)
    rate_col = to_col(rate_row, eye)
    return gram, norm_row, norm_col, rate_col


def prepare(shards):
    size = shards[0][0].shape[0]
    rows, cols = grids(size)
    eye = rows == cols
    strict = rows > cols
    grams, rights, norms = [], [], []
    for dirs, keys, rate_row in shards:
        gram, norm_row, norm_col, rate_col = shard_scales(dirs, rate_row, eye)
        scale = rate_col * norm_col
        grams.append(jnp.where(strict, gram * norm_row * scale, 0.0))
        rights.append(
            jnp.concatenate(
                [jnp.where(strict, mm(dirs, keys, "nt") * scale, 0.0), dirs.astype(F32) * scale], axis=1
            )
        )
        norms.append((norm_row, norm_col))
    inverses = unit_lower_inverses(grams)
    return [
        (inverse, mm3(inverse, right), norm) for inverse, right, norm in zip(inverses, rights, norms)
    ]


def pack_kernel(key_ref, dir_ref, value_ref, rate_ref, out_ref):
    size, width = key_ref.shape
    out_ref[0:size, 0:width] = key_ref[...]
    out_ref[0:size, width : 2 * width] = dir_ref[...]
    out_ref[0:size, 2 * width : 3 * width] = value_ref[...]
    heads = rate_ref.shape[0]
    rate = jnp.concatenate([rate_ref[h : h + 1, :] for h in range(heads)], axis=1)
    first = rate.astype(BF16).astype(F32)
    rest = rate - first
    second = rest.astype(BF16).astype(F32)
    third = rest - second
    row = lax.broadcasted_iota(jnp.int32, (16, width), 0)
    pieces = jnp.where(row == 0, first, jnp.where(row == 1, second, jnp.where(row == 2, third, 0.0)))
    out_ref[size : size + 16, 0:width] = pieces.astype(BF16)
    out_ref[size : size + 16, width : 3 * width] = jnp.zeros((16, 2 * width), BF16)


def own_kernel(query_ref, key_ref, dir_ref, rate_ref, inv_ref, kw_ref, raw_ref):
    size = query_ref.shape[0]
    heads = rate_ref.shape[0]
    rows, cols = grids(size)
    shards = []
    for h in range(heads):
        lanes = slice(h * DH, (h + 1) * DH)
        shards.append((dir_ref[:, lanes], key_ref[:, lanes], rate_ref[h : h + 1, :]))
    prepared = prepare(shards)
    for h in range(heads):
        lanes = slice(h * DH, (h + 1) * DH)
        inverse, coef, (norm_row, _) = prepared[h]
        query = query_ref[:, lanes]
        dirs, keys, _ = shards[h]
        applied = jnp.where(rows >= cols, mm(query, dirs, "nt") * norm_row, 0.0)
        base = jnp.concatenate([mm(query, keys, "nt"), query.astype(F32)], axis=1)
        raw_ref[h] = base - mm3(applied, coef)
        inv_ref[h] = inverse.astype(BF16)
        kw_ref[h] = coef.astype(BF16)


def attend_kernel(
    heads,
    raw_ref,
    value_ref,
    cot_ref,
    gain_ref,
    halo1_ref,
    halo2_ref,
    halo3_ref,
    halo4_ref,
    len_ref,
    first_ref,
    att_ref,
    tot_ref,
    prob_ref,
    frame_ref,
    kt_ref,
    sums_ref,
):
    size = value_ref.shape[0]
    width = heads * DH
    halos = (halo1_ref, halo2_ref, halo3_ref, halo4_ref)
    rows, cols = grids(size)
    eye = rows == cols
    eye_f = jnp.where(eye, 1.0, 0.0)
    first = first_ref[0]
    pos_row = first + lax.broadcasted_iota(jnp.int32, (1, size), 1)
    start_row = jnp.zeros((1, size), jnp.int32)
    end = jnp.int32(0)
    for d in range(len_ref.shape[0]):
        end = end + len_ref[d]
        start_row = jnp.where(end <= pos_row, end, start_row)
    start = to_col(start_row.astype(F32), eye).astype(jnp.int32)
    seen = [(rows >= cols) & (first + cols >= start)]
    for s in range(1, WIN + 1):
        seen.append(first - s * size + cols >= start)
    shards = []
    for s in range(WIN):
        for h in range(heads):
            keys = halos[s][0:size, h * DH : (h + 1) * DH]
            dirs = halos[s][0:size, width + h * DH : width + (h + 1) * DH]
            rate = halos[s][size : size + 16, h * DH : (h + 1) * DH].astype(F32)
            shards.append((dirs, keys, jnp.sum(rate, axis=0, keepdims=True)))
    prepared = prepare(shards)
    carry = []
    for (dirs, keys, _), (_, coef, (_, norm_col)) in zip(shards, prepared):
        base = jnp.concatenate([keys.astype(F32).T, eye_f], axis=1)
        high, low = split(coef * norm_col)
        turned = dirs.astype(F32).T.astype(BF16)
        carry.append(base - (mm(turned, high) + mm(turned, low)))
    square = jnp.zeros((size, 1), F32)
    inner = jnp.zeros((size, 1), F32)
    for h in range(heads):
        lanes = slice(h * DH, (h + 1) * DH)
        scores = [raw_ref[h, :, 0:DH]]
        frame = raw_ref[h, :, DH : 2 * DH]
        for s in range(WIN):
            matrix = carry[s * heads + h]
            kt_ref[h, s] = matrix.astype(BF16)
            frame_ref[h, s] = frame.astype(BF16)
            if s < WIN - 1:
                product = mm3(frame, matrix)
                scores.append(product[:, 0:DH])
                frame = product[:, DH : 2 * DH]
            else:
                scores.append(mm3(frame, matrix[:, 0:DH]))
        scaled = [
            jnp.where(seen[s], scores[s] * (DH ** (-0.5)), NEG_FILL) for s in range(WIN + 1)
        ]
        top = scaled[0]
        for s in range(1, WIN + 1):
            top = jnp.maximum(top, scaled[s])
        top = jnp.max(top, axis=1, keepdims=True)
        weights = [jnp.where(seen[s], jnp.exp(scaled[s] - top), 0.0) for s in range(WIN + 1)]
        total = weights[0]
        for s in range(1, WIN + 1):
            total = total + weights[s]
        total = jnp.sum(total, axis=1, keepdims=True)
        numer = None
        for s in range(WIN + 1):
            half = weights[s].astype(BF16)
            prob_ref[h, s] = half
            if s == 0:
                value = value_ref[:, lanes]
            else:
                value = halos[s - 1][0:size, 2 * width + h * DH : 2 * width + (h + 1) * DH]
            term = mm(half, value)
            numer = term if numer is None else numer + term
        att = numer / total
        att_ref[:, lanes] = att
        tot_ref[h] = jnp.broadcast_to(total, (size, 8))
        weighted = cot_ref[:, lanes].astype(F32) * gain_ref[:, lanes]
        square = square + jnp.sum(att * att, axis=1, keepdims=True)
        inner = inner + jnp.sum(weighted * att, axis=1, keepdims=True)
    sums_ref[0:1, :] = to_row(square, eye)
    sums_ref[1:2, :] = to_row(inner, eye)


def back_kernel(
    heads,
    features,
    sums_ref,
    att_ref,
    tot_ref,
    prob_ref,
    frame_ref,
    kt_ref,
    value_ref,
    cot_ref,
    gain_ref,
    halo1_ref,
    halo2_ref,
    halo3_ref,
    halo4_ref,
    normed_ref,
    part_ref,
    own_ref,
    dval_ref,
    send1_ref,
    send2_ref,
    send3_ref,
    send4_ref,
):
    size = value_ref.shape[0]
    width = heads * DH
    halos = (halo1_ref, halo2_ref, halo3_ref, halo4_ref)
    sends = (send1_ref, send2_ref, send3_ref, send4_ref)
    rows, cols = grids(size)
    eye = rows == cols
    square = to_col(sums_ref[0:1, :], eye)
    inner = to_col(sums_ref[1:2, :], eye)
    inverse = lax.rsqrt(square / features + EPSILON)
    pull = inverse * inverse * inverse * inner / features
    att_all = att_ref[...]
    cot_all = cot_ref[...].astype(F32)
    gain = gain_ref[...]
    normed = att_all * inverse
    normed_ref[...] = (normed * gain).astype(BF16)
    part_ref[...] = jnp.sum(cot_all * normed, axis=0, keepdims=True)
    grad_att = cot_all * gain * inverse - att_all * pull
    scale = DH ** (-0.5)
    for h in range(heads):
        lanes = slice(h * DH, (h + 1) * DH)
        total = tot_ref[h, :, 0:1]
        grad = grad_att[:, lanes]
        scaled = (grad / total).astype(BF16)
        delta = jnp.sum(grad * att_all[:, lanes], axis=1, keepdims=True) / total
        carried = None
        for s in range(WIN, -1, -1):
            if s == 0:
                value = value_ref[:, lanes]
            else:
                value = halos[s - 1][0:size, 2 * width + h * DH : 2 * width + (h + 1) * DH]
            prob = prob_ref[h, s]
            through = mm(scaled, value, "nt")
            dscore = (prob.astype(F32) * ((through - delta) * scale)).astype(BF16)
            dvalue = mm(prob, scaled, "tn")
            if s == 0:
                dval_ref[:, lanes] = dvalue
                own_ref[h] = jnp.concatenate([dscore, carried], axis=1)
                continue
            send = sends[s - 1]
            send[:, lanes] = dvalue.astype(BF16)
            if carried is None:
                send[:, width + h * DH : width + (h + 1) * DH] = mm(frame_ref[h, s - 1], dscore, "tn").astype(BF16)
                carried = mm(dscore, kt_ref[h, s - 1, :, 0:DH], "nt").astype(BF16)
            else:
                both = jnp.concatenate([dscore, carried], axis=1)
                grads = mm(frame_ref[h, s - 1], both, "tn").astype(BF16)
                send[:, width + h * DH : width + (h + 1) * DH] = grads[:, 0:DH]
                send[:, 2 * width + h * DH : 2 * width + (h + 1) * DH] = grads[:, DH : 2 * DH]
                carried = mm(both, kt_ref[h, s - 1], "nt").astype(BF16)


def local_kernel(heads, own_ref, kw_ref, query_ref, key_ref, dir_ref, dquery_ref, dkey_ref, ddir_ref, pulled_ref):
    size = query_ref.shape[0]
    rows, cols = grids(size)
    eye = rows == cols
    lower = rows >= cols
    for h in range(heads):
        lanes = slice(h * DH, (h + 1) * DH)
        query = query_ref[:, lanes]
        keys = key_ref[:, lanes]
        raw_dirs = dir_ref[:, lanes].astype(F32)
        norm_col = lax.rsqrt(jnp.sum(raw_dirs * raw_dirs, axis=1, keepdims=True) + EPSILON)
        unit = (raw_dirs * norm_col).astype(BF16)
        grads = own_ref[h]
        applied = jnp.where(lower, mm(query, unit, "nt"), 0.0).astype(BF16)
        dapplied = jnp.where(lower, mm(grads, kw_ref[h], "nt"), 0.0).astype(BF16)
        dquery = mm(grads[:, 0:DH], keys) + grads[:, DH : 2 * DH].astype(F32) - mm(dapplied, unit)
        dquery_ref[:, lanes] = dquery.astype(BF16)
        dkey_ref[h] = mm(grads[:, 0:DH], query, "tn")
        ddir_ref[h] = -mm(dapplied, query, "tn")
        pulled_ref[h] = mm(applied, grads, "tn")


def shard_kernel(
    heads,
    recv1_ref,
    recv2_ref,
    recv3_ref,
    recv4_ref,
    inv_ref,
    kw_ref,
    pulled_ref,
    dkey_in_ref,
    ddir_in_ref,
    dval_in_ref,
    key_ref,
    dir_ref,
    rate_ref,
    dkey_ref,
    dvalue_ref,
    ddir_ref,
    drate_ref,
):
    size = key_ref.shape[0]
    width = heads * DH
    recvs = (recv1_ref, recv2_ref, recv3_ref, recv4_ref)
    rows, cols = grids(size)
    eye = rows == cols
    strict = rows > cols
    dvalue = dval_in_ref[...]
    for s in range(WIN):
        dvalue = dvalue + recvs[s][:, 0:width].astype(F32)
    dvalue_ref[...] = dvalue.astype(BF16)
    for h in range(heads):
        lanes = slice(h * DH, (h + 1) * DH)
        keys = key_ref[:, lanes]
        raw_dirs = dir_ref[:, lanes].astype(F32)
        norm_col = lax.rsqrt(jnp.sum(raw_dirs * raw_dirs, axis=1, keepdims=True) + EPSILON)
        unit = raw_dirs * norm_col
        unit_half = unit.astype(BF16)
        rate_col = to_col(rate_ref[h : h + 1, :], eye)
        dend = recvs[0][:, width + h * DH : width + (h + 1) * DH].astype(F32)
        dtrans = recvs[0][:, 2 * width + h * DH : 2 * width + (h + 1) * DH].astype(F32)
        for s in range(1, WIN):
            dend = dend + recvs[s][:, width + h * DH : width + (h + 1) * DH].astype(F32)
            if s < WIN - 1:
                dtrans = dtrans + recvs[s][:, 2 * width + h * DH : 2 * width + (h + 1) * DH].astype(F32)
        both = jnp.concatenate([dend, dtrans], axis=1).astype(BF16)
        coef = kw_ref[h]
        dcoef = -(pulled_ref[h] + mm(unit_half, both))
        solved = mm(inv_ref[h], dcoef, "tn")
        dstrict = jnp.where(strict, -mm(solved, coef, "nt"), 0.0)
        dinner = jnp.where(strict, solved[:, 0:DH], 0.0).astype(BF16)
        local = mm(dstrict, unit_half) + mm(dinner, keys) + solved[:, DH : 2 * DH]
        dunit = (
            rate_col * local
            + mm(rate_col * dstrict, unit_half, "tn")
            + ddir_in_ref[h]
            - mm(coef, both, "nt")
        )
        drate_ref[h : h + 1, :] = to_row(jnp.sum(local * unit, axis=1, keepdims=True), eye)
        dkey_ref[:, lanes] = (
            dkey_in_ref[h] + mm(dinner, rate_col * unit, "tn") + dend.T
        ).astype(BF16)
        along = jnp.sum(unit * dunit, axis=1, keepdims=True)
        ddir_ref[:, lanes] = (norm_col * (dunit - unit * along)).astype(BF16)


def call(body, outs, flops, *operands, scalars=()):
    vmem = pl.BlockSpec(memory_space=pltpu.VMEM)
    smem = pl.BlockSpec(memory_space=pltpu.SMEM)
    moved = sum(x.size * x.dtype.itemsize for x in operands) + sum(
        jnp.dtype(d).itemsize * functools.reduce(lambda a, b: a * b, s) for s, d in outs
    )
    return pl.pallas_call(
        body,
        out_shape=[jax.ShapeDtypeStruct(s, d) for s, d in outs],
        in_specs=[vmem] * len(operands) + [smem] * len(scalars),
        out_specs=[vmem] * len(outs),
        compiler_params=pltpu.CompilerParams(vmem_limit_bytes=VMEM_LIMIT),
        cost_estimate=pl.CostEstimate(flops=flops, bytes_accessed=moved, transcendentals=0),
    )(*operands, *scalars)


def passed_along(value, steps):
    count = lax.axis_size("ctx")
    first, last = (max(0, -steps), min(count, count - steps))
    return lax.ppermute(value, "ctx", [(source, source + steps) for source in range(first, last)])


def grouped_sum(value, axis, width):
    count = lax.axis_size(axis)
    inner = [[g * width + i for i in range(width)] for g in range(count // width)]
    outer = [[g * width + i for g in range(count // width)] for i in range(width)]
    value = lax.psum(value, axis, axis_index_groups=inner)
    return lax.psum(value, axis, axis_index_groups=outer)


def per_device(query, keys, values, dirs, rates, gain, doc_lengths, cotangent):
    size, width = query.shape
    heads = width // DH
    features = width * lax.axis_size("head")
    gain_row = gain.reshape(1, width)
    first = (lax.axis_index("ctx") * size).astype(jnp.int32).reshape(1)
    unit_flops = 2 * size * size * DH
    (packed,) = call(pack_kernel, [((size + 16, 3 * width), BF16)], 0, keys, dirs, values, rates)
    halos = [passed_along(packed, s) for s in range(1, WIN + 1)]
    inverse, coef, raw = call(
        own_kernel,
        [((heads, size, size), BF16), ((heads, size, 2 * DH), BF16), ((heads, size, 2 * DH), F32)],
        heads * 60 * unit_flops,
        query,
        keys,
        dirs,
        rates,
    )
    att, total, prob, frame, carry, sums = call(
        functools.partial(attend_kernel, heads),
        [
            ((size, width), F32),
            ((heads, size, 8), F32),
            ((heads, WIN + 1, size, size), BF16),
            ((heads, WIN, size, DH), BF16),
            ((heads, WIN, DH, 2 * DH), BF16),
            ((2, size), F32),
        ],
        heads * 300 * unit_flops,
        raw,
        values,
        cotangent,
        gain_row,
        *halos,
        scalars=(doc_lengths, first),
    )
    sums = lax.psum(sums, "head")
    normed, part, own, dval, *sends = call(
        functools.partial(back_kernel, heads, features),
        [
            ((size, width), BF16),
            ((1, width), F32),
            ((heads, size, 2 * DH), BF16),
            ((size, width), F32),
            ((size, 3 * width), BF16),
            ((size, 3 * width), BF16),
            ((size, 3 * width), BF16),
            ((size, 2 * width), BF16),
        ],
        heads * 30 * unit_flops,
        sums,
        att,
        total,
        prob,
        frame,
        carry,
        values,
        cotangent,
        gain_row,
        *halos,
    )
    recvs = [passed_along(sends[s - 1], -s) for s in range(1, WIN + 1)]
    dquery, dkey_part, ddir_part, pulled = call(
        functools.partial(local_kernel, heads),
        [
            ((size, width), BF16),
            ((heads, size, DH), F32),
            ((heads, size, DH), F32),
            ((heads, size, 2 * DH), F32),
        ],
        heads * 10 * unit_flops,
        own,
        coef,
        query,
        keys,
        dirs,
    )
    grad_gain = grouped_sum(part, "ctx", 8).reshape(width)
    dkey, dvalue, ddir, drate = call(
        functools.partial(shard_kernel, heads),
        [((size, width), BF16), ((size, width), BF16), ((size, width), BF16), ((heads, size), F32)],
        heads * 20 * unit_flops,
        *recvs,
        inverse,
        coef,
        pulled,
        dkey_part,
        ddir_part,
        dval,
        keys,
        dirs,
        rates,
    )
    return normed, dquery, dkey, dvalue, ddir, drate, grad_gain


def solution(mesh):
    rows = P("ctx", "head")
    return jax.shard_map(
        per_device,
        mesh=mesh,
        in_specs=(rows, rows, rows, rows, P("head", "ctx"), P("head"), P(), rows),
        out_specs=(rows, rows, rows, rows, rows, P("head", "ctx"), P("head")),
        check_vma=False,
    )
```

time: 509 us -> 106 us (0.21)
  the two profiles are of different devices: /device:TPU:199 before, /device:TPU:6 now
where the time goes in v1:
time: 106 us; the launch traced here: 105 us
  blocking collectives  56.2 us (53%)
  starting transfers between devices  26 us (25%)
  Pallas kernels  14.9 us (14%)
  local copies, waits for them, and re-layouts  4.52 us (4%)
  waiting for transfers between devices  2.11 us (2%)
    ppermute x8, starting transfers between devices, passed_along(): lax.ppermute(value, 'ctx', [(source, source + steps) for source in range(...  26 us
    psum x1, blocking collectives, grouped_sum(): return lax.psum(value, axis, axis_index_groups=outer)  23.7 us
    psum x1, blocking collectives, per_device(): sums = lax.psum(sums, 'head')  17.6 us
    pallas_call x6, Pallas kernels, call(): pl.pallas_call(body, out_shape=[jax.ShapeDtypeStruct(s, d) for s, d in ou...  14.9 us
    psum x1, blocking collectives, grouped_sum(): value = lax.psum(value, axis, axis_index_groups=inner)  14.8 us
    unnamed x24, local copies, waits for them, and re-layouts  4.52 us
  transfers between devices with their start and end apart: 8, of which 2 were waited for; matrix products, arithmetic and copies ran while one was open for 0% of the time, Pallas kernels for 4%

profile of v1, /device:TPU:6, one launch (start us, length us, event | category | flops | bytes accessed | tf_op | source)
XLA Modules:
  0.0 104.5 jit_solution(8776073674069046)
XLA Ops:
  0.6 0.8 copy-done
  1.5 0.8 copy-done.2
  2.3 0.8 copy-done.4
  3.2 0.7 copy-done.8
  3.9 5.3 %collective-permute-start.3 = (bf16[144,768]{1,0:T(8,128)(2,1)S(1)}, bf16[144,768]{1,0:T(8,128)(2,1)S(1)}, u32[]{:S(2)}, u32[]{:S(2)}) collective-permute-start(bf16[144,768]{1,0:T(8,128)(2,1)S(1)} %shard_map.136), channel_id=1, source_target_pairs={{0,32},{8,40},{16,48},{24,56},{32,64},{40,72},{48,80},{56,88},{64,... | collective-permute-start | bytes 663560 | tf_op jit(solution)/shard_map/ppermute | solution.py:420
  9.1 3.2 %collective-permute-start.2 = (bf16[144,768]{1,0:T(8,128)(2,1)S(1)}, bf16[144,768]{1,0:T(8,128)(2,1)S(1)}, u32[]{:S(2)}, u32[]{:S(2)}) collective-permute-start(bf16[144,768]{1,0:T(8,128)(2,1)S(1)} %shard_map.136), channel_id=1, source_target_pairs={{0,24},{8,32},{16,40},{24,48},{32,56},{40,64},{48,72},{56,80},{64,... | collective-permute-start | bytes 663560 | tf_op jit(solution)/shard_map/ppermute | solution.py:420
  12.3 2.8 %collective-permute-start.1 = (bf16[144,768]{1,0:T(8,128)(2,1)S(1)}, bf16[144,768]{1,0:T(8,128)(2,1)S(1)}, u32[]{:S(2)}, u32[]{:S(2)}) collective-permute-start(bf16[144,768]{1,0:T(8,128)(2,1)S(1)} %shard_map.136), channel_id=1, source_target_pairs={{0,16},{8,24},{16,32},{24,40},{32,48},{40,56},{48,64},{56,72},{64,... | collective-permute-start | bytes 663560 | tf_op jit(solution)/shard_map/ppermute | solution.py:420
  15.1 4.0 %collective-permute-start = (bf16[144,768]{1,0:T(8,128)(2,1)S(1)}, bf16[144,768]{1,0:T(8,128)(2,1)S(1)}, u32[]{:S(2)}, u32[]{:S(2)}) collective-permute-start(bf16[144,768]{1,0:T(8,128)(2,1)S(1)} %shard_map.136), channel_id=1, source_target_pairs={{0,8},{8,16},{16,24},{24,32},{32,40},{40,48},{48,56},{56,64},{64,7... | collective-permute-start | bytes 663560 | tf_op jit(solution)/shard_map/ppermute | solution.py:420
  19.2 0.6 copy-done.9
  19.8 2.9 %shard_map.135 = (bf16[2,128,128]{2,1,0:T(8,128)(2,1)S(1)}, bf16[2,128,256]{2,1,0:T(8,128)(2,1)S(1)}, f32[2,128,256]{2,1,0:T(8,128)S(1)}) custom-call(bf16[128,256]{1,0:T(8,128)(2,1)S(1)} %copy-done.7, bf16[128,256]{1,0:T(8,128)(2,1)S(1)} %copy-done.1, bf16[128,256]{1,0:T(8,128)(2,1)S(1)} %copy-done.3, f32[2,128]{1,0:T(2,128)S(1)} %copy-done.9), custom_call_target="tpu_custom_call" | custom-call | flops 503316480 | bytes 656384 | tf_op jit(solution)/shard_map/pallas_call | solution.py:407
  22.8 0.7 collective-permute-done.1.halo2_ref
  23.4 1.4 %collective-permute-done.halo1_ref = bf16[144,768]{1,0:T(8,128)(2,1)S(1)} collective-permute-done((bf16[144,768]{1,0:T(8,128)(2,1)S(1)}, bf16[144,768]{1,0:T(8,128)(2,1)S(1)}, u32[]{:S(2)}, u32[]{:S(2)}) %collective-permute-start) | collective-permute-done | bytes 221216 | tf_op jit(solution)/shard_map/ppermute | solution.py:420
  24.9 0.7 copy-done.10
  25.6 6.2 %shard_map.137 = (f32[128,256]{1,0:T(8,128)S(1)}, f32[2,128,8]{2,1,0:T(8,128)S(1)}, bf16[2,5,128,128]{3,2,1,0:T(8,128)(2,1)S(1)}, bf16[2,4,128,128]{3,2,1,0:T(8,...) custom-call(f32[2,128,256]{2,1,0:T(8,128)S(1)} %get-tuple-element.32.raw_ref, ...), custom_call_target="tpu_custom_call" | custom-call | flops 2516582400 | bytes 2533376 | tf_op jit(solution)/shard_map/pallas_call | solution.py:407
  31.8 17.6 %psum.21.sums_ref = f32[2,128]{1,0:T(2,128)S(1)} all-reduce(f32[2,128]{1,0:T(2,128)S(1)} %get-tuple-element.33), channel_id=1, replica_groups=mesh['ctx'=64,'head'=8] {'head'}, use_global_device_ids=true, to_apply=%region_0.0 | all-reduce | flops 256 | bytes 2048 | tf_op jit(solution)/shard_map/psum | solution.py:467
  49.4 2.5 %shard_map.138 = (bf16[128,256]{1,0:T(8,128)(2,1)}, f32[1,256]{1,0:T(1,128)S(1)}, bf16[2,128,256]{2,1,0:T(8,128)(2,1)S(1)}, f32[128,256]{1,0:T(8,128)S(1)}, bf16...) custom-call(f32[2,128]{1,0:T(2,128)S(1)} %psum.21.sums_ref, ...), custom_call_target="tpu_custom_call" | custom-call | flops 251658240 | bytes 3320832 | tf_op jit(solution)/shard_map/pallas_call | solution.py:407
  51.9 1.9 %collective-permute-start.4 = (bf16[128,768]{1,0:T(8,128)(2,1)}, bf16[128,768]{1,0:T(8,128)(2,1)S(1)}, u32[]{:S(2)}, u32[]{:S(2)}) collective-permute-start(bf16[128,768]{1,0:T(8,128)(2,1)} %get-tuple-element.43), channel_id=1, source_target_pairs={{8,0},{16,8},{24,16},{32,24},{40,32},{48,40},{56,48},{64,56},{72,6... | collective-permute-start | bytes 589832 | tf_op jit(solution)/shard_map/ppermute | solution.py:420
  53.8 4.3 %collective-permute-start.5 = (bf16[128,768]{1,0:T(8,128)(2,1)S(1)}, bf16[128,768]{1,0:T(8,128)(2,1)S(1)}, u32[]{:S(2)}, u32[]{:S(2)}) collective-permute-start(bf16[128,768]{1,0:T(8,128)(2,1)S(1)} %get-tuple-element.44), channel_id=1, source_target_pairs={{16,0},{24,8},{32,16},{40,24},{48,32},{56,40},{64,48},{72,56},{80,... | collective-permute-start | bytes 589832 | tf_op jit(solution)/shard_map/ppermute | solution.py:420
  58.1 2.7 %collective-permute-start.6 = (bf16[128,768]{1,0:T(8,128)(2,1)S(1)}, bf16[128,768]{1,0:T(8,128)(2,1)S(1)}, u32[]{:S(2)}, u32[]{:S(2)}) collective-permute-start(bf16[128,768]{1,0:T(8,128)(2,1)S(1)} %get-tuple-element.45), channel_id=1, source_target_pairs={{24,0},{32,8},{40,16},{48,24},{56,32},{64,40},{72,48},{80,56},{88,... | collective-permute-start | bytes 589832 | tf_op jit(solution)/shard_map/ppermute | solution.py:420
  60.7 1.9 %collective-permute-start.7 = (bf16[128,512]{1,0:T(8,128)(2,1)}, bf16[128,512]{1,0:T(8,128)(2,1)S(1)}, u32[]{:S(2)}, u32[]{:S(2)}) collective-permute-start(bf16[128,512]{1,0:T(8,128)(2,1)} %get-tuple-element.46), channel_id=1, source_target_pairs={{32,0},{40,8},{48,16},{56,24},{64,32},{72,40},{80,48},{88,56},{96,... | collective-permute-start | bytes 393224 | tf_op jit(solution)/shard_map/ppermute | solution.py:420
  62.7 14.8 %psum.22 = f32[1,256]{1,0:T(1,128)S(1)} all-reduce(f32[1,256]{1,0:T(1,128)S(1)} %get-tuple-element.56), channel_id=1, replica_groups={{0,8,16,24,32,40,48,56},{64,72,80,88,96,104,112,120},{128,136,144,152,1..., use_global_device_ids=true, to_apply=%region_1.0 | all-reduce | flops 256 | bytes 2048 | tf_op jit(solution)/shard_map/psum | solution.py:427
  77.5 23.7 %psum.23 = f32[256]{0:T(256)} all-reduce(f32[256]{0:T(256)S(1)} %bitcast.5), channel_id=1, replica_groups={{0,64,128,192,256,320,384,448},{8,72,136,200,264,328,392,456},{16,80,14..., use_global_device_ids=true, to_apply=%region_2.0 | all-reduce | flops 256 | bytes 2048 | tf_op jit(solution)/shard_map/psum | solution.py:428
  101.2 1.2 %shard_map.139 = (bf16[128,256]{1,0:T(8,128)(2,1)}, f32[2,128,128]{2,1,0:T(8,128)S(1)}, f32[2,128,128]{2,1,0:T(8,128)S(1)}, f32[2,128,256]{2,1,0:T(8,128)S(1)}) custom-call(bf16[2,128,256]{2,1,0:T(8,128)(2,1)S(1)} %get-tuple-element.40.own_ref, bf16[2,128,256]{2,1,0:T(8,128)(2,1)S(1)} %get-tuple-element.41.kw_ref, bf16[128,256]{1,0:T(8,128)(2,1)S(1)} %copy-done.7, ...), custom_call_target="tpu_custom_call" | custom-call | flops 83886080 | bytes 1048576 | tf_op jit(solution)/shard_map/pallas_call | solution.py:407
  102.5 2.0 %shard_map.140 = (bf16[128,256]{1,0:T(8,128)(2,1)}, bf16[128,256]{1,0:T(8,128)(2,1)}, bf16[128,256]{1,0:T(8,128)(2,1)}, f32[2,128]{1,0:T(2,128)}) custom-call(bf16[128,768]{1,0:T(8,128)(2,1)S(1)} %collective-permute-done.4.recv1_ref, bf16[128,768]{1,0:T(8,128)(2,1)S(1)} %collective-permute-done.5.recv2_ref, ...), custom_call_target="tpu_custom_call" | custom-call | flops 167772160 | bytes 1902592 | tf_op jit(solution)/shard_map/pallas_call | solution.py:407
  (25 shorter events, 0.1 us)
Async XLA Ops:
  0.6 0.8 copy-start
  1.5 0.8 copy-start.2
  2.3 0.8 copy-start.4
  3.2 0.7 copy-start.8
  3.8 15.3 %copy-start.1 = (bf16[128,256]{1,0:T(8,128)(2,1)S(1)}, bf16[128,256]{1,0:T(8,128)(2,1)}, u32[]{:S(2)}) copy-start(bf16[128,256]{1,0:T(8,128)(2,1)} %key_ref.7) | copy-start | bytes 196612
  3.8 15.3 %copy-start.3 = (bf16[128,256]{1,0:T(8,128)(2,1)S(1)}, bf16[128,256]{1,0:T(8,128)(2,1)}, u32[]{:S(2)}) copy-start(bf16[128,256]{1,0:T(8,128)(2,1)} %dir_ref.7) | copy-start | bytes 196612
  3.8 15.3 %copy-start.7 = (bf16[128,256]{1,0:T(8,128)(2,1)S(1)}, bf16[128,256]{1,0:T(8,128)(2,1)}, u32[]{:S(2)}) copy-start(bf16[128,256]{1,0:T(8,128)(2,1)} %query_ref.3) | copy-start | bytes 196612
  3.9 18.9 %collective-permute-start.3 = (bf16[144,768]{1,0:T(8,128)(2,1)S(1)}, bf16[144,768]{1,0:T(8,128)(2,1)S(1)}, u32[]{:S(2)}, u32[]{:S(2)}) collective-permute-start(bf16[144,768]{1,0:T(8,128)(2,1)S(1)} %shard_map.136), channel_id=1, source_target_pairs={{0,32},{8,40},{16,48},{24,56},{32,64},{40,72},{48,80},{56,88},{64,... | collective-permute-start | bytes 663560 | tf_op jit(solution)/shard_map/ppermute | solution.py:420
  9.1 13.6 %collective-permute-start.2 = (bf16[144,768]{1,0:T(8,128)(2,1)S(1)}, bf16[144,768]{1,0:T(8,128)(2,1)S(1)}, u32[]{:S(2)}, u32[]{:S(2)}) collective-permute-start(bf16[144,768]{1,0:T(8,128)(2,1)S(1)} %shard_map.136), channel_id=1, source_target_pairs={{0,24},{8,32},{16,40},{24,48},{32,56},{40,64},{48,72},{56,80},{64,... | collective-permute-start | bytes 663560 | tf_op jit(solution)/shard_map/ppermute | solution.py:420
  12.3 11.1 %collective-permute-start.1 = (bf16[144,768]{1,0:T(8,128)(2,1)S(1)}, bf16[144,768]{1,0:T(8,128)(2,1)S(1)}, u32[]{:S(2)}, u32[]{:S(2)}) collective-permute-start(bf16[144,768]{1,0:T(8,128)(2,1)S(1)} %shard_map.136), channel_id=1, source_target_pairs={{0,16},{8,24},{16,32},{24,40},{32,48},{40,56},{48,64},{56,72},{64,... | collective-permute-start | bytes 663560 | tf_op jit(solution)/shard_map/ppermute | solution.py:420
  15.1 9.8 %collective-permute-start = (bf16[144,768]{1,0:T(8,128)(2,1)S(1)}, bf16[144,768]{1,0:T(8,128)(2,1)S(1)}, u32[]{:S(2)}, u32[]{:S(2)}) collective-permute-start(bf16[144,768]{1,0:T(8,128)(2,1)S(1)} %shard_map.136), channel_id=1, source_target_pairs={{0,8},{8,16},{16,24},{24,32},{32,40},{40,48},{48,56},{56,64},{64,7... | collective-permute-start | bytes 663560 | tf_op jit(solution)/shard_map/ppermute | solution.py:420
  19.1 0.7 copy-start.9
  19.8 5.1 %copy-start.5 = (bf16[128,256]{1,0:T(8,128)(2,1)S(1)}, bf16[128,256]{1,0:T(8,128)(2,1)}, u32[]{:S(2)}) copy-start(bf16[128,256]{1,0:T(8,128)(2,1)} %value_ref.5) | copy-start | bytes 196612
  19.8 5.1 %copy-start.6 = (bf16[128,256]{1,0:T(8,128)(2,1)S(1)}, bf16[128,256]{1,0:T(8,128)(2,1)}, u32[]{:S(2)}) copy-start(bf16[128,256]{1,0:T(8,128)(2,1)} %cot_ref.3) | copy-start | bytes 196612
  24.9 0.7 copy-start.10
  24.9 0.7 copy-start.11
  51.9 50.6 %collective-permute-start.4 = (bf16[128,768]{1,0:T(8,128)(2,1)}, bf16[128,768]{1,0:T(8,128)(2,1)S(1)}, u32[]{:S(2)}, u32[]{:S(2)}) collective-permute-start(bf16[128,768]{1,0:T(8,128)(2,1)} %get-tuple-element.43), channel_id=1, source_target_pairs={{8,0},{16,8},{24,16},{32,24},{40,32},{48,40},{56,48},{64,56},{72,6... | collective-permute-start | bytes 589832 | tf_op jit(solution)/shard_map/ppermute | solution.py:420
  53.8 48.7 %collective-permute-start.5 = (bf16[128,768]{1,0:T(8,128)(2,1)S(1)}, bf16[128,768]{1,0:T(8,128)(2,1)S(1)}, u32[]{:S(2)}, u32[]{:S(2)}) collective-permute-start(bf16[128,768]{1,0:T(8,128)(2,1)S(1)} %get-tuple-element.44), channel_id=1, source_target_pairs={{16,0},{24,8},{32,16},{40,24},{48,32},{56,40},{64,48},{72,56},{80,... | collective-permute-start | bytes 589832 | tf_op jit(solution)/shard_map/ppermute | solution.py:420
  58.1 44.4 %collective-permute-start.6 = (bf16[128,768]{1,0:T(8,128)(2,1)S(1)}, bf16[128,768]{1,0:T(8,128)(2,1)S(1)}, u32[]{:S(2)}, u32[]{:S(2)}) collective-permute-start(bf16[128,768]{1,0:T(8,128)(2,1)S(1)} %get-tuple-element.45), channel_id=1, source_target_pairs={{24,0},{32,8},{40,16},{48,24},{56,32},{64,40},{72,48},{80,56},{88,... | collective-permute-start | bytes 589832 | tf_op jit(solution)/shard_map/ppermute | solution.py:420
  60.7 41.7 %collective-permute-start.7 = (bf16[128,512]{1,0:T(8,128)(2,1)}, bf16[128,512]{1,0:T(8,128)(2,1)S(1)}, u32[]{:S(2)}, u32[]{:S(2)}) collective-permute-start(bf16[128,512]{1,0:T(8,128)(2,1)} %get-tuple-element.46), channel_id=1, source_target_pairs={{32,0},{40,8},{48,16},{56,24},{64,32},{72,40},{80,48},{88,56},{96,... | collective-permute-start | bytes 393224 | tf_op jit(solution)/shard_map/ppermute | solution.py:420

commit v2 on v1

--- a/solution.py
+++ b/solution.py
@@ -99,21 +99,50 @@
     ]
 
 
-def pack_kernel(key_ref, dir_ref, value_ref, rate_ref, out_ref):
+def pack_kernel(key_ref, dir_ref, value_ref, rate_ref, out_ref, rate_in, rate_out, sems):
     size, width = key_ref.shape
-    out_ref[0:size, 0:width] = key_ref[...]
-    out_ref[0:size, width : 2 * width] = dir_ref[...]
-    out_ref[0:size, 2 * width : 3 * width] = value_ref[...]
     heads = rate_ref.shape[0]
-    rate = jnp.concatenate([rate_ref[h : h + 1, :] for h in range(heads)], axis=1)
+    bring = pltpu.make_async_copy(rate_ref, rate_in, sems.at[0])
+    bring.start()
+    copies = [
+        pltpu.make_async_copy(
+            ref, out_ref.at[pl.ds(0, size), pl.ds(at * width, width)], sems.at[at + 1]
+        )
+        for at, ref in enumerate((key_ref, dir_ref, value_ref))
+    ]
+    for copy in copies:
+        copy.start()
+    bring.wait()
+    rate = jnp.concatenate([rate_in[h : h + 1, :] for h in range(heads)], axis=1)
     first = rate.astype(BF16).astype(F32)
     rest = rate - first
     second = rest.astype(BF16).astype(F32)
     third = rest - second
     row = lax.broadcasted_iota(jnp.int32, (16, width), 0)
     pieces = jnp.where(row == 0, first, jnp.where(row == 1, second, jnp.where(row == 2, third, 0.0)))
-    out_ref[size : size + 16, 0:width] = pieces.astype(BF16)
-    out_ref[size : size + 16, width : 3 * width] = jnp.zeros((16, 2 * width), BF16)
+    rate_out[:, 0:width] = pieces.astype(BF16)
+    rate_out[:, width : 3 * width] = jnp.zeros((16, 2 * width), BF16)
+    last = pltpu.make_async_copy(rate_out, out_ref.at[pl.ds(size, 16)], sems.at[4])
+    last.start()
+    for copy in copies:
+        copy.wait()
+    last.wait()
+
+
+def pack(keys, dirs, values, rates):
+    size, width = keys.shape
+    anywhere = pl.BlockSpec(memory_space=pl.ANY)
+    return pl.pallas_call(
+        pack_kernel,
+        out_shape=jax.ShapeDtypeStruct((size + 16, 3 * width), BF16),
+        in_specs=[anywhere] * 4,
+        out_specs=anywhere,
+        scratch_shapes=[
+            pltpu.VMEM(rates.shape, F32),
+            pltpu.VMEM((16, 3 * width), BF16),
+            pltpu.SemaphoreType.DMA((5,)),
+        ],
+    )(keys, dirs, values, rates)
 
 
 def own_kernel(query_ref, key_ref, dir_ref, rate_ref, inv_ref, kw_ref, raw_ref):
@@ -143,26 +172,43 @@
     value_ref,
     cot_ref,
     gain_ref,
-    halo1_ref,
     halo2_ref,
-    halo3_ref,
     halo4_ref,
+    even_ref,
+    cross2_ref,
+    cross4_ref,
     len_ref,
-    first_ref,
+    place_ref,
     att_ref,
     tot_ref,
     prob_ref,
     frame_ref,
     kt_ref,
     sums_ref,
+    far_ref,
+    halo1_ref,
+    halo3_ref,
 ):
     size = value_ref.shape[0]
     width = heads * DH
+
+    @pl.when(place_ref[1] == 0)
+    def _():
+        halo1_ref[...] = cross2_ref[...]
+        halo3_ref[...] = cross4_ref[...]
+
+    @pl.when(place_ref[1] != 0)
+    def _():
+        halo1_ref[...] = even_ref[...]
+        halo3_ref[...] = cross2_ref[...]
+
     halos = (halo1_ref, halo2_ref, halo3_ref, halo4_ref)
+    for s in range(WIN):
+        far_ref[s] = halos[s][0:size, 2 * width : 3 * width]
     rows, cols = grids(size)
     eye = rows == cols
     eye_f = jnp.where(eye, 1.0, 0.0)
-    first = first_ref[0]
+    first = place_ref[0]
     pos_row = first + lax.broadcasted_iota(jnp.int32, (1, size), 1)
     start_row = jnp.zeros((1, size), jnp.int32)
     end = jnp.int32(0)
@@ -231,8 +277,8 @@
         weighted = cot_ref[:, lanes].astype(F32) * gain_ref[:, lanes]
         square = square + jnp.sum(att * att, axis=1, keepdims=True)
         inner = inner + jnp.sum(weighted * att, axis=1, keepdims=True)
-    sums_ref[0:1, :] = to_row(square, eye)
-    sums_ref[1:2, :] = to_row(inner, eye)
+    row = jnp.concatenate([to_row(square, eye), to_row(inner, eye)], axis=1)
+    sums_ref[...] = jnp.broadcast_to(row, sums_ref.shape)
 
 
 def back_kernel(
@@ -247,10 +293,7 @@
     value_ref,
     cot_ref,
     gain_ref,
-    halo1_ref,
-    halo2_ref,
-    halo3_ref,
-    halo4_ref,
+    far_ref,
     normed_ref,
     part_ref,
     own_ref,
@@ -262,12 +305,12 @@
 ):
     size = value_ref.shape[0]
     width = heads * DH
-    halos = (halo1_ref, halo2_ref, halo3_ref, halo4_ref)
     sends = (send1_ref, send2_ref, send3_ref, send4_ref)
     rows, cols = grids(size)
     eye = rows == cols
-    square = to_col(sums_ref[0:1, :], eye)
-    inner = to_col(sums_ref[1:2, :], eye)
+    sums = jnp.sum(sums_ref[...], axis=0, keepdims=True)
+    square = to_col(sums[:, 0:size], eye)
+    inner = to_col(sums[:, size : 2 * size], eye)
     inverse = lax.rsqrt(square / features + EPSILON)
     pull = inverse * inverse * inverse * inner / features
     att_all = att_ref[...]
@@ -275,7 +318,7 @@
     gain = gain_ref[...]
     normed = att_all * inverse
     normed_ref[...] = (normed * gain).astype(BF16)
-    part_ref[...] = jnp.sum(cot_all * normed, axis=0, keepdims=True)
+    part_ref[...] = jnp.broadcast_to(jnp.sum(cot_all * normed, axis=0, keepdims=True), part_ref.shape)
     grad_att = cot_all * gain * inverse - att_all * pull
     scale = DH ** (-0.5)
     for h in range(heads):
@@ -289,7 +332,7 @@
             if s == 0:
                 value = value_ref[:, lanes]
             else:
-                value = halos[s - 1][0:size, 2 * width + h * DH : 2 * width + (h + 1) * DH]
+                value = far_ref[s - 1, :, lanes]
             prob = prob_ref[h, s]
             through = mm(scaled, value, "nt")
             dscore = (prob.astype(F32) * ((through - delta) * scale)).astype(BF16)
@@ -348,10 +391,12 @@
     key_ref,
     dir_ref,
     rate_ref,
+    parts_ref,
     dkey_ref,
     dvalue_ref,
     ddir_ref,
     drate_ref,
+    dgain_ref,
 ):
     size = key_ref.shape[0]
     width = heads * DH
@@ -363,6 +408,7 @@
     for s in range(WIN):
         dvalue = dvalue + recvs[s][:, 0:width].astype(F32)
     dvalue_ref[...] = dvalue.astype(BF16)
+    dgain_ref[...] = jnp.sum(parts_ref[...], axis=0, keepdims=True)
     for h in range(heads):
         lanes = slice(h * DH, (h + 1) * DH)
         keys = key_ref[:, lanes]
@@ -398,7 +444,7 @@
         ddir_ref[:, lanes] = (norm_col * (dunit - unit * along)).astype(BF16)
 
 
-def call(body, outs, flops, *operands, scalars=()):
+def call(body, outs, flops, *operands, scalars=(), scratch=()):
     vmem = pl.BlockSpec(memory_space=pltpu.VMEM)
     smem = pl.BlockSpec(memory_space=pltpu.SMEM)
     moved = sum(x.size * x.dtype.itemsize for x in operands) + sum(
@@ -409,6 +455,7 @@
         out_shape=[jax.ShapeDtypeStruct(s, d) for s, d in outs],
         in_specs=[vmem] * len(operands) + [smem] * len(scalars),
         out_specs=[vmem] * len(outs),
+        scratch_shapes=list(scratch),
         compiler_params=pltpu.CompilerParams(vmem_limit_bytes=VMEM_LIMIT),
         cost_estimate=pl.CostEstimate(flops=flops, bytes_accessed=moved, transcendentals=0),
     )(*operands, *scalars)
@@ -420,12 +467,18 @@
     return lax.ppermute(value, "ctx", [(source, source + steps) for source in range(first, last)])
 
 
-def grouped_sum(value, axis, width):
-    count = lax.axis_size(axis)
-    inner = [[g * width + i for i in range(width)] for g in range(count // width)]
-    outer = [[g * width + i for g in range(count // width)] for i in range(width)]
-    value = lax.psum(value, axis, axis_index_groups=inner)
-    return lax.psum(value, axis, axis_index_groups=outer)
+def paired(value, first, step):
+    count = lax.axis_size("ctx")
+    return lax.ppermute(value, "ctx", [(source, source + step) for source in range(first, count, 2)])
+
+
+def swapped(value):
+    count = lax.axis_size("ctx")
+    return lax.ppermute(value, "ctx", [(source, source ^ 1) for source in range(count)])
+
+
+def gathered(value, axis):
+    return lax.all_to_all(value, axis, 0, 0, tiled=True)
 
 
 def per_device(query, keys, values, dirs, rates, gain, doc_lengths, cotangent):
@@ -433,10 +486,13 @@
     heads = width // DH
     features = width * lax.axis_size("head")
     gain_row = gain.reshape(1, width)
-    first = (lax.axis_index("ctx") * size).astype(jnp.int32).reshape(1)
+    ctx = lax.axis_index("ctx").astype(jnp.int32)
+    place = jnp.stack([ctx * size, ctx % 2])
     unit_flops = 2 * size * size * DH
-    (packed,) = call(pack_kernel, [((size + 16, 3 * width), BF16)], 0, keys, dirs, values, rates)
-    halos = [passed_along(packed, s) for s in range(1, WIN + 1)]
+    packed = pack(keys, dirs, values, rates)
+    halo2 = passed_along(packed, 2)
+    halo4 = passed_along(packed, 4)
+    halos = (halo2, halo4, paired(packed, 0, 1), swapped(halo2), paired(halo4, 1, -1))
     inverse, coef, raw = call(
         own_kernel,
         [((heads, size, size), BF16), ((heads, size, 2 * DH), BF16), ((heads, size, 2 * DH), F32)],
@@ -446,7 +502,7 @@
         dirs,
         rates,
     )
-    att, total, prob, frame, carry, sums = call(
+    att, total, prob, frame, carry, sums, far = call(
         functools.partial(attend_kernel, heads),
         [
             ((size, width), F32),
@@ -454,7 +510,8 @@
             ((heads, WIN + 1, size, size), BF16),
             ((heads, WIN, size, DH), BF16),
             ((heads, WIN, DH, 2 * DH), BF16),
-            ((2, size), F32),
+            ((lax.axis_size("head"), 2 * size), F32),
+            ((WIN, size, width), BF16),
         ],
         heads * 300 * unit_flops,
         raw,
@@ -462,14 +519,15 @@
         cotangent,
         gain_row,
         *halos,
-        scalars=(doc_lengths, first),
-    )
-    sums = lax.psum(sums, "head")
+        scalars=(doc_lengths, place),
+        scratch=[pltpu.VMEM((size + 16, 3 * width), BF16)] * 2,
+    )
+    sums = gathered(sums, "head")
     normed, part, own, dval, *sends = call(
         functools.partial(back_kernel, heads, features),
         [
             ((size, width), BF16),
-            ((1, width), F32),
+            ((lax.axis_size("ctx"), width), F32),
             ((heads, size, 2 * DH), BF16),
             ((size, width), F32),
             ((size, 3 * width), BF16),
@@ -487,7 +545,7 @@
         values,
         cotangent,
         gain_row,
-        *halos,
+        far,
     )
     recvs = [passed_along(sends[s - 1], -s) for s in range(1, WIN + 1)]
     dquery, dkey_part, ddir_part, pulled = call(
@@ -505,10 +563,10 @@
         keys,
         dirs,
     )
-    grad_gain = grouped_sum(part, "ctx", 8).reshape(width)
-    dkey, dvalue, ddir, drate = call(
+    parts = gathered(part, "ctx")
+    dkey, dvalue, ddir, drate, dgain = call(
         functools.partial(shard_kernel, heads),
-        [((size, width), BF16), ((size, width), BF16), ((size, width), BF16), ((heads, size), F32)],
+        [((size, width), BF16), ((size, width), BF16), ((size, width), BF16), ((heads, size), F32), ((1, width), F32)],
         heads * 20 * unit_flops,
         *recvs,
         inverse,
@@ -520,8 +578,9 @@
         keys,
         dirs,
         rates,
-    )
-    return normed, dquery, dkey, dvalue, ddir, drate, grad_gain
+        parts,
+    )
+    return normed, dquery, dkey, dvalue, ddir, drate, dgain.reshape(width)
 
 
 def solution(mesh):

time: 106 us -> 93.7 us (0.88)
  the two profiles are of different devices: /device:TPU:6 before, /device:TPU:1 now
where the time goes in v2:
time: 93.7 us; the launch traced here: 93.2 us
  starting transfers between devices  46.3 us (49%)
  Pallas kernels  21.9 us (23%)
  blocking collectives  13.2 us (14%)
  waiting for transfers between devices  8.88 us (9%)
  local copies, waits for them, and re-layouts  2.02 us (2%)
    all_to_all x1, starting transfers between devices, gathered(): return lax.all_to_all(value, axis, 0, 0, tiled=True)  21.1 us
    ppermute x6, starting transfers between devices, passed_along(): lax.ppermute(value, 'ctx', [(source, source + steps) for source in range(...  14.9 us
    pallas_call x5, Pallas kernels, call(): pl.pallas_call(body, out_shape=[jax.ShapeDtypeStruct(s, d) for s, d in ou...  14.7 us
    all_to_all x1, blocking collectives, gathered(): return lax.all_to_all(value, axis, 0, 0, tiled=True)  13.2 us
    all_to_all x1, waiting for transfers between devices, gathered(): return lax.all_to_all(value, axis, 0, 0, tiled=True)  8.86 us
    ppermute x2, starting transfers between devices, paired(): lax.ppermute(value, 'ctx', [(source, source + step) for source in range(f...  7.95 us
    pallas_call x1, Pallas kernels, pack(): pl.pallas_call(pack_kernel, out_shape=jax.ShapeDtypeStruct((size + 16, 3...  7.11 us
    ppermute x1, starting transfers between devices, swapped(): lax.ppermute(value, 'ctx', [(source, source ^ 1) for source in range(coun...  2.34 us
  transfers between devices with their start and end apart: 10, of which 1 were waited for; matrix products, arithmetic and copies ran while one was open for 1% of the time, Pallas kernels for 4%

profile of v2, /device:TPU:1, one launch (start us, length us, event | category | flops | bytes accessed | tf_op | source)
XLA Modules:
  0.0 93.2 jit_solution(472349162781006200)
XLA Ops:
  0.7 7.1 %shard_map.136 = bf16[144,768]{1,0:T(8,128)(2,1)} custom-call(bf16[128,256]{1,0:T(8,128)(2,1)} %key_ref.7, bf16[128,256]{1,0:T(8,128)(2,1)} %dir_ref.7, bf16[128,256]{1,0:T(8,128)(2,1)} %value_ref.5, f32[2,128]{1,0:T(2,128)} %rate_ref.5), custom_call_target="tpu_custom_call" | custom-call | tf_op jit(solution)/shard_map/pallas_call | solution.py:135
  7.8 5.5 %collective-permute-start.1 = (bf16[144,768]{1,0:T(8,128)(2,1)}, bf16[144,768]{1,0:T(8,128)(2,1)S(1)}, u32[]{:S(2)}, u32[]{:S(2)}) collective-permute-start(bf16[144,768]{1,0:T(8,128)(2,1)} %shard_map.136), channel_id=1, source_target_pairs={{0,32},{8,40},{16,48},{24,56},{32,64},{40,72},{48,80},{56,88},{64,... | collective-permute-start | bytes 663560 | tf_op jit(solution)/shard_map/ppermute | solution.py:467
  13.3 2.2 %collective-permute-start = (bf16[144,768]{1,0:T(8,128)(2,1)}, bf16[144,768]{1,0:T(8,128)(2,1)S(1)}, u32[]{:S(2)}, u32[]{:S(2)}) collective-permute-start(bf16[144,768]{1,0:T(8,128)(2,1)} %shard_map.136), channel_id=1, source_target_pairs={{0,16},{8,24},{16,32},{24,40},{32,48},{40,56},{48,64},{56,72},{64,... | collective-permute-start | bytes 663560 | tf_op jit(solution)/shard_map/ppermute | solution.py:467
  15.5 1.3 %collective-permute-start.2 = (bf16[144,768]{1,0:T(8,128)(2,1)}, bf16[144,768]{1,0:T(8,128)(2,1)S(1)}, u32[]{:S(2)}, u32[]{:S(2)}) collective-permute-start(bf16[144,768]{1,0:T(8,128)(2,1)} %shard_map.136), channel_id=1, source_target_pairs={{0,8},{16,24},{32,40},{48,56},{64,72},{80,88},{96,104},{112,120},{... | collective-permute-start | bytes 663560 | tf_op jit(solution)/shard_map/ppermute | solution.py:472
  16.8 6.7 %collective-permute-start.4 = (bf16[144,768]{1,0:T(8,128)(2,1)S(1)}, bf16[144,768]{1,0:T(8,128)(2,1)S(1)}, u32[]{:S(2)}, u32[]{:S(2)}) collective-permute-start(bf16[144,768]{1,0:T(8,128)(2,1)S(1)} %collective-permute-done.1.halo4_ref), channel_id=1, source_target_pairs={{8,0},{24,16},{40,32},{56,48},{72,64},{88,80},{104,96},{120,112},{... | collective-permute-start | bytes 663560 | tf_op jit(solution)/shard_map/ppermute | solution.py:472
  23.5 2.3 %collective-permute-start.3 = (bf16[144,768]{1,0:T(8,128)(2,1)S(1)}, bf16[144,768]{1,0:T(8,128)(2,1)S(1)}, u32[]{:S(2)}, u32[]{:S(2)}) collective-permute-start(bf16[144,768]{1,0:T(8,128)(2,1)S(1)} %collective-permute-done.halo2_ref), channel_id=1, source_target_pairs={{0,8},{8,0},{16,24},{24,16},{32,40},{40,32},{48,56},{56,48},{64,72... | collective-permute-start | bytes 663560 | tf_op jit(solution)/shard_map/ppermute | solution.py:477
  25.9 0.0 copy-start.5
  25.9 0.6 copy-done.5
  26.5 3.0 %shard_map.135 = (bf16[2,128,128]{2,1,0:T(8,128)(2,1)S(1)}, bf16[2,128,256]{2,1,0:T(8,128)(2,1)S(1)}, f32[2,128,256]{2,1,0:T(8,128)S(1)}) custom-call(bf16[128,256]{1,0:T(8,128)(2,1)S(1)} %copy-done.4, bf16[128,256]{1,0:T(8,128)(2,1)S(1)} %copy-done, bf16[128,256]{1,0:T(8,128)(2,1)S(1)} %copy-done.1, f32[2,128]{1,0:T(2,128)S(1)} %copy-done.5), custom_call_target="tpu_custom_call" | custom-call | flops 503316480 | bytes 656384 | tf_op jit(solution)/shard_map/pallas_call | solution.py:453
  29.5 0.1 pad_add_fusion.place_ref
  29.6 0.0 copy-start.6
  29.6 0.6 copy-done.6
  30.3 6.3 %shard_map.137 = (f32[128,256]{1,0:T(8,128)S(1)}, f32[2,128,8]{2,1,0:T(8,128)S(1)}, bf16[2,5,128,128]{3,2,1,0:T(8,128)(2,1)S(1)}, bf16[2,4,128,128]{3,2,1,0:T(8,...) custom-call(f32[2,128,256]{2,1,0:T(8,128)S(1)} %get-tuple-element.34.raw, ...), custom_call_target="tpu_custom_call" | custom-call | flops 2516582400 | bytes 3023872 | tf_op jit(solution)/shard_map/pallas_call | solution.py:453
  36.6 13.2 %all_to_all.22 = f32[8,1,256]{2,1,0:T(1,128)S(1)} all-to-all(f32[8,1,256]{2,1,0:T(1,128)S(1)} %copy.15), channel_id=1, replica_groups=mesh['ctx'=64,'head'=8] {'head'}, dimensions={0} | all-to-all | bytes 16384 | tf_op jit(solution)/shard_map/all_to_all | solution.py:481
  49.8 2.2 %shard_map.138 = (bf16[128,256]{1,0:T(8,128)(2,1)}, f32[64,256]{1,0:T(8,128)S(1)}, bf16[2,128,256]{2,1,0:T(8,128)(2,1)S(1)}, f32[128,256]{1,0:T(8,128)S(1)}, bf1...) custom-call(f32[8,256]{1,0:T(8,128)S(1)} %bitcast.14, ...), custom_call_target="tpu_custom_call" | custom-call | flops 251658240 | bytes 2769920 | tf_op jit(solution)/shard_map/pallas_call | solution.py:453
  52.0 3.3 %collective-permute-start.5 = (bf16[128,768]{1,0:T(8,128)(2,1)S(1)}, bf16[128,768]{1,0:T(8,128)(2,1)S(1)}, u32[]{:S(2)}, u32[]{:S(2)}) collective-permute-start(bf16[128,768]{1,0:T(8,128)(2,1)S(1)} %get-tuple-element.46), channel_id=1, source_target_pairs={{8,0},{16,8},{24,16},{32,24},{40,32},{48,40},{56,48},{64,56},{72,6... | collective-permute-start | bytes 589832 | tf_op jit(solution)/shard_map/ppermute | solution.py:467
  55.3 1.3 %collective-permute-start.6 = (bf16[128,768]{1,0:T(8,128)(2,1)S(1)}, bf16[128,768]{1,0:T(8,128)(2,1)S(1)}, u32[]{:S(2)}, u32[]{:S(2)}) collective-permute-start(bf16[128,768]{1,0:T(8,128)(2,1)S(1)} %get-tuple-element.47), channel_id=1, source_target_pairs={{16,0},{24,8},{32,16},{40,24},{48,32},{56,40},{64,48},{72,56},{80,... | collective-permute-start | bytes 589832 | tf_op jit(solution)/shard_map/ppermute | solution.py:467
  56.6 1.3 %collective-permute-start.7 = (bf16[128,768]{1,0:T(8,128)(2,1)S(1)}, bf16[128,768]{1,0:T(8,128)(2,1)S(1)}, u32[]{:S(2)}, u32[]{:S(2)}) collective-permute-start(bf16[128,768]{1,0:T(8,128)(2,1)S(1)} %get-tuple-element.48), channel_id=1, source_target_pairs={{24,0},{32,8},{40,16},{48,24},{56,32},{64,40},{72,48},{80,56},{88,... | collective-permute-start | bytes 589832 | tf_op jit(solution)/shard_map/ppermute | solution.py:467
  57.9 1.3 %collective-permute-start.8 = (bf16[128,512]{1,0:T(8,128)(2,1)S(1)}, bf16[128,512]{1,0:T(8,128)(2,1)S(1)}, u32[]{:S(2)}, u32[]{:S(2)}) collective-permute-start(bf16[128,512]{1,0:T(8,128)(2,1)S(1)} %get-tuple-element.49), channel_id=1, source_target_pairs={{32,0},{40,8},{48,16},{56,24},{64,32},{72,40},{80,48},{88,56},{96,... | collective-permute-start | bytes 393224 | tf_op jit(solution)/shard_map/ppermute | solution.py:467
  59.2 0.7 copy.16
  59.9 21.1 %all-to-all-start.1 = ((f32[64,1,256]{2,1,0:T(1,128)}), f32[64,1,256]{2,1,0:T(1,128)S(1)}, u32[]{:S(2)}, u32[]{:S(2)}) async-start(f32[64,1,256]{2,1,0:T(1,128)} %copy.16), calls=%async_computation.1 | async-start | bytes 131072 | tf_op jit(solution)/shard_map/all_to_all | solution.py:481
  81.1 1.2 %shard_map.139 = (bf16[128,256]{1,0:T(8,128)(2,1)}, f32[2,128,128]{2,1,0:T(8,128)S(1)}, f32[2,128,128]{2,1,0:T(8,128)S(1)}, f32[2,128,256]{2,1,0:T(8,128)S(1)}) custom-call(bf16[2,128,256]{2,1,0:T(8,128)(2,1)S(1)} %get-tuple-element.43.own_ref, bf16[2,128,256]{2,1,0:T(8,128)(2,1)S(1)} %get-tuple-element.44.kw_ref, bf16[128,256]{1,0:T(8,128)(2,1)S(1)} %copy-done.4, ...), custom_call_target="tpu_custom_call" | custom-call | flops 83886080 | bytes 1048576 | tf_op jit(solution)/shard_map/pallas_call | solution.py:453
  82.3 8.9 %all-to-all-done.1 = f32[64,1,256]{2,1,0:T(1,128)S(1)} async-done(((f32[64,1,256]{2,1,0:T(1,128)}), f32[64,1,256]{2,1,0:T(1,128)S(1)}, u32[]{:S(2)}, u32[]{:S(2)}) %all-to-all-start.1) | async-done | bytes 65568 | tf_op jit(solution)/shard_map/all_to_all | solution.py:481
  91.2 2.0 %shard_map.140 = (bf16[128,256]{1,0:T(8,128)(2,1)}, bf16[128,256]{1,0:T(8,128)(2,1)}, bf16[128,256]{1,0:T(8,128)(2,1)}, f32[2,128]{1,0:T(2,128)}, f32[1,256]{1,0:T(1,128)}) custom-call(bf16[128,768]{1,0:T(8,128)(2,1)S(1)} %collective-permute-done.5.recv1_ref, bf16[128,768]{1,0:T(8,128)(2,1)S(1)} %collective-permute-done.6.recv2_ref, ...), custom_call_target="tpu_custom_call" | custom-call | flops 167772160 | bytes 1969152 | tf_op jit(solution)/shard_map/pallas_call | solution.py:453
  (24 shorter events, 0.1 us)
Async XLA Ops:
  0.6 25.2 %copy-start.1 = (bf16[128,256]{1,0:T(8,128)(2,1)S(1)}, bf16[128,256]{1,0:T(8,128)(2,1)}, u32[]{:S(2)}) copy-start(bf16[128,256]{1,0:T(8,128)(2,1)} %dir_ref.7) | copy-start | bytes 196612
  0.6 25.2 %copy-start = (bf16[128,256]{1,0:T(8,128)(2,1)S(1)}, bf16[128,256]{1,0:T(8,128)(2,1)}, u32[]{:S(2)}) copy-start(bf16[128,256]{1,0:T(8,128)(2,1)} %key_ref.7) | copy-start | bytes 196612
  0.7 25.2 %copy-start.4 = (bf16[128,256]{1,0:T(8,128)(2,1)S(1)}, bf16[128,256]{1,0:T(8,128)(2,1)}, u32[]{:S(2)}) copy-start(bf16[128,256]{1,0:T(8,128)(2,1)} %query_ref.3) | copy-start | bytes 196612
  7.8 9.0 %collective-permute-start.1 = (bf16[144,768]{1,0:T(8,128)(2,1)}, bf16[144,768]{1,0:T(8,128)(2,1)S(1)}, u32[]{:S(2)}, u32[]{:S(2)}) collective-permute-start(bf16[144,768]{1,0:T(8,128)(2,1)} %shard_map.136), channel_id=1, source_target_pairs={{0,32},{8,40},{16,48},{24,56},{32,64},{40,72},{48,80},{56,88},{64,... | collective-permute-start | bytes 663560 | tf_op jit(solution)/shard_map/ppermute | solution.py:467
  13.3 10.2 %collective-permute-start = (bf16[144,768]{1,0:T(8,128)(2,1)}, bf16[144,768]{1,0:T(8,128)(2,1)S(1)}, u32[]{:S(2)}, u32[]{:S(2)}) collective-permute-start(bf16[144,768]{1,0:T(8,128)(2,1)} %shard_map.136), channel_id=1, source_target_pairs={{0,16},{8,24},{16,32},{24,40},{32,48},{40,56},{48,64},{56,72},{64,... | collective-permute-start | bytes 663560 | tf_op jit(solution)/shard_map/ppermute | solution.py:467
  15.5 14.1 %collective-permute-start.2 = (bf16[144,768]{1,0:T(8,128)(2,1)}, bf16[144,768]{1,0:T(8,128)(2,1)S(1)}, u32[]{:S(2)}, u32[]{:S(2)}) collective-permute-start(bf16[144,768]{1,0:T(8,128)(2,1)} %shard_map.136), channel_id=1, source_target_pairs={{0,8},{16,24},{32,40},{48,56},{64,72},{80,88},{96,104},{112,120},{... | collective-permute-start | bytes 663560 | tf_op jit(solution)/shard_map/ppermute | solution.py:472
  16.8 12.8 %collective-permute-start.4 = (bf16[144,768]{1,0:T(8,128)(2,1)S(1)}, bf16[144,768]{1,0:T(8,128)(2,1)S(1)}, u32[]{:S(2)}, u32[]{:S(2)}) collective-permute-start(bf16[144,768]{1,0:T(8,128)(2,1)S(1)} %collective-permute-done.1.halo4_ref), channel_id=1, source_target_pairs={{8,0},{24,16},{40,32},{56,48},{72,64},{88,80},{104,96},{120,112},{... | collective-permute-start | bytes 663560 | tf_op jit(solution)/shard_map/ppermute | solution.py:472
  23.5 6.1 %collective-permute-start.3 = (bf16[144,768]{1,0:T(8,128)(2,1)S(1)}, bf16[144,768]{1,0:T(8,128)(2,1)S(1)}, u32[]{:S(2)}, u32[]{:S(2)}) collective-permute-start(bf16[144,768]{1,0:T(8,128)(2,1)S(1)} %collective-permute-done.halo2_ref), channel_id=1, source_target_pairs={{0,8},{8,0},{16,24},{24,16},{32,40},{40,32},{48,56},{56,48},{64,72... | collective-permute-start | bytes 663560 | tf_op jit(solution)/shard_map/ppermute | solution.py:477
  25.9 0.7 copy-start.5
  26.5 3.1 %copy-start.2 = (bf16[128,256]{1,0:T(8,128)(2,1)S(1)}, bf16[128,256]{1,0:T(8,128)(2,1)}, u32[]{:S(2)}) copy-start(bf16[128,256]{1,0:T(8,128)(2,1)} %value_ref.5) | copy-start | bytes 196612
  26.5 3.1 %copy-start.3 = (bf16[128,256]{1,0:T(8,128)(2,1)S(1)}, bf16[128,256]{1,0:T(8,128)(2,1)}, u32[]{:S(2)}) copy-start(bf16[128,256]{1,0:T(8,128)(2,1)} %cot_ref.3) | copy-start | bytes 196612
  29.6 0.7 copy-start.6
  29.6 0.7 copy-start.7
  52.0 39.2 %collective-permute-start.5 = (bf16[128,768]{1,0:T(8,128)(2,1)S(1)}, bf16[128,768]{1,0:T(8,128)(2,1)S(1)}, u32[]{:S(2)}, u32[]{:S(2)}) collective-permute-start(bf16[128,768]{1,0:T(8,128)(2,1)S(1)} %get-tuple-element.46), channel_id=1, source_target_pairs={{8,0},{16,8},{24,16},{32,24},{40,32},{48,40},{56,48},{64,56},{72,6... | collective-permute-start | bytes 589832 | tf_op jit(solution)/shard_map/ppermute | solution.py:467
  55.3 35.8 %collective-permute-start.6 = (bf16[128,768]{1,0:T(8,128)(2,1)S(1)}, bf16[128,768]{1,0:T(8,128)(2,1)S(1)}, u32[]{:S(2)}, u32[]{:S(2)}) collective-permute-start(bf16[128,768]{1,0:T(8,128)(2,1)S(1)} %get-tuple-element.47), channel_id=1, source_target_pairs={{16,0},{24,8},{32,16},{40,24},{48,32},{56,40},{64,48},{72,56},{80,... | collective-permute-start | bytes 589832 | tf_op jit(solution)/shard_map/ppermute | solution.py:467
  56.6 34.5 %collective-permute-start.7 = (bf16[128,768]{1,0:T(8,128)(2,1)S(1)}, bf16[128,768]{1,0:T(8,128)(2,1)S(1)}, u32[]{:S(2)}, u32[]{:S(2)}) collective-permute-start(bf16[128,768]{1,0:T(8,128)(2,1)S(1)} %get-tuple-element.48), channel_id=1, source_target_pairs={{24,0},{32,8},{40,16},{48,24},{56,32},{64,40},{72,48},{80,56},{88,... | collective-permute-start | bytes 589832 | tf_op jit(solution)/shard_map/ppermute | solution.py:467
  57.9 33.2 %collective-permute-start.8 = (bf16[128,512]{1,0:T(8,128)(2,1)S(1)}, bf16[128,512]{1,0:T(8,128)(2,1)S(1)}, u32[]{:S(2)}, u32[]{:S(2)}) collective-permute-start(bf16[128,512]{1,0:T(8,128)(2,1)S(1)} %get-tuple-element.49), channel_id=1, source_target_pairs={{32,0},{40,8},{48,16},{56,24},{64,32},{72,40},{80,48},{88,56},{96,... | collective-permute-start | bytes 393224 | tf_op jit(solution)/shard_map/ppermute | solution.py:467
  59.9 31.2 %all-to-all-start.1 = ((f32[64,1,256]{2,1,0:T(1,128)}), f32[64,1,256]{2,1,0:T(1,128)S(1)}, u32[]{:S(2)}, u32[]{:S(2)}) async-start(f32[64,1,256]{2,1,0:T(1,128)} %copy.16), calls=%async_computation.1 | async-start | bytes 131072 | tf_op jit(solution)/shard_map/all_to_all | solution.py:481

commit v3 on v2

--- a/solution.py
+++ b/solution.py
@@ -99,14 +99,23 @@
     ]
 
 
-def pack_kernel(key_ref, dir_ref, value_ref, rate_ref, out_ref, rate_in, rate_out, sems):
+def rate_pieces(row, height, width):
+    first = row.astype(BF16).astype(F32)
+    rest = row - first
+    second = rest.astype(BF16).astype(F32)
+    third = rest - second
+    at = lax.broadcasted_iota(jnp.int32, (height, width), 0)
+    return jnp.where(at == 0, first, jnp.where(at == 1, second, jnp.where(at == 2, third, 0.0))).astype(BF16)
+
+
+def pack_kernel(key_ref, dir_ref, value_ref, rate_ref, out_ref, rate_in, sems):
     size, width = key_ref.shape
     heads = rate_ref.shape[0]
-    bring = pltpu.make_async_copy(rate_ref, rate_in, sems.at[0])
+    bring = pltpu.make_async_copy(rate_ref, rate_in, sems.at[3])
     bring.start()
     copies = [
         pltpu.make_async_copy(
-            ref, out_ref.at[pl.ds(0, size), pl.ds(at * width, width)], sems.at[at + 1]
+            ref, out_ref.at[pl.ds(0, size), pl.ds(at * width, width)], sems.at[at]
         )
         for at, ref in enumerate((key_ref, dir_ref, value_ref))
     ]
@@ -114,34 +123,20 @@
         copy.start()
     bring.wait()
     rate = jnp.concatenate([rate_in[h : h + 1, :] for h in range(heads)], axis=1)
-    first = rate.astype(BF16).astype(F32)
-    rest = rate - first
-    second = rest.astype(BF16).astype(F32)
-    third = rest - second
-    row = lax.broadcasted_iota(jnp.int32, (16, width), 0)
-    pieces = jnp.where(row == 0, first, jnp.where(row == 1, second, jnp.where(row == 2, third, 0.0)))
-    rate_out[:, 0:width] = pieces.astype(BF16)
-    rate_out[:, width : 3 * width] = jnp.zeros((16, 2 * width), BF16)
-    last = pltpu.make_async_copy(rate_out, out_ref.at[pl.ds(size, 16)], sems.at[4])
-    last.start()
+    out_ref[size : size + 16, 0:width] = rate_pieces(rate, 16, width)
+    out_ref[size : size + 16, width : 3 * width] = jnp.zeros((16, 2 * width), BF16)
     for copy in copies:
         copy.wait()
-    last.wait()
 
 
 def pack(keys, dirs, values, rates):
     size, width = keys.shape
-    anywhere = pl.BlockSpec(memory_space=pl.ANY)
     return pl.pallas_call(
         pack_kernel,
         out_shape=jax.ShapeDtypeStruct((size + 16, 3 * width), BF16),
-        in_specs=[anywhere] * 4,
-        out_specs=anywhere,
-        scratch_shapes=[
-            pltpu.VMEM(rates.shape, F32),
-            pltpu.VMEM((16, 3 * width), BF16),
-            pltpu.SemaphoreType.DMA((5,)),
-        ],
+        in_specs=[pl.BlockSpec(memory_space=pl.ANY)] * 4,
+        out_specs=pl.BlockSpec(memory_space=pltpu.VMEM),
+        scratch_shapes=[pltpu.VMEM(rates.shape, F32), pltpu.SemaphoreType.DMA((4,))],
     )(keys, dirs, values, rates)
 
 
@@ -298,14 +293,14 @@
     part_ref,
     own_ref,
     dval_ref,
-    send1_ref,
+    cross_ref,
     send2_ref,
-    send3_ref,
     send4_ref,
 ):
     size = value_ref.shape[0]
     width = heads * DH
-    sends = (send1_ref, send2_ref, send3_ref, send4_ref)
+    block = 3 * width
+    places = ((cross_ref, 0), (send2_ref, 0), (cross_ref, block), (send4_ref, 0))
     rows, cols = grids(size)
     eye = rows == cols
     sums = jnp.sum(sums_ref[...], axis=0, keepdims=True)
@@ -318,7 +313,11 @@
     gain = gain_ref[...]
     normed = att_all * inverse
     normed_ref[...] = (normed * gain).astype(BF16)
-    part_ref[...] = jnp.broadcast_to(jnp.sum(cot_all * normed, axis=0, keepdims=True), part_ref.shape)
+    part = jnp.sum(cot_all * normed, axis=0, keepdims=True)
+    part_ref[...] = part
+    cross_ref[size : size + 16, 0:width] = rate_pieces(part, 16, width)
+    cross_ref[size : size + 16, width : 2 * block] = jnp.zeros((16, 2 * block - width), BF16)
+    send4_ref[:, 2 * width : block] = jnp.zeros((size, width), BF16)
     grad_att = cot_all * gain * inverse - att_all * pull
     scale = DH ** (-0.5)
     for h in range(heads):
@@ -341,17 +340,42 @@
                 dval_ref[:, lanes] = dvalue
                 own_ref[h] = jnp.concatenate([dscore, carried], axis=1)
                 continue
-            send = sends[s - 1]
-            send[:, lanes] = dvalue.astype(BF16)
+            send, base = places[s - 1]
+            at_value = slice(base + h * DH, base + (h + 1) * DH)
+            at_end = slice(base + width + h * DH, base + width + (h + 1) * DH)
+            at_trans = slice(base + 2 * width + h * DH, base + 2 * width + (h + 1) * DH)
+            send[0:size, at_value] = dvalue.astype(BF16)
             if carried is None:
-                send[:, width + h * DH : width + (h + 1) * DH] = mm(frame_ref[h, s - 1], dscore, "tn").astype(BF16)
+                send[0:size, at_end] = mm(frame_ref[h, s - 1], dscore, "tn").astype(BF16)
                 carried = mm(dscore, kt_ref[h, s - 1, :, 0:DH], "nt").astype(BF16)
             else:
                 both = jnp.concatenate([dscore, carried], axis=1)
                 grads = mm(frame_ref[h, s - 1], both, "tn").astype(BF16)
-                send[:, width + h * DH : width + (h + 1) * DH] = grads[:, 0:DH]
-                send[:, 2 * width + h * DH : 2 * width + (h + 1) * DH] = grads[:, DH : 2 * DH]
+                send[0:size, at_end] = grads[:, 0:DH]
+                send[0:size, at_trans] = grads[:, DH : 2 * DH]
                 carried = mm(both, kt_ref[h, s - 1], "nt").astype(BF16)
+
+
+def merge_kernel(part_ref, mine2_ref, mine4_ref, cross_ref, place_ref, parts_ref, near_ref, send2_ref, send4_ref):
+    size, block = mine2_ref.shape
+    width = part_ref.shape[1]
+    other = jnp.sum(cross_ref[size : size + 16, 0:width].astype(F32), axis=0, keepdims=True)
+    parts_ref[...] = jnp.broadcast_to(part_ref[...] + other, parts_ref.shape)
+
+    @pl.when(place_ref[1] == 0)
+    def _():
+        near_ref[...] = cross_ref[0:size, 0:block]
+        total = mine2_ref[...].astype(F32) + cross_ref[0:size, block : 2 * block].astype(F32)
+        send2_ref[...] = total.astype(BF16)
+        send4_ref[...] = mine4_ref[...]
+
+    @pl.when(place_ref[1] != 0)
+    def _():
+        near_ref[...] = jnp.zeros((size, block), BF16)
+        total = mine2_ref[...].astype(F32) + cross_ref[0:size, 0:block].astype(F32)
+        send2_ref[...] = total.astype(BF16)
+        total = mine4_ref[...].astype(F32) + cross_ref[0:size, block : 2 * block].astype(F32)
+        send4_ref[...] = total.astype(BF16)
 
 
 def local_kernel(heads, own_ref, kw_ref, query_ref, key_ref, dir_ref, dquery_ref, dkey_ref, ddir_ref, pulled_ref):
@@ -378,9 +402,8 @@
 
 def shard_kernel(
     heads,
-    recv1_ref,
+    near_ref,
     recv2_ref,
-    recv3_ref,
     recv4_ref,
     inv_ref,
     kw_ref,
@@ -400,13 +423,13 @@
 ):
     size = key_ref.shape[0]
     width = heads * DH
-    recvs = (recv1_ref, recv2_ref, recv3_ref, recv4_ref)
+    recvs = (near_ref, recv2_ref, recv4_ref)
     rows, cols = grids(size)
     eye = rows == cols
     strict = rows > cols
     dvalue = dval_in_ref[...]
-    for s in range(WIN):
-        dvalue = dvalue + recvs[s][:, 0:width].astype(F32)
+    for recv in recvs:
+        dvalue = dvalue + recv[:, 0:width].astype(F32)
     dvalue_ref[...] = dvalue.astype(BF16)
     dgain_ref[...] = jnp.sum(parts_ref[...], axis=0, keepdims=True)
     for h in range(heads):
@@ -417,12 +440,11 @@
         unit = raw_dirs * norm_col
         unit_half = unit.astype(BF16)
         rate_col = to_col(rate_ref[h : h + 1, :], eye)
-        dend = recvs[0][:, width + h * DH : width + (h + 1) * DH].astype(F32)
-        dtrans = recvs[0][:, 2 * width + h * DH : 2 * width + (h + 1) * DH].astype(F32)
-        for s in range(1, WIN):
-            dend = dend + recvs[s][:, width + h * DH : width + (h + 1) * DH].astype(F32)
-            if s < WIN - 1:
-                dtrans = dtrans + recvs[s][:, 2 * width + h * DH : 2 * width + (h + 1) * DH].astype(F32)
+        dend = jnp.zeros((size, DH), F32)
+        dtrans = jnp.zeros((size, DH), F32)
+        for recv in recvs:
+            dend = dend + recv[:, width + h * DH : width + (h + 1) * DH].astype(F32)
+            dtrans = dtrans + recv[:, 2 * width + h * DH : 2 * width + (h + 1) * DH].astype(F32)
         both = jnp.concatenate([dend, dtrans], axis=1).astype(BF16)
         coef = kw_ref[h]
         dcoef = -(pulled_ref[h] + mm(unit_half, both))
@@ -477,8 +499,8 @@
     return lax.ppermute(value, "ctx", [(source, source ^ 1) for source in range(count)])
 
 
-def gathered(value, axis):
-    return lax.all_to_all(value, axis, 0, 0, tiled=True)
+def gathered(value, axis, groups=None):
+    return lax.all_to_all(value, axis, 0, 0, axis_index_groups=groups, tiled=True)
 
 
 def per_device(query, keys, values, dirs, rates, gain, doc_lengths, cotangent):
@@ -492,7 +514,6 @@
     packed = pack(keys, dirs, values, rates)
     halo2 = passed_along(packed, 2)
     halo4 = passed_along(packed, 4)
-    halos = (halo2, halo4, paired(packed, 0, 1), swapped(halo2), paired(halo4, 1, -1))
     inverse, coef, raw = call(
         own_kernel,
         [((heads, size, size), BF16), ((heads, size, 2 * DH), BF16), ((heads, size, 2 * DH), F32)],
@@ -502,6 +523,8 @@
         dirs,
         rates,
     )
+    halo2, raw = lax.optimization_barrier((halo2, raw))
+    halos = (halo2, halo4, paired(packed, 0, 1), swapped(halo2), paired(halo4, 1, -1))
     att, total, prob, frame, carry, sums, far = call(
         functools.partial(attend_kernel, heads),
         [
@@ -523,17 +546,16 @@
         scratch=[pltpu.VMEM((size + 16, 3 * width), BF16)] * 2,
     )
     sums = gathered(sums, "head")
-    normed, part, own, dval, *sends = call(
+    normed, part, own, dval, cross, mine2, mine4 = call(
         functools.partial(back_kernel, heads, features),
         [
             ((size, width), BF16),
-            ((lax.axis_size("ctx"), width), F32),
+            ((1, width), F32),
             ((heads, size, 2 * DH), BF16),
             ((size, width), F32),
+            ((size + 16, 6 * width), BF16),
             ((size, 3 * width), BF16),
             ((size, 3 * width), BF16),
-            ((size, 3 * width), BF16),
-            ((size, 2 * width), BF16),
         ],
         heads * 30 * unit_flops,
         sums,
@@ -547,7 +569,18 @@
         gain_row,
         far,
     )
-    recvs = [passed_along(sends[s - 1], -s) for s in range(1, WIN + 1)]
+    count = lax.axis_size("ctx")
+    parts, near, send2, send4 = call(
+        merge_kernel,
+        [((count // 2, width), F32)] + [((size, 3 * width), BF16)] * 3,
+        0,
+        part,
+        mine2,
+        mine4,
+        swapped(cross),
+        scalars=(place,),
+    )
+    recvs = (near, passed_along(send2, -2), passed_along(send4, -4))
     dquery, dkey_part, ddir_part, pulled = call(
         functools.partial(local_kernel, heads),
         [
@@ -563,7 +596,7 @@
         keys,
         dirs,
     )
-    parts = gathered(part, "ctx")
+    parts = gathered(parts, "ctx", [list(range(core, count, 2)) for core in range(2)])
     dkey, dvalue, ddir, drate, dgain = call(
         functools.partial(shard_kernel, heads),
         [((size, width), BF16), ((size, width), BF16), ((size, width), BF16), ((heads, size), F32), ((1, width), F32)],

time: 93.7 us -> 83.6 us (0.89)
  the two profiles are of different devices: /device:TPU:1 before, /device:TPU:6 now
where the time goes in v3:
time: 83.6 us; the launch traced here: 82.5 us
  starting transfers between devices  37.7 us (45%)
  Pallas kernels  17.1 us (20%)
  blocking collectives  14.6 us (17%)
  waiting for transfers between devices  11.5 us (14%)
  between operations  0.86 us (1%)
    all_to_all x1, starting transfers between devices, gathered(): lax.all_to_all(value, axis, 0, 0, axis_index_groups=groups, tiled=True)  17.3 us
    pallas_call x6, Pallas kernels, call(): pl.pallas_call(body, out_shape=[jax.ShapeDtypeStruct(s, d) for s, d in ou...  15.4 us
    all_to_all x1, blocking collectives, gathered(): lax.all_to_all(value, axis, 0, 0, axis_index_groups=groups, tiled=True)  14.6 us
    ppermute x4, starting transfers between devices, passed_along(): lax.ppermute(value, 'ctx', [(source, source + steps) for source in range(...  12.8 us
    all_to_all x1, waiting for transfers between devices, gathered(): lax.all_to_all(value, axis, 0, 0, axis_index_groups=groups, tiled=True)  6.92 us
    ppermute x2, starting transfers between devices, swapped(): lax.ppermute(value, 'ctx', [(source, source ^ 1) for source in range(coun...  4.95 us
    ppermute x2, waiting for transfers between devices, swapped(): lax.ppermute(value, 'ctx', [(source, source ^ 1) for source in range(coun...  2.74 us
    ppermute x2, starting transfers between devices, paired(): lax.ppermute(value, 'ctx', [(source, source + step) for source in range(f...  2.58 us
  transfers between devices with their start and end apart: 9, of which 4 were waited for; matrix products, arithmetic and copies ran while one was open for 1% of the time, Pallas kernels for 5%

profile of v3, /device:TPU:6, one launch (start us, length us, event | category | flops | bytes accessed | tf_op | source)
XLA Modules:
  0.0 82.5 jit_solution(18217117976433538277)
XLA Ops:
  0.7 1.7 %shard_map.135 = bf16[144,768]{1,0:T(8,128)(2,1)} custom-call(bf16[128,256]{1,0:T(8,128)(2,1)} %key_ref.7, bf16[128,256]{1,0:T(8,128)(2,1)} %dir_ref.7, bf16[128,256]{1,0:T(8,128)(2,1)} %value_ref.5, f32[2,128]{1,0:T(2,128)} %rate_ref.5), custom_call_target="tpu_custom_call" | custom-call | tf_op jit(solution)/shard_map/pallas_call | solution.py:134
  2.4 0.0 copy-start.2
  2.4 4.3 %collective-permute-start = (bf16[144,768]{1,0:T(8,128)(2,1)}, bf16[144,768]{1,0:T(8,128)(2,1)S(1)}, u32[]{:S(2)}, u32[]{:S(2)}) collective-permute-start(bf16[144,768]{1,0:T(8,128)(2,1)} %shard_map.135), channel_id=1, source_target_pairs={{0,16},{8,24},{16,32},{24,40},{32,48},{40,56},{48,64},{56,72},{64,... | collective-permute-start | bytes 663560 | tf_op jit(solution)/shard_map/ppermute | solution.py:489
  6.7 4.3 %collective-permute-start.1 = (bf16[144,768]{1,0:T(8,128)(2,1)}, bf16[144,768]{1,0:T(8,128)(2,1)S(1)}, u32[]{:S(2)}, u32[]{:S(2)}) collective-permute-start(bf16[144,768]{1,0:T(8,128)(2,1)} %shard_map.135), channel_id=1, source_target_pairs={{0,32},{8,40},{16,48},{24,56},{32,64},{40,72},{48,80},{56,88},{64,... | collective-permute-start | bytes 663560 | tf_op jit(solution)/shard_map/ppermute | solution.py:489
  11.1 1.3 %collective-permute-start.2 = (bf16[144,768]{1,0:T(8,128)(2,1)}, bf16[144,768]{1,0:T(8,128)(2,1)S(1)}, u32[]{:S(2)}, u32[]{:S(2)}) collective-permute-start(bf16[144,768]{1,0:T(8,128)(2,1)} %shard_map.135), channel_id=1, source_target_pairs={{0,8},{16,24},{32,40},{48,56},{64,72},{80,88},{96,104},{112,120},{... | collective-permute-start | bytes 663560 | tf_op jit(solution)/shard_map/ppermute | solution.py:494
  12.4 2.9 %shard_map.136 = (bf16[2,128,128]{2,1,0:T(8,128)(2,1)S(1)}, bf16[2,128,256]{2,1,0:T(8,128)(2,1)S(1)}, f32[2,128,256]{2,1,0:T(8,128)S(1)}) custom-call(bf16[128,256]{1,0:T(8,128)(2,1)S(1)} %copy-done.4, bf16[128,256]{1,0:T(8,128)(2,1)S(1)} %copy-done, bf16[128,256]{1,0:T(8,128)(2,1)S(1)} %copy-done.1, f32[2,128]{1,0:T(2,128)S(1)} %copy-done.5), custom_call_target="tpu_custom_call" | custom-call | flops 503316480 | bytes 656384 | tf_op jit(solution)/shard_map/pallas_call | solution.py:475
  15.4 1.8 %collective-permute-done.1.halo4_ref = bf16[144,768]{1,0:T(8,128)(2,1)S(1)} collective-permute-done((bf16[144,768]{1,0:T(8,128)(2,1)}, bf16[144,768]{1,0:T(8,128)(2,1)S(1)}, u32[]{:S(2)}, u32[]{:S(2)}) %collective-permute-start.1) | collective-permute-done | bytes 221216 | tf_op jit(solution)/shard_map/ppermute | solution.py:489
  17.2 1.3 %collective-permute-start.4 = (bf16[144,768]{1,0:T(8,128)(2,1)S(1)}, bf16[144,768]{1,0:T(8,128)(2,1)S(1)}, u32[]{:S(2)}, u32[]{:S(2)}) collective-permute-start(bf16[144,768]{1,0:T(8,128)(2,1)S(1)} %collective-permute-done.1.halo4_ref), channel_id=1, source_target_pairs={{8,0},{24,16},{40,32},{56,48},{72,64},{88,80},{104,96},{120,112},{... | collective-permute-start | bytes 663560 | tf_op jit(solution)/shard_map/ppermute | solution.py:494
  18.5 3.0 %collective-permute-start.3 = (bf16[144,768]{1,0:T(8,128)(2,1)S(1)}, bf16[144,768]{1,0:T(8,128)(2,1)S(1)}, u32[]{:S(2)}, u32[]{:S(2)}) collective-permute-start(bf16[144,768]{1,0:T(8,128)(2,1)S(1)} %collective-permute-done.halo2_ref), channel_id=1, source_target_pairs={{0,8},{8,0},{16,24},{24,16},{32,40},{40,32},{48,56},{56,48},{64,72... | collective-permute-start | bytes 663560 | tf_op jit(solution)/shard_map/ppermute | solution.py:499
  21.6 0.1 pad_add_fusion.place_ref
  21.7 1.0 %collective-permute-done.3.cross2_ref = bf16[144,768]{1,0:T(8,128)(2,1)S(1)} collective-permute-done((bf16[144,768]{1,0:T(8,128)(2,1)S(1)}, bf16[144,768]{1,0:T(8,128)(2,1)S(1)}, u32[]{:S(2)}, u32[]{:S(2)}) %collective-permute-start.3) | collective-permute-done | bytes 221216 | tf_op jit(solution)/shard_map/ppermute | solution.py:499
  22.7 6.3 %shard_map.137 = (f32[128,256]{1,0:T(8,128)S(1)}, f32[2,128,8]{2,1,0:T(8,128)S(1)}, bf16[2,5,128,128]{3,2,1,0:T(8,128)(2,1)S(1)}, bf16[2,4,128,128]{3,2,1,0:T(8,...) custom-call(f32[2,128,256]{2,1,0:T(8,128)S(1)} %get-tuple-element.40.raw, ...), custom_call_target="tpu_custom_call" | custom-call | flops 2516582400 | bytes 3023872 | tf_op jit(solution)/shard_map/pallas_call | solution.py:475
  29.0 14.6 %all_to_all.22 = f32[8,1,256]{2,1,0:T(1,128)S(1)} all-to-all(f32[8,1,256]{2,1,0:T(1,128)S(1)} %copy.15), channel_id=1, replica_groups=mesh['ctx'=64,'head'=8] {'head'}, dimensions={0} | all-to-all | bytes 16384 | tf_op jit(solution)/shard_map/all_to_all | solution.py:503
  43.6 2.2 %shard_map.138 = (bf16[128,256]{1,0:T(8,128)(2,1)}, f32[1,256]{1,0:T(1,128)S(1)}, bf16[2,128,256]{2,1,0:T(8,128)(2,1)S(1)}, f32[128,256]{1,0:T(8,128)S(1)}, bf16...) custom-call(f32[8,256]{1,0:T(8,128)S(1)} %bitcast.13, ...), custom_call_target="tpu_custom_call" | custom-call | flops 251658240 | bytes 2820096 | tf_op jit(solution)/shard_map/pallas_call | solution.py:475
  45.9 1.9 %collective-permute-start.5 = (bf16[144,1536]{1,0:T(8,128)(2,1)S(1)}, bf16[144,1536]{1,0:T(8,128)(2,1)S(1)}, u32[]{:S(2)}, u32[]{:S(2)}) collective-permute-start(bf16[144,1536]{1,0:T(8,128)(2,1)S(1)} %get-tuple-element.56), channel_id=1, source_target_pairs={{0,8},{8,0},{16,24},{24,16},{32,40},{40,32},{48,56},{56,48},{64,72... | collective-permute-start | bytes 1327112 | tf_op jit(solution)/shard_map/ppermute | solution.py:499
  47.8 1.8 %collective-permute-done.5.cross_ref = bf16[144,1536]{1,0:T(8,128)(2,1)S(1)} collective-permute-done((bf16[144,1536]{1,0:T(8,128)(2,1)S(1)}, bf16[144,1536]{1,0:T(8,128)(2,1)S(1)}, u32[]{:S(2)}, u32[]{:S(2)}) %collective-permute-start.5) | collective-permute-done | bytes 442400 | tf_op jit(solution)/shard_map/ppermute | solution.py:499
  49.6 0.6 shard_map.140
  50.2 2.0 %collective-permute-start.6 = (bf16[128,768]{1,0:T(8,128)(2,1)S(1)}, bf16[128,768]{1,0:T(8,128)(2,1)S(1)}, u32[]{:S(2)}, u32[]{:S(2)}) collective-permute-start(bf16[128,768]{1,0:T(8,128)(2,1)S(1)} %get-tuple-element.58), channel_id=1, source_target_pairs={{16,0},{24,8},{32,16},{40,24},{48,32},{56,40},{64,48},{72,56},{80,... | collective-permute-start | bytes 589832 | tf_op jit(solution)/shard_map/ppermute | solution.py:489
  52.2 2.1 %collective-permute-start.7 = (bf16[128,768]{1,0:T(8,128)(2,1)S(1)}, bf16[128,768]{1,0:T(8,128)(2,1)S(1)}, u32[]{:S(2)}, u32[]{:S(2)}) collective-permute-start(bf16[128,768]{1,0:T(8,128)(2,1)S(1)} %get-tuple-element.59), channel_id=1, source_target_pairs={{32,0},{40,8},{48,16},{56,24},{64,32},{72,40},{80,48},{88,56},{96,... | collective-permute-start | bytes 589832 | tf_op jit(solution)/shard_map/ppermute | solution.py:489
  54.4 0.6 copy.16
  55.0 17.3 %all-to-all-start.1 = ((f32[32,1,256]{2,1,0:T(1,128)}), f32[32,1,256]{2,1,0:T(1,128)S(1)}, u32[]{:S(2)}, u32[]{:S(2)}) async-start(f32[32,1,256]{2,1,0:T(1,128)} %copy.16), calls=%async_computation.1 | async-start | bytes 65536 | tf_op jit(solution)/shard_map/all_to_all | solution.py:503
  72.4 1.2 %shard_map.139 = (bf16[128,256]{1,0:T(8,128)(2,1)}, f32[2,128,128]{2,1,0:T(8,128)S(1)}, f32[2,128,128]{2,1,0:T(8,128)S(1)}, f32[2,128,256]{2,1,0:T(8,128)S(1)}) custom-call(bf16[2,128,256]{2,1,0:T(8,128)(2,1)S(1)} %get-tuple-element.50.own_ref, bf16[2,128,256]{2,1,0:T(8,128)(2,1)S(1)} %get-tuple-element.51.kw_ref, bf16[128,256]{1,0:T(8,128)(2,1)S(1)} %copy-done.4, ...), custom_call_target="tpu_custom_call" | custom-call | flops 83886080 | bytes 1048576 | tf_op jit(solution)/shard_map/pallas_call | solution.py:475
  73.6 6.9 %all-to-all-done.1 = f32[32,1,256]{2,1,0:T(1,128)S(1)} async-done(((f32[32,1,256]{2,1,0:T(1,128)}), f32[32,1,256]{2,1,0:T(1,128)S(1)}, u32[]{:S(2)}, u32[]{:S(2)}) %all-to-all-start.1) | async-done | bytes 32800 | tf_op jit(solution)/shard_map/all_to_all | solution.py:503
  80.5 2.0 %shard_map.141 = (bf16[128,256]{1,0:T(8,128)(2,1)}, bf16[128,256]{1,0:T(8,128)(2,1)}, bf16[128,256]{1,0:T(8,128)(2,1)}, f32[2,128]{1,0:T(2,128)}, f32[1,256]{1,0:T(1,128)}) custom-call(bf16[128,768]{1,0:T(8,128)(2,1)S(1)} %get-tuple-element.57.near_ref, bf16[128,768]{1,0:T(8,128)(2,1)S(1)} %collective-permute-done.6.recv2_ref, ...), custom_call_target="tpu_custom_call" | custom-call | flops 167772160 | bytes 1805312 | tf_op jit(solution)/shard_map/pallas_call | solution.py:475
  (23 shorter events, 0.1 us)
Async XLA Ops:
  0.6 11.8 %copy-start.1 = (bf16[128,256]{1,0:T(8,128)(2,1)S(1)}, bf16[128,256]{1,0:T(8,128)(2,1)}, u32[]{:S(2)}) copy-start(bf16[128,256]{1,0:T(8,128)(2,1)} %dir_ref.7) | copy-start | bytes 196612
  0.6 11.8 %copy-start = (bf16[128,256]{1,0:T(8,128)(2,1)S(1)}, bf16[128,256]{1,0:T(8,128)(2,1)}, u32[]{:S(2)}) copy-start(bf16[128,256]{1,0:T(8,128)(2,1)} %key_ref.7) | copy-start | bytes 196612
  0.7 11.8 %copy-start.5 = (f32[2,128]{1,0:T(2,128)S(1)}, f32[2,128]{1,0:T(2,128)}, u32[]{:S(2)}) copy-start(f32[2,128]{1,0:T(2,128)} %rate_ref.5) | copy-start | bytes 3076
  0.7 11.8 %copy-start.4 = (bf16[128,256]{1,0:T(8,128)(2,1)S(1)}, bf16[128,256]{1,0:T(8,128)(2,1)}, u32[]{:S(2)}) copy-start(bf16[128,256]{1,0:T(8,128)(2,1)} %query_ref.3) | copy-start | bytes 196612
  2.4 20.3 %copy-start.2 = (bf16[128,256]{1,0:T(8,128)(2,1)S(1)}, bf16[128,256]{1,0:T(8,128)(2,1)}, u32[]{:S(2)}) copy-start(bf16[128,256]{1,0:T(8,128)(2,1)} %value_ref.5) | copy-start | bytes 196612
  2.4 20.3 %copy-start.3 = (bf16[128,256]{1,0:T(8,128)(2,1)S(1)}, bf16[128,256]{1,0:T(8,128)(2,1)}, u32[]{:S(2)}) copy-start(bf16[128,256]{1,0:T(8,128)(2,1)} %cot_ref.3) | copy-start | bytes 196612
  2.4 13.0 %collective-permute-start = (bf16[144,768]{1,0:T(8,128)(2,1)}, bf16[144,768]{1,0:T(8,128)(2,1)S(1)}, u32[]{:S(2)}, u32[]{:S(2)}) collective-permute-start(bf16[144,768]{1,0:T(8,128)(2,1)} %shard_map.135), channel_id=1, source_target_pairs={{0,16},{8,24},{16,32},{24,40},{32,48},{40,56},{48,64},{56,72},{64,... | collective-permute-start | bytes 663560 | tf_op jit(solution)/shard_map/ppermute | solution.py:489
  6.7 10.5 %collective-permute-start.1 = (bf16[144,768]{1,0:T(8,128)(2,1)}, bf16[144,768]{1,0:T(8,128)(2,1)S(1)}, u32[]{:S(2)}, u32[]{:S(2)}) collective-permute-start(bf16[144,768]{1,0:T(8,128)(2,1)} %shard_map.135), channel_id=1, source_target_pairs={{0,32},{8,40},{16,48},{24,56},{32,64},{40,72},{48,80},{56,88},{64,... | collective-permute-start | bytes 663560 | tf_op jit(solution)/shard_map/ppermute | solution.py:489
  11.1 10.6 %collective-permute-start.2 = (bf16[144,768]{1,0:T(8,128)(2,1)}, bf16[144,768]{1,0:T(8,128)(2,1)S(1)}, u32[]{:S(2)}, u32[]{:S(2)}) collective-permute-start(bf16[144,768]{1,0:T(8,128)(2,1)} %shard_map.135), channel_id=1, source_target_pairs={{0,8},{16,24},{32,40},{48,56},{64,72},{80,88},{96,104},{112,120},{... | collective-permute-start | bytes 663560 | tf_op jit(solution)/shard_map/ppermute | solution.py:494
  17.2 4.4 %collective-permute-start.4 = (bf16[144,768]{1,0:T(8,128)(2,1)S(1)}, bf16[144,768]{1,0:T(8,128)(2,1)S(1)}, u32[]{:S(2)}, u32[]{:S(2)}) collective-permute-start(bf16[144,768]{1,0:T(8,128)(2,1)S(1)} %collective-permute-done.1.halo4_ref), channel_id=1, source_target_pairs={{8,0},{24,16},{40,32},{56,48},{72,64},{88,80},{104,96},{120,112},{... | collective-permute-start | bytes 663560 | tf_op jit(solution)/shard_map/ppermute | solution.py:494
  18.5 4.1 %collective-permute-start.3 = (bf16[144,768]{1,0:T(8,128)(2,1)S(1)}, bf16[144,768]{1,0:T(8,128)(2,1)S(1)}, u32[]{:S(2)}, u32[]{:S(2)}) collective-permute-start(bf16[144,768]{1,0:T(8,128)(2,1)S(1)} %collective-permute-done.halo2_ref), channel_id=1, source_target_pairs={{0,8},{8,0},{16,24},{24,16},{32,40},{40,32},{48,56},{56,48},{64,72... | collective-permute-start | bytes 663560 | tf_op jit(solution)/shard_map/ppermute | solution.py:499
  21.7 1.0 %copy-start.6 = (f32[256]{0:T(256)S(1)}, f32[256]{0:T(256)}, u32[]{:S(2)}) copy-start(f32[256]{0:T(256)} %param.13) | copy-start | bytes 3076
  21.7 1.0 %copy-start.7 = (s32[32]{0:T(128)S(1)}, s32[32]{0:T(128)}, u32[]{:S(2)}) copy-start(s32[32]{0:T(128)} %len_ref.1) | copy-start | bytes 388
  45.9 3.7 %collective-permute-start.5 = (bf16[144,1536]{1,0:T(8,128)(2,1)S(1)}, bf16[144,1536]{1,0:T(8,128)(2,1)S(1)}, u32[]{:S(2)}, u32[]{:S(2)}) collective-permute-start(bf16[144,1536]{1,0:T(8,128)(2,1)S(1)} %get-tuple-element.56), channel_id=1, source_target_pairs={{0,8},{8,0},{16,24},{24,16},{32,40},{40,32},{48,56},{56,48},{64,72... | collective-permute-start | bytes 1327112 | tf_op jit(solution)/shard_map/ppermute | solution.py:499
  50.2 30.3 %collective-permute-start.6 = (bf16[128,768]{1,0:T(8,128)(2,1)S(1)}, bf16[128,768]{1,0:T(8,128)(2,1)S(1)}, u32[]{:S(2)}, u32[]{:S(2)}) collective-permute-start(bf16[128,768]{1,0:T(8,128)(2,1)S(1)} %get-tuple-element.58), channel_id=1, source_target_pairs={{16,0},{24,8},{32,16},{40,24},{48,32},{56,40},{64,48},{72,56},{80,... | collective-permute-start | bytes 589832 | tf_op jit(solution)/shard_map/ppermute | solution.py:489
  52.2 28.3 %collective-permute-start.7 = (bf16[128,768]{1,0:T(8,128)(2,1)S(1)}, bf16[128,768]{1,0:T(8,128)(2,1)S(1)}, u32[]{:S(2)}, u32[]{:S(2)}) collective-permute-start(bf16[128,768]{1,0:T(8,128)(2,1)S(1)} %get-tuple-element.59), channel_id=1, source_target_pairs={{32,0},{40,8},{48,16},{56,24},{64,32},{72,40},{80,48},{88,56},{96,... | collective-permute-start | bytes 589832 | tf_op jit(solution)/shard_map/ppermute | solution.py:489
  55.0 25.5 %all-to-all-start.1 = ((f32[32,1,256]{2,1,0:T(1,128)}), f32[32,1,256]{2,1,0:T(1,128)S(1)}, u32[]{:S(2)}, u32[]{:S(2)}) async-start(f32[32,1,256]{2,1,0:T(1,128)} %copy.16), calls=%async_computation.1 | async-start | bytes 65536 | tf_op jit(solution)/shard_map/all_to_all | solution.py:503

commit v4 on v3

--- a/solution.py
+++ b/solution.py
@@ -33,7 +33,7 @@
 def mm3(left, right):
     lh, ll = split(left)
     rh, rl = split(right)
-    return mm(lh, rh) + (mm(lh, rl) + mm(ll, rh))
+    return mm(jnp.concatenate([lh, lh, ll], axis=1), jnp.concatenate([rh, rl, rh], axis=0))
 
 
 def grids(size):
@@ -53,18 +53,22 @@
 def unit_lower_inverses(strict_list):
     size = strict_list[0].shape[0]
     rows, cols = grids(size)
-    width = 1
-    inverses = None
+    eye = jnp.where(rows == cols, 1.0, 0.0)
+    pair = (rows // 2 == cols // 2) & (rows > cols)
+    inverses = [eye - jnp.where(pair, strict, 0.0) for strict in strict_list]
+    width = 2
     while width < size:
-        row_block = rows // width
-        coupling = (row_block - cols // width == 1) & (row_block % 2 == 1)
-        parts = [jnp.where(coupling, strict, 0.0) for strict in strict_list]
-        if inverses is None:
-            inverses = [jnp.where(rows == cols, 1.0, 0.0) - part for part in parts]
+        wide = min(4 * width, size)
+        between = (rows // wide == cols // wide) & (rows // width > cols // width)
+        parts = [jnp.where(between, strict, 0.0) for strict in strict_list]
+        steps = [mm3(inverse, part) for inverse, part in zip(inverses, parts)]
+        once = [inverse - mm3(step, inverse) for step, inverse in zip(steps, inverses)]
+        if wide > 2 * width:
+            twice = [mm3(step, step) for step in steps]
+            inverses = [first + mm3(second, first) for first, second in zip(once, twice)]
         else:
-            halves = [mm3(part, inverse) for part, inverse in zip(parts, inverses)]
-            inverses = [inverse - mm3(inverse, half) for inverse, half in zip(inverses, halves)]
-        width = 2 * width
+            inverses = once
+        width = wide
     return inverses
 
 
@@ -273,7 +277,7 @@
         square = square + jnp.sum(att * att, axis=1, keepdims=True)
         inner = inner + jnp.sum(weighted * att, axis=1, keepdims=True)
     row = jnp.concatenate([to_row(square, eye), to_row(inner, eye)], axis=1)
-    sums_ref[...] = jnp.broadcast_to(row, sums_ref.shape)
+    sums_ref[...] = jnp.broadcast_to(row[None], sums_ref.shape)
 
 
 def back_kernel(
@@ -303,7 +307,7 @@
     places = ((cross_ref, 0), (send2_ref, 0), (cross_ref, block), (send4_ref, 0))
     rows, cols = grids(size)
     eye = rows == cols
-    sums = jnp.sum(sums_ref[...], axis=0, keepdims=True)
+    sums = jnp.sum(sums_ref[...], axis=0)
     square = to_col(sums[:, 0:size], eye)
     inner = to_col(sums[:, size : 2 * size], eye)
     inverse = lax.rsqrt(square / features + EPSILON)
@@ -360,7 +364,7 @@
     size, block = mine2_ref.shape
     width = part_ref.shape[1]
     other = jnp.sum(cross_ref[size : size + 16, 0:width].astype(F32), axis=0, keepdims=True)
-    parts_ref[...] = jnp.broadcast_to(part_ref[...] + other, parts_ref.shape)
+    parts_ref[...] = jnp.broadcast_to((part_ref[...] + other)[None], parts_ref.shape)
 
     @pl.when(place_ref[1] == 0)
     def _():
@@ -431,7 +435,7 @@
     for recv in recvs:
         dvalue = dvalue + recv[:, 0:width].astype(F32)
     dvalue_ref[...] = dvalue.astype(BF16)
-    dgain_ref[...] = jnp.sum(parts_ref[...], axis=0, keepdims=True)
+    dgain_ref[...] = jnp.sum(parts_ref[...], axis=0)
     for h in range(heads):
         lanes = slice(h * DH, (h + 1) * DH)
         keys = key_ref[:, lanes]
@@ -509,7 +513,7 @@
     features = width * lax.axis_size("head")
     gain_row = gain.reshape(1, width)
     ctx = lax.axis_index("ctx").astype(jnp.int32)
-    place = jnp.stack([ctx * size, ctx % 2])
+    place = jnp.stack([ctx * size, ctx & 1])
     unit_flops = 2 * size * size * DH
     packed = pack(keys, dirs, values, rates)
     halo2 = passed_along(packed, 2)
@@ -524,7 +528,10 @@
         rates,
     )
     halo2, raw = lax.optimization_barrier((halo2, raw))
-    halos = (halo2, halo4, paired(packed, 0, 1), swapped(halo2), paired(halo4, 1, -1))
+    even = paired(packed, 0, 1)
+    cross2 = swapped(halo2)
+    cross2, halo4 = lax.optimization_barrier((cross2, halo4))
+    halos = (halo2, halo4, even, cross2, paired(halo4, 1, -1))
     att, total, prob, frame, carry, sums, far = call(
         functools.partial(attend_kernel, heads),
         [
@@ -533,7 +540,7 @@
             ((heads, WIN + 1, size, size), BF16),
             ((heads, WIN, size, DH), BF16),
             ((heads, WIN, DH, 2 * DH), BF16),
-            ((lax.axis_size("head"), 2 * size), F32),
+            ((lax.axis_size("head"), 1, 2 * size), F32),
             ((WIN, size, width), BF16),
         ],
         heads * 300 * unit_flops,
@@ -572,7 +579,7 @@
     count = lax.axis_size("ctx")
     parts, near, send2, send4 = call(
         merge_kernel,
-        [((count // 2, width), F32)] + [((size, 3 * width), BF16)] * 3,
+        [((count // 2, 1, width), F32)] + [((size, 3 * width), BF16)] * 3,
         0,
         part,
         mine2,
@@ -580,7 +587,6 @@
         swapped(cross),
         scalars=(place,),
     )
-    recvs = (near, passed_along(send2, -2), passed_along(send4, -4))
     dquery, dkey_part, ddir_part, pulled = call(
         functools.partial(local_kernel, heads),
         [
@@ -596,6 +602,7 @@
         keys,
         dirs,
     )
+    recvs = (near, passed_along(send2, -2), passed_along(send4, -4))
     parts = gathered(parts, "ctx", [list(range(core, count, 2)) for core in range(2)])
     dkey, dvalue, ddir, drate, dgain = call(
         functools.partial(shard_kernel, heads),

time: 83.6 us -> 83.8 us (level)
  starting transfers between devices: 37.7 us -> 39.9 us
    ppermute x2, waiting for transfers between devices: 0.01 us -> 1.99 us  [paired(): lax.ppermute(value, 'ctx', [(source, source + step) for source in range(f...]
    ppermute x4, waiting for transfers between devices: 1.86 us -> 0.01 us  [passed_along(): lax.ppermute(value, 'ctx', [(source, source + steps) for source in range(...]
    ppermute x2, starting transfers between devices: 2.58 us -> 3.71 us  [paired(): lax.ppermute(value, 'ctx', [(source, source + step) for source in range(f...]
    ppermute x2, starting transfers between devices: 4.95 us -> 3.83 us  [swapped(): lax.ppermute(value, 'ctx', [(source, source ^ 1) for source in range(coun...]
    all_to_all x1, starting transfers between devices: 17.3 us -> 18.4 us  [gathered(): lax.all_to_all(value, axis, 0, 0, axis_index_groups=groups, tiled=True)]
    ppermute x4, starting transfers between devices: 12.8 us -> 13.9 us  [passed_along(): lax.ppermute(value, 'ctx', [(source, source + steps) for source in range(...]
    ppermute x2, waiting for transfers between devices: 2.74 us -> 1.76 us  [swapped(): lax.ppermute(value, 'ctx', [(source, source ^ 1) for source in range(coun...]
  transfers between devices with their start and end apart: 9 -> 9, of which waited for: 4 -> 3; matrix products, arithmetic and copies ran while one was open for 1% -> 0% of each run, Pallas kernels for 5% -> 4%
where the time goes in v4:
time: 83.8 us; the launch traced here: 82.7 us
  starting transfers between devices  39.9 us (48%)
  Pallas kernels  16.6 us (20%)
  blocking collectives  14.6 us (17%)
  waiting for transfers between devices  10.7 us (13%)
  between operations  0.87 us (1%)
    all_to_all x1, starting transfers between devices, gathered(): lax.all_to_all(value, axis, 0, 0, axis_index_groups=groups, tiled=True)  18.4 us
    pallas_call x6, Pallas kernels, call(): pl.pallas_call(body, out_shape=[jax.ShapeDtypeStruct(s, d) for s, d in ou...  14.9 us
    all_to_all x1, blocking collectives, gathered(): lax.all_to_all(value, axis, 0, 0, axis_index_groups=groups, tiled=True)  14.6 us
    ppermute x4, starting transfers between devices, passed_along(): lax.ppermute(value, 'ctx', [(source, source + steps) for source in range(...  13.9 us
    all_to_all x1, waiting for transfers between devices, gathered(): lax.all_to_all(value, axis, 0, 0, axis_index_groups=groups, tiled=True)  6.92 us
    ppermute x2, starting transfers between devices, swapped(): lax.ppermute(value, 'ctx', [(source, source ^ 1) for source in range(coun...  3.83 us
    ppermute x2, starting transfers between devices, paired(): lax.ppermute(value, 'ctx', [(source, source + step) for source in range(f...  3.71 us
    ppermute x2, waiting for transfers between devices, paired(): lax.ppermute(value, 'ctx', [(source, source + step) for source in range(f...  1.99 us
  transfers between devices with their start and end apart: 9, of which 3 were waited for; matrix products, arithmetic and copies ran while one was open for 0% of the time, Pallas kernels for 4%

profile of v4, /device:TPU:6, one launch (start us, length us, event | category | flops | bytes accessed | tf_op | source)
XLA Modules:
  0.0 82.7 jit_solution(16019934299472012618)
XLA Ops:
  0.7 1.7 %shard_map.135 = bf16[144,768]{1,0:T(8,128)(2,1)} custom-call(bf16[128,256]{1,0:T(8,128)(2,1)} %key_ref.7, bf16[128,256]{1,0:T(8,128)(2,1)} %dir_ref.7, bf16[128,256]{1,0:T(8,128)(2,1)} %value_ref.5, f32[2,128]{1,0:T(2,128)} %rate_ref.5), custom_call_target="tpu_custom_call" | custom-call | tf_op jit(solution)/shard_map/pallas_call | solution.py:138
  2.4 0.0 copy-start.2
  2.4 0.0 copy-start.3
  2.4 4.3 %collective-permute-start = (bf16[144,768]{1,0:T(8,128)(2,1)}, bf16[144,768]{1,0:T(8,128)(2,1)S(1)}, u32[]{:S(2)}, u32[]{:S(2)}) collective-permute-start(bf16[144,768]{1,0:T(8,128)(2,1)} %shard_map.135), channel_id=1, source_target_pairs={{0,16},{8,24},{16,32},{24,40},{32,48},{40,56},{48,64},{56,72},{64,... | collective-permute-start | bytes 663560 | tf_op jit(solution)/shard_map/ppermute | solution.py:493
  6.7 4.3 %collective-permute-start.2 = (bf16[144,768]{1,0:T(8,128)(2,1)}, bf16[144,768]{1,0:T(8,128)(2,1)S(1)}, u32[]{:S(2)}, u32[]{:S(2)}) collective-permute-start(bf16[144,768]{1,0:T(8,128)(2,1)} %shard_map.135), channel_id=1, source_target_pairs={{0,32},{8,40},{16,48},{24,56},{32,64},{40,72},{48,80},{56,88},{64,... | collective-permute-start | bytes 663560 | tf_op jit(solution)/shard_map/ppermute | solution.py:493
  11.1 2.2 %shard_map.136 = (bf16[2,128,128]{2,1,0:T(8,128)(2,1)S(1)}, bf16[2,128,256]{2,1,0:T(8,128)(2,1)S(1)}, f32[2,128,256]{2,1,0:T(8,128)S(1)}) custom-call(bf16[128,256]{1,0:T(8,128)(2,1)S(1)} %copy-done.4, bf16[128,256]{1,0:T(8,128)(2,1)S(1)} %copy-done, bf16[128,256]{1,0:T(8,128)(2,1)S(1)} %copy-done.1, f32[2,128]{1,0:T(2,128)S(1)} %copy-done.5), custom_call_target="tpu_custom_call" | custom-call | flops 503316480 | bytes 656384 | tf_op jit(solution)/shard_map/pallas_call | solution.py:479
  13.3 1.9 %collective-permute-start.1 = (bf16[144,768]{1,0:T(8,128)(2,1)S(1)}, bf16[144,768]{1,0:T(8,128)(2,1)S(1)}, u32[]{:S(2)}, u32[]{:S(2)}) collective-permute-start(bf16[144,768]{1,0:T(8,128)(2,1)S(1)} %collective-permute-done.halo2_ref), channel_id=1, source_target_pairs={{0,8},{8,0},{16,24},{24,16},{32,40},{40,32},{48,56},{56,48},{64,72... | collective-permute-start | bytes 663560 | tf_op jit(solution)/shard_map/ppermute | solution.py:503
  15.3 2.4 %collective-permute-start.3 = (bf16[144,768]{1,0:T(8,128)(2,1)S(1)}, bf16[144,768]{1,0:T(8,128)(2,1)S(1)}, u32[]{:S(2)}, u32[]{:S(2)}) collective-permute-start(bf16[144,768]{1,0:T(8,128)(2,1)S(1)} %copy-done.8), channel_id=1, source_target_pairs={{0,8},{16,24},{32,40},{48,56},{64,72},{80,88},{96,104},{112,120},{... | collective-permute-start | bytes 663560 | tf_op jit(solution)/shard_map/ppermute | solution.py:498
  17.7 0.0 collective-permute-done.2.halo4_ref
  17.7 1.3 %collective-permute-start.4 = (bf16[144,768]{1,0:T(8,128)(2,1)S(1)}, bf16[144,768]{1,0:T(8,128)(2,1)S(1)}, u32[]{:S(2)}, u32[]{:S(2)}) collective-permute-start(bf16[144,768]{1,0:T(8,128)(2,1)S(1)} %collective-permute-done.2.halo4_ref), channel_id=1, source_target_pairs={{8,0},{24,16},{40,32},{56,48},{72,64},{88,80},{104,96},{120,112},{... | collective-permute-start | bytes 663560 | tf_op jit(solution)/shard_map/ppermute | solution.py:498
  19.0 0.1 pad_add_fusion.place_ref
  19.1 2.0 %collective-permute-done.4.cross4_ref = bf16[144,768]{1,0:T(8,128)(2,1)S(1)} collective-permute-done((bf16[144,768]{1,0:T(8,128)(2,1)S(1)}, bf16[144,768]{1,0:T(8,128)(2,1)S(1)}, u32[]{:S(2)}, u32[]{:S(2)}) %collective-permute-start.4) | collective-permute-done | bytes 221216 | tf_op jit(solution)/shard_map/ppermute | solution.py:498
  21.1 5.9 %shard_map.137 = (f32[128,256]{1,0:T(8,128)S(1)}, f32[2,128,8]{2,1,0:T(8,128)S(1)}, bf16[2,5,128,128]{3,2,1,0:T(8,128)(2,1)S(1)}, bf16[2,4,128,128]{3,2,1,0:T(8,...) custom-call(f32[2,128,256]{2,1,0:T(8,128)S(1)} %get-tuple-element.42, ...), custom_call_target="tpu_custom_call" | custom-call | flops 2516582400 | bytes 3023872 | tf_op jit(solution)/shard_map/pallas_call | solution.py:479
  27.1 14.6 %all_to_all.10.sums_ref = f32[8,1,256]{2,1,0:T(1,128)S(1)} all-to-all(f32[8,1,256]{2,1,0:T(1,128)S(1)} %get-tuple-element.46), channel_id=1, replica_groups=mesh['ctx'=64,'head'=8] {'head'}, dimensions={0} | all-to-all | bytes 16384 | tf_op jit(solution)/shard_map/all_to_all | solution.py:507
  41.7 2.2 %shard_map.138 = (bf16[128,256]{1,0:T(8,128)(2,1)}, f32[1,256]{1,0:T(1,128)S(1)}, bf16[2,128,256]{2,1,0:T(8,128)(2,1)S(1)}, f32[128,256]{1,0:T(8,128)S(1)}, bf16...) custom-call(f32[8,1,256]{2,1,0:T(1,128)S(1)} %all_to_all.10.sums_ref, ...), custom_call_target="tpu_custom_call" | custom-call | flops 251658240 | bytes 2820096 | tf_op jit(solution)/shard_map/pallas_call | solution.py:479
  43.9 1.9 %collective-permute-start.5 = (bf16[144,1536]{1,0:T(8,128)(2,1)S(1)}, bf16[144,1536]{1,0:T(8,128)(2,1)S(1)}, u32[]{:S(2)}, u32[]{:S(2)}) collective-permute-start(bf16[144,1536]{1,0:T(8,128)(2,1)S(1)} %get-tuple-element.60), channel_id=1, source_target_pairs={{0,8},{8,0},{16,24},{24,16},{32,40},{40,32},{48,56},{56,48},{64,72... | collective-permute-start | bytes 1327112 | tf_op jit(solution)/shard_map/ppermute | solution.py:503
  45.8 1.8 %collective-permute-done.5.cross_ref = bf16[144,1536]{1,0:T(8,128)(2,1)S(1)} collective-permute-done((bf16[144,1536]{1,0:T(8,128)(2,1)S(1)}, bf16[144,1536]{1,0:T(8,128)(2,1)S(1)}, u32[]{:S(2)}, u32[]{:S(2)}) %collective-permute-start.5) | collective-permute-done | bytes 442400 | tf_op jit(solution)/shard_map/ppermute | solution.py:503
  47.6 1.2 %shard_map.140 = (f32[32,1,256]{2,1,0:T(1,128)}, bf16[128,768]{1,0:T(8,128)(2,1)S(1)}, bf16[128,768]{1,0:T(8,128)(2,1)S(1)}, bf16[128,768]{1,0:T(8,128)(2,1)S(1)}) custom-call(f32[1,256]{1,0:T(1,128)S(1)} %get-tuple-element.57.part_ref, bf16[128,768]{1,0:T(8,128)(2,1)S(1)} %get-tuple-element.58.mine2_ref, bf16[128,768]{1,0:T(8,128)(2,1)S(1)} %get-tuple-element.59.mine4_ref, ...), custom_call_target="tpu_custom_call" | custom-call | bytes 1459200 | tf_op jit(solution)/shard_map/pallas_call | solution.py:479
  48.8 1.9 %collective-permute-start.6 = (bf16[128,768]{1,0:T(8,128)(2,1)S(1)}, bf16[128,768]{1,0:T(8,128)(2,1)S(1)}, u32[]{:S(2)}, u32[]{:S(2)}) collective-permute-start(bf16[128,768]{1,0:T(8,128)(2,1)S(1)} %get-tuple-element.62), channel_id=1, source_target_pairs={{16,0},{24,8},{32,16},{40,24},{48,32},{56,40},{64,48},{72,56},{80,... | collective-permute-start | bytes 589832 | tf_op jit(solution)/shard_map/ppermute | solution.py:493
  50.8 3.4 %collective-permute-start.7 = (bf16[128,768]{1,0:T(8,128)(2,1)S(1)}, bf16[128,768]{1,0:T(8,128)(2,1)S(1)}, u32[]{:S(2)}, u32[]{:S(2)}) collective-permute-start(bf16[128,768]{1,0:T(8,128)(2,1)S(1)} %get-tuple-element.63), channel_id=1, source_target_pairs={{32,0},{40,8},{48,16},{56,24},{64,32},{72,40},{80,48},{88,56},{96,... | collective-permute-start | bytes 589832 | tf_op jit(solution)/shard_map/ppermute | solution.py:493
  54.1 18.4 %all-to-all-start.1 = ((f32[32,1,256]{2,1,0:T(1,128)}), f32[32,1,256]{2,1,0:T(1,128)S(1)}, u32[]{:S(2)}, u32[]{:S(2)}) async-start(f32[32,1,256]{2,1,0:T(1,128)} %get-tuple-element.69), calls=%async_computation.1 | async-start | bytes 65536 | tf_op jit(solution)/shard_map/all_to_all | solution.py:507
  72.5 1.2 %shard_map.139 = (bf16[128,256]{1,0:T(8,128)(2,1)}, f32[2,128,128]{2,1,0:T(8,128)S(1)}, f32[2,128,128]{2,1,0:T(8,128)S(1)}, f32[2,128,256]{2,1,0:T(8,128)S(1)}) custom-call(bf16[2,128,256]{2,1,0:T(8,128)(2,1)S(1)} %get-tuple-element.54.own_ref, bf16[2,128,256]{2,1,0:T(8,128)(2,1)S(1)} %get-tuple-element.55.kw_ref, bf16[128,256]{1,0:T(8,128)(2,1)S(1)} %copy-done.4, ...), custom_call_target="tpu_custom_call" | custom-call | flops 83886080 | bytes 1048576 | tf_op jit(solution)/shard_map/pallas_call | solution.py:479
  73.8 6.9 %all-to-all-done.1.parts_ref = f32[32,1,256]{2,1,0:T(1,128)S(1)} async-done(((f32[32,1,256]{2,1,0:T(1,128)}), f32[32,1,256]{2,1,0:T(1,128)S(1)}, u32[]{:S(2)}, u32[]{:S(2)}) %all-to-all-start.1) | async-done | bytes 32800 | tf_op jit(solution)/shard_map/all_to_all | solution.py:507
  80.7 2.0 %shard_map.141 = (bf16[128,256]{1,0:T(8,128)(2,1)}, bf16[128,256]{1,0:T(8,128)(2,1)}, bf16[128,256]{1,0:T(8,128)(2,1)}, f32[2,128]{1,0:T(2,128)}, f32[1,256]{1,0:T(1,128)}) custom-call(bf16[128,768]{1,0:T(8,128)(2,1)S(1)} %get-tuple-element.61.near_ref, bf16[128,768]{1,0:T(8,128)(2,1)S(1)} %collective-permute-done.6.recv2_ref, ...), custom_call_target="tpu_custom_call" | custom-call | flops 167772160 | bytes 1805312 | tf_op jit(solution)/shard_map/pallas_call | solution.py:479
  (21 shorter events, 0.0 us)
Async XLA Ops:
  0.6 10.5 %copy-start.1 = (bf16[128,256]{1,0:T(8,128)(2,1)S(1)}, bf16[128,256]{1,0:T(8,128)(2,1)}, u32[]{:S(2)}) copy-start(bf16[128,256]{1,0:T(8,128)(2,1)} %dir_ref.7) | copy-start | bytes 196612
  0.6 10.5 %copy-start = (bf16[128,256]{1,0:T(8,128)(2,1)S(1)}, bf16[128,256]{1,0:T(8,128)(2,1)}, u32[]{:S(2)}) copy-start(bf16[128,256]{1,0:T(8,128)(2,1)} %key_ref.7) | copy-start | bytes 196612
  0.7 10.5 %copy-start.5 = (f32[2,128]{1,0:T(2,128)S(1)}, f32[2,128]{1,0:T(2,128)}, u32[]{:S(2)}) copy-start(f32[2,128]{1,0:T(2,128)} %rate_ref.5) | copy-start | bytes 3076
  0.7 10.5 %copy-start.4 = (bf16[128,256]{1,0:T(8,128)(2,1)S(1)}, bf16[128,256]{1,0:T(8,128)(2,1)}, u32[]{:S(2)}) copy-start(bf16[128,256]{1,0:T(8,128)(2,1)} %query_ref.3) | copy-start | bytes 196612
  2.4 12.9 %copy-start.8 = (bf16[144,768]{1,0:T(8,128)(2,1)S(1)}, bf16[144,768]{1,0:T(8,128)(2,1)}, u32[]{:S(2)}) copy-start(bf16[144,768]{1,0:T(8,128)(2,1)} %shard_map.135) | copy-start | bytes 663556
  2.4 18.7 %copy-start.2 = (bf16[128,256]{1,0:T(8,128)(2,1)S(1)}, bf16[128,256]{1,0:T(8,128)(2,1)}, u32[]{:S(2)}) copy-start(bf16[128,256]{1,0:T(8,128)(2,1)} %value_ref.5) | copy-start | bytes 196612
  2.4 18.7 %copy-start.3 = (bf16[128,256]{1,0:T(8,128)(2,1)S(1)}, bf16[128,256]{1,0:T(8,128)(2,1)}, u32[]{:S(2)}) copy-start(bf16[128,256]{1,0:T(8,128)(2,1)} %cot_ref.3) | copy-start | bytes 196612
  2.4 10.9 %collective-permute-start = (bf16[144,768]{1,0:T(8,128)(2,1)}, bf16[144,768]{1,0:T(8,128)(2,1)S(1)}, u32[]{:S(2)}, u32[]{:S(2)}) collective-permute-start(bf16[144,768]{1,0:T(8,128)(2,1)} %shard_map.135), channel_id=1, source_target_pairs={{0,16},{8,24},{16,32},{24,40},{32,48},{40,56},{48,64},{56,72},{64,... | collective-permute-start | bytes 663560 | tf_op jit(solution)/shard_map/ppermute | solution.py:493
  6.7 11.0 %collective-permute-start.2 = (bf16[144,768]{1,0:T(8,128)(2,1)}, bf16[144,768]{1,0:T(8,128)(2,1)S(1)}, u32[]{:S(2)}, u32[]{:S(2)}) collective-permute-start(bf16[144,768]{1,0:T(8,128)(2,1)} %shard_map.135), channel_id=1, source_target_pairs={{0,32},{8,40},{16,48},{24,56},{32,64},{40,72},{48,80},{56,88},{64,... | collective-permute-start | bytes 663560 | tf_op jit(solution)/shard_map/ppermute | solution.py:493
  13.3 4.4 %collective-permute-start.1 = (bf16[144,768]{1,0:T(8,128)(2,1)S(1)}, bf16[144,768]{1,0:T(8,128)(2,1)S(1)}, u32[]{:S(2)}, u32[]{:S(2)}) collective-permute-start(bf16[144,768]{1,0:T(8,128)(2,1)S(1)} %collective-permute-done.halo2_ref), channel_id=1, source_target_pairs={{0,8},{8,0},{16,24},{24,16},{32,40},{40,32},{48,56},{56,48},{64,72... | collective-permute-start | bytes 663560 | tf_op jit(solution)/shard_map/ppermute | solution.py:503
  15.3 3.8 %collective-permute-start.3 = (bf16[144,768]{1,0:T(8,128)(2,1)S(1)}, bf16[144,768]{1,0:T(8,128)(2,1)S(1)}, u32[]{:S(2)}, u32[]{:S(2)}) collective-permute-start(bf16[144,768]{1,0:T(8,128)(2,1)S(1)} %copy-done.8), channel_id=1, source_target_pairs={{0,8},{16,24},{32,40},{48,56},{64,72},{80,88},{96,104},{112,120},{... | collective-permute-start | bytes 663560 | tf_op jit(solution)/shard_map/ppermute | solution.py:498
  17.7 3.4 %collective-permute-start.4 = (bf16[144,768]{1,0:T(8,128)(2,1)S(1)}, bf16[144,768]{1,0:T(8,128)(2,1)S(1)}, u32[]{:S(2)}, u32[]{:S(2)}) collective-permute-start(bf16[144,768]{1,0:T(8,128)(2,1)S(1)} %collective-permute-done.2.halo4_ref), channel_id=1, source_target_pairs={{8,0},{24,16},{40,32},{56,48},{72,64},{88,80},{104,96},{120,112},{... | collective-permute-start | bytes 663560 | tf_op jit(solution)/shard_map/ppermute | solution.py:498
  19.1 2.0 %copy-start.6 = (f32[256]{0:T(256)S(1)}, f32[256]{0:T(256)}, u32[]{:S(2)}) copy-start(f32[256]{0:T(256)} %param.13) | copy-start | bytes 3076
  19.1 2.0 %copy-start.7 = (s32[32]{0:T(128)S(1)}, s32[32]{0:T(128)}, u32[]{:S(2)}) copy-start(s32[32]{0:T(128)} %len_ref.1) | copy-start | bytes 388
  43.9 3.7 %collective-permute-start.5 = (bf16[144,1536]{1,0:T(8,128)(2,1)S(1)}, bf16[144,1536]{1,0:T(8,128)(2,1)S(1)}, u32[]{:S(2)}, u32[]{:S(2)}) collective-permute-start(bf16[144,1536]{1,0:T(8,128)(2,1)S(1)} %get-tuple-element.60), channel_id=1, source_target_pairs={{0,8},{8,0},{16,24},{24,16},{32,40},{40,32},{48,56},{56,48},{64,72... | collective-permute-start | bytes 1327112 | tf_op jit(solution)/shard_map/ppermute | solution.py:503
  48.8 31.9 %collective-permute-start.6 = (bf16[128,768]{1,0:T(8,128)(2,1)S(1)}, bf16[128,768]{1,0:T(8,128)(2,1)S(1)}, u32[]{:S(2)}, u32[]{:S(2)}) collective-permute-start(bf16[128,768]{1,0:T(8,128)(2,1)S(1)} %get-tuple-element.62), channel_id=1, source_target_pairs={{16,0},{24,8},{32,16},{40,24},{48,32},{56,40},{64,48},{72,56},{80,... | collective-permute-start | bytes 589832 | tf_op jit(solution)/shard_map/ppermute | solution.py:493
  50.8 29.9 %collective-permute-start.7 = (bf16[128,768]{1,0:T(8,128)(2,1)S(1)}, bf16[128,768]{1,0:T(8,128)(2,1)S(1)}, u32[]{:S(2)}, u32[]{:S(2)}) collective-permute-start(bf16[128,768]{1,0:T(8,128)(2,1)S(1)} %get-tuple-element.63), channel_id=1, source_target_pairs={{32,0},{40,8},{48,16},{56,24},{64,32},{72,40},{80,48},{88,56},{96,... | collective-permute-start | bytes 589832 | tf_op jit(solution)/shard_map/ppermute | solution.py:493
  54.1 26.6 %all-to-all-start.1 = ((f32[32,1,256]{2,1,0:T(1,128)}), f32[32,1,256]{2,1,0:T(1,128)S(1)}, u32[]{:S(2)}, u32[]{:S(2)}) async-start(f32[32,1,256]{2,1,0:T(1,128)} %get-tuple-element.69), calls=%async_computation.1 | async-start | bytes 65536 | tf_op jit(solution)/shard_map/all_to_all | solution.py:507

commit v5 on v4

--- a/solution.py
+++ b/solution.py
@@ -280,7 +280,27 @@
     sums_ref[...] = jnp.broadcast_to(row[None], sums_ref.shape)
 
 
-def back_kernel(
+def back_block(h, s, scaled, delta, prob, value, frame, matrix, carried, send):
+    width = scaled.shape[1]
+    lanes = slice(h * DH, (h + 1) * DH)
+    through = mm(scaled[:, lanes], value, "nt")
+    dscore = (prob.astype(F32) * ((through - delta) * (DH ** (-0.5)))).astype(BF16)
+    send[:, lanes] = mm(prob, scaled[:, lanes], "tn").astype(send.dtype)
+    if frame is None:
+        return jnp.concatenate([dscore, carried], axis=1)
+    at_end = slice(width + h * DH, width + (h + 1) * DH)
+    at_trans = slice(2 * width + h * DH, 2 * width + (h + 1) * DH)
+    if carried is None:
+        send[:, at_end] = mm(frame, dscore, "tn").astype(BF16)
+        return mm(dscore, matrix[:, 0:DH], "nt").astype(BF16)
+    both = jnp.concatenate([dscore, carried], axis=1)
+    grads = mm(frame, both, "tn").astype(BF16)
+    send[:, at_end] = grads[:, 0:DH]
+    send[:, at_trans] = grads[:, DH : 2 * DH]
+    return mm(both, matrix, "nt").astype(BF16)
+
+
+def far_back_kernel(
     heads,
     features,
     sums_ref,
@@ -289,22 +309,18 @@
     prob_ref,
     frame_ref,
     kt_ref,
-    value_ref,
     cot_ref,
     gain_ref,
     far_ref,
     normed_ref,
-    part_ref,
-    own_ref,
-    dval_ref,
-    cross_ref,
-    send2_ref,
+    parts_ref,
+    scaled_ref,
+    delta_ref,
+    carried_ref,
+    send3_ref,
     send4_ref,
 ):
-    size = value_ref.shape[0]
-    width = heads * DH
-    block = 3 * width
-    places = ((cross_ref, 0), (send2_ref, 0), (cross_ref, block), (send4_ref, 0))
+    size = att_ref.shape[0]
     rows, cols = grids(size)
     eye = rows == cols
     sums = jnp.sum(sums_ref[...], axis=0)
@@ -318,68 +334,49 @@
     normed = att_all * inverse
     normed_ref[...] = (normed * gain).astype(BF16)
     part = jnp.sum(cot_all * normed, axis=0, keepdims=True)
-    part_ref[...] = part
-    cross_ref[size : size + 16, 0:width] = rate_pieces(part, 16, width)
-    cross_ref[size : size + 16, width : 2 * block] = jnp.zeros((16, 2 * block - width), BF16)
-    send4_ref[:, 2 * width : block] = jnp.zeros((size, width), BF16)
+    parts_ref[...] = jnp.broadcast_to(part[None], parts_ref.shape)
     grad_att = cot_all * gain * inverse - att_all * pull
-    scale = DH ** (-0.5)
     for h in range(heads):
         lanes = slice(h * DH, (h + 1) * DH)
         total = tot_ref[h, :, 0:1]
         grad = grad_att[:, lanes]
-        scaled = (grad / total).astype(BF16)
+        scaled_ref[:, lanes] = (grad / total).astype(BF16)
         delta = jnp.sum(grad * att_all[:, lanes], axis=1, keepdims=True) / total
+        delta_ref[h] = jnp.broadcast_to(delta, (size, 8))
         carried = None
-        for s in range(WIN, -1, -1):
-            if s == 0:
-                value = value_ref[:, lanes]
-            else:
-                value = far_ref[s - 1, :, lanes]
-            prob = prob_ref[h, s]
-            through = mm(scaled, value, "nt")
-            dscore = (prob.astype(F32) * ((through - delta) * scale)).astype(BF16)
-            dvalue = mm(prob, scaled, "tn")
-            if s == 0:
-                dval_ref[:, lanes] = dvalue
-                own_ref[h] = jnp.concatenate([dscore, carried], axis=1)
-                continue
-            send, base = places[s - 1]
-            at_value = slice(base + h * DH, base + (h + 1) * DH)
-            at_end = slice(base + width + h * DH, base + width + (h + 1) * DH)
-            at_trans = slice(base + 2 * width + h * DH, base + 2 * width + (h + 1) * DH)
-            send[0:size, at_value] = dvalue.astype(BF16)
-            if carried is None:
-                send[0:size, at_end] = mm(frame_ref[h, s - 1], dscore, "tn").astype(BF16)
-                carried = mm(dscore, kt_ref[h, s - 1, :, 0:DH], "nt").astype(BF16)
-            else:
-                both = jnp.concatenate([dscore, carried], axis=1)
-                grads = mm(frame_ref[h, s - 1], both, "tn").astype(BF16)
-                send[0:size, at_end] = grads[:, 0:DH]
-                send[0:size, at_trans] = grads[:, DH : 2 * DH]
-                carried = mm(both, kt_ref[h, s - 1], "nt").astype(BF16)
-
-
-def merge_kernel(part_ref, mine2_ref, mine4_ref, cross_ref, place_ref, parts_ref, near_ref, send2_ref, send4_ref):
-    size, block = mine2_ref.shape
-    width = part_ref.shape[1]
-    other = jnp.sum(cross_ref[size : size + 16, 0:width].astype(F32), axis=0, keepdims=True)
-    parts_ref[...] = jnp.broadcast_to((part_ref[...] + other)[None], parts_ref.shape)
-
-    @pl.when(place_ref[1] == 0)
-    def _():
-        near_ref[...] = cross_ref[0:size, 0:block]
-        total = mine2_ref[...].astype(F32) + cross_ref[0:size, block : 2 * block].astype(F32)
-        send2_ref[...] = total.astype(BF16)
-        send4_ref[...] = mine4_ref[...]
-
-    @pl.when(place_ref[1] != 0)
-    def _():
-        near_ref[...] = jnp.zeros((size, block), BF16)
-        total = mine2_ref[...].astype(F32) + cross_ref[0:size, 0:block].astype(F32)
-        send2_ref[...] = total.astype(BF16)
-        total = mine4_ref[...].astype(F32) + cross_ref[0:size, block : 2 * block].astype(F32)
-        send4_ref[...] = total.astype(BF16)
+        for s, send in ((4, send4_ref), (3, send3_ref)):
+            carried = back_block(
+                h, s, scaled_ref, delta, prob_ref[h, s], far_ref[s - 1, :, lanes], frame_ref[h, s - 1], kt_ref[h, s - 1], carried, send
+            )
+        carried_ref[h] = carried
+
+
+def near_back_kernel(
+    heads,
+    scaled_ref,
+    delta_ref,
+    carried_ref,
+    prob_ref,
+    frame_ref,
+    kt_ref,
+    value_ref,
+    far_ref,
+    own_ref,
+    dval_ref,
+    send1_ref,
+    send2_ref,
+):
+    for h in range(heads):
+        lanes = slice(h * DH, (h + 1) * DH)
+        delta = delta_ref[h, :, 0:1]
+        carried = carried_ref[h]
+        for s, send in ((2, send2_ref), (1, send1_ref)):
+            carried = back_block(
+                h, s, scaled_ref, delta, prob_ref[h, s], far_ref[s - 1, :, lanes], frame_ref[h, s - 1], kt_ref[h, s - 1], carried, send
+            )
+        own_ref[h] = back_block(
+            h, 0, scaled_ref, delta, prob_ref[h, 0], value_ref[:, lanes], None, None, carried, dval_ref
+        )
 
 
 def local_kernel(heads, own_ref, kw_ref, query_ref, key_ref, dir_ref, dquery_ref, dkey_ref, ddir_ref, pulled_ref):
@@ -406,8 +403,9 @@
 
 def shard_kernel(
     heads,
-    near_ref,
+    recv1_ref,
     recv2_ref,
+    recv3_ref,
     recv4_ref,
     inv_ref,
     kw_ref,
@@ -427,7 +425,7 @@
 ):
     size = key_ref.shape[0]
     width = heads * DH
-    recvs = (near_ref, recv2_ref, recv4_ref)
+    recvs = (recv1_ref, recv2_ref, recv3_ref, recv4_ref)
     rows, cols = grids(size)
     eye = rows == cols
     strict = rows > cols
@@ -448,7 +446,8 @@
         dtrans = jnp.zeros((size, DH), F32)
         for recv in recvs:
             dend = dend + recv[:, width + h * DH : width + (h + 1) * DH].astype(F32)
-            dtrans = dtrans + recv[:, 2 * width + h * DH : 2 * width + (h + 1) * DH].astype(F32)
+            if recv.shape[1] == 3 * width:
+                dtrans = dtrans + recv[:, 2 * width + h * DH : 2 * width + (h + 1) * DH].astype(F32)
         both = jnp.concatenate([dend, dtrans], axis=1).astype(BF16)
         coef = kw_ref[h]
         dcoef = -(pulled_ref[h] + mm(unit_half, both))
@@ -483,7 +482,7 @@
         out_specs=[vmem] * len(outs),
         scratch_shapes=list(scratch),
         compiler_params=pltpu.CompilerParams(vmem_limit_bytes=VMEM_LIMIT),
-        cost_estimate=pl.CostEstimate(flops=flops, bytes_accessed=moved, transcendentals=0),
+        cost_estimate=pl.CostEstimate(flops=flops, bytes_accessed=moved if flops else 0, transcendentals=0),
     )(*operands, *scalars)
 
 
@@ -518,17 +517,18 @@
     packed = pack(keys, dirs, values, rates)
     halo2 = passed_along(packed, 2)
     halo4 = passed_along(packed, 4)
+    even = paired(packed, 0, 1)
+    even, own_keys = lax.optimization_barrier((even, keys))
     inverse, coef, raw = call(
         own_kernel,
         [((heads, size, size), BF16), ((heads, size, 2 * DH), BF16), ((heads, size, 2 * DH), F32)],
         heads * 60 * unit_flops,
         query,
-        keys,
+        own_keys,
         dirs,
         rates,
     )
     halo2, raw = lax.optimization_barrier((halo2, raw))
-    even = paired(packed, 0, 1)
     cross2 = swapped(halo2)
     cross2, halo4 = lax.optimization_barrier((cross2, halo4))
     halos = (halo2, halo4, even, cross2, paired(halo4, 1, -1))
@@ -553,40 +553,53 @@
         scratch=[pltpu.VMEM((size + 16, 3 * width), BF16)] * 2,
     )
     sums = gathered(sums, "head")
-    normed, part, own, dval, cross, mine2, mine4 = call(
-        functools.partial(back_kernel, heads, features),
+    count = lax.axis_size("ctx")
+    normed, parts, scaled, delta, carried, send3, send4 = call(
+        functools.partial(far_back_kernel, heads, features),
         [
             ((size, width), BF16),
-            ((1, width), F32),
-            ((heads, size, 2 * DH), BF16),
-            ((size, width), F32),
-            ((size + 16, 6 * width), BF16),
+            ((count, 1, width), F32),
+            ((size, width), BF16),
+            ((heads, size, 8), F32),
+            ((heads, size, DH), BF16),
             ((size, 3 * width), BF16),
-            ((size, 3 * width), BF16),
+            ((size, 2 * width), BF16),
         ],
-        heads * 30 * unit_flops,
+        heads * 15 * unit_flops,
         sums,
         att,
         total,
         prob,
         frame,
         carry,
-        values,
         cotangent,
         gain_row,
         far,
     )
-    count = lax.axis_size("ctx")
-    parts, near, send2, send4 = call(
-        merge_kernel,
-        [((count // 2, 1, width), F32)] + [((size, 3 * width), BF16)] * 3,
-        0,
-        part,
-        mine2,
-        mine4,
-        swapped(cross),
-        scalars=(place,),
-    )
+    recv4 = passed_along(send4, -4)
+    recv3 = passed_along(send3, -3)
+    parts = gathered(parts, "ctx")
+    scaled, recv3, recv4 = lax.optimization_barrier((scaled, recv3, recv4))
+    own, dval, send1, send2 = call(
+        functools.partial(near_back_kernel, heads),
+        [
+            ((heads, size, 2 * DH), BF16),
+            ((size, width), F32),
+            ((size, 3 * width), BF16),
+            ((size, 3 * width), BF16),
+        ],
+        heads * 3000 * unit_flops,
+        scaled,
+        delta,
+        carried,
+        prob,
+        frame,
+        carry,
+        values,
+        far,
+    )
+    own, parts = lax.optimization_barrier((own, parts))
+    recvs = (passed_along(send1, -1), passed_along(send2, -2), recv3, recv4)
     dquery, dkey_part, ddir_part, pulled = call(
         functools.partial(local_kernel, heads),
         [
@@ -595,15 +608,13 @@
             ((heads, size, DH), F32),
             ((heads, size, 2 * DH), F32),
         ],
-        heads * 10 * unit_flops,
+        heads * 150 * unit_flops,
         own,
         coef,
         query,
         keys,
         dirs,
     )
-    recvs = (near, passed_along(send2, -2), passed_along(send4, -4))
-    parts = gathered(parts, "ctx", [list(range(core, count, 2)) for core in range(2)])
     dkey, dvalue, ddir, drate, dgain = call(
         functools.partial(shard_kernel, heads),
         [((size, width), BF16), ((size, width), BF16), ((size, width), BF16), ((heads, size), F32), ((1, width), F32)],

time: 83.8 us -> 84 us (level)
  starting transfers between devices: 39.9 us -> 41.6 us
  Pallas kernels: 16.6 us -> 15.5 us
    ppermute x4 -> x6, waiting for transfers between devices: 0.01 us -> 6.79 us  [passed_along(): lax.ppermute(value, 'ctx', [(source, source + steps) for source in range(...]
    all_to_all x1, waiting for transfers between devices: 6.92 us -> 2.12 us  [gathered(): lax.all_to_all(value, axis, 0, 0, axis_index_groups=groups, tiled=True)]
    ppermute x4 -> x6, starting transfers between devices: 13.9 us -> 17.8 us  [passed_along(): lax.ppermute(value, 'ctx', [(source, source + steps) for source in range(...]
    ppermute x2 -> x1, starting transfers between devices: 3.83 us -> 1.92 us  [swapped(): lax.ppermute(value, 'ctx', [(source, source ^ 1) for source in range(coun...]
    ppermute x2 -> x1, waiting for transfers between devices: 1.76 us -> 0.01 us  [swapped(): lax.ppermute(value, 'ctx', [(source, source ^ 1) for source in range(coun...]
    pallas_call x6, Pallas kernels: 14.9 us -> 13.8 us  [call(): pl.pallas_call(body, out_shape=[jax.ShapeDtypeStruct(s, d) for s, d in ou...]
  transfers between devices with their start and end apart: 9 -> 10, of which waited for: 3 -> 4; matrix products, arithmetic and copies ran while one was open for 0% -> 0% of each run, Pallas kernels for 4% -> 5%
where the time goes in v5:
time: 84 us; the launch traced here: 83.6 us
  starting transfers between devices  41.6 us (50%)
  Pallas kernels  15.5 us (18%)
  blocking collectives  14.6 us (17%)
  waiting for transfers between devices  10.9 us (13%)
  between operations  0.87 us (1%)
    all_to_all x1, starting transfers between devices, gathered(): lax.all_to_all(value, axis, 0, 0, axis_index_groups=groups, tiled=True)  18.7 us
    ppermute x6, starting transfers between devices, passed_along(): lax.ppermute(value, 'ctx', [(source, source + steps) for source in range(...  17.8 us
    all_to_all x1, blocking collectives, gathered(): lax.all_to_all(value, axis, 0, 0, axis_index_groups=groups, tiled=True)  14.6 us
    pallas_call x6, Pallas kernels, call(): pl.pallas_call(body, out_shape=[jax.ShapeDtypeStruct(s, d) for s, d in ou...  13.8 us
    ppermute x6, waiting for transfers between devices, passed_along(): lax.ppermute(value, 'ctx', [(source, source + steps) for source in range(...  6.79 us
    ppermute x2, starting transfers between devices, paired(): lax.ppermute(value, 'ctx', [(source, source + step) for source in range(f...  3.16 us
    all_to_all x1, waiting for transfers between devices, gathered(): lax.all_to_all(value, axis, 0, 0, axis_index_groups=groups, tiled=True)  2.12 us
    ppermute x2, waiting for transfers between devices, paired(): lax.ppermute(value, 'ctx', [(source, source + step) for source in range(f...  1.99 us
  transfers between devices with their start and end apart: 10, of which 4 were waited for; matrix products, arithmetic and copies ran while one was open for 0% of the time, Pallas kernels for 5%

profile of v5, /device:TPU:6, one launch (start us, length us, event | category | flops | bytes accessed | tf_op | source)
XLA Modules:
  0.0 83.6 jit_solution(2700983743608635489)
XLA Ops:
  0.7 1.7 %shard_map.135 = bf16[144,768]{1,0:T(8,128)(2,1)} custom-call(bf16[128,256]{1,0:T(8,128)(2,1)} %key_ref.6, bf16[128,256]{1,0:T(8,128)(2,1)} %dir_ref.7, bf16[128,256]{1,0:T(8,128)(2,1)} %value_ref.5, f32[2,128]{1,0:T(2,128)} %rate_ref.5), custom_call_target="tpu_custom_call" | custom-call | tf_op jit(solution)/shard_map/pallas_call | solution.py:138
  2.4 0.0 copy-start.2
  2.4 1.9 %collective-permute-start.1 = (bf16[144,768]{1,0:T(8,128)(2,1)}, bf16[144,768]{1,0:T(8,128)(2,1)S(1)}, u32[]{:S(2)}, u32[]{:S(2)}) collective-permute-start(bf16[144,768]{1,0:T(8,128)(2,1)} %shard_map.135), channel_id=1, source_target_pairs={{0,8},{16,24},{32,40},{48,56},{64,72},{80,88},{96,104},{112,120},{... | collective-permute-start | bytes 663560 | tf_op jit(solution)/shard_map/ppermute | solution.py:497
  4.3 4.2 %collective-permute-start = (bf16[144,768]{1,0:T(8,128)(2,1)}, bf16[144,768]{1,0:T(8,128)(2,1)S(1)}, u32[]{:S(2)}, u32[]{:S(2)}) collective-permute-start(bf16[144,768]{1,0:T(8,128)(2,1)} %shard_map.135), channel_id=1, source_target_pairs={{0,16},{8,24},{16,32},{24,40},{32,48},{40,56},{48,64},{56,72},{64,... | collective-permute-start | bytes 663560 | tf_op jit(solution)/shard_map/ppermute | solution.py:492
  8.5 4.3 %collective-permute-start.3 = (bf16[144,768]{1,0:T(8,128)(2,1)}, bf16[144,768]{1,0:T(8,128)(2,1)S(1)}, u32[]{:S(2)}, u32[]{:S(2)}) collective-permute-start(bf16[144,768]{1,0:T(8,128)(2,1)} %shard_map.135), channel_id=1, source_target_pairs={{0,32},{8,40},{16,48},{24,56},{32,64},{40,72},{48,80},{56,88},{64,... | collective-permute-start | bytes 663560 | tf_op jit(solution)/shard_map/ppermute | solution.py:492
  12.9 2.2 %shard_map.136 = (bf16[2,128,128]{2,1,0:T(8,128)(2,1)S(1)}, bf16[2,128,256]{2,1,0:T(8,128)(2,1)S(1)}, f32[2,128,256]{2,1,0:T(8,128)S(1)}) custom-call(bf16[128,256]{1,0:T(8,128)(2,1)S(1)} %copy-done.6, bf16[128,256]{1,0:T(8,128)(2,1)S(1)} %copy-done, bf16[128,256]{1,0:T(8,128)(2,1)S(1)} %copy-done.1, f32[2,128]{1,0:T(2,128)S(1)} %copy-done.4), custom_call_target="tpu_custom_call" | custom-call | flops 503316480 | bytes 656384 | tf_op jit(solution)/shard_map/pallas_call | solution.py:478
  15.1 1.9 %collective-permute-start.2 = (bf16[144,768]{1,0:T(8,128)(2,1)S(1)}, bf16[144,768]{1,0:T(8,128)(2,1)S(1)}, u32[]{:S(2)}, u32[]{:S(2)}) collective-permute-start(bf16[144,768]{1,0:T(8,128)(2,1)S(1)} %collective-permute-done.halo2_ref), channel_id=1, source_target_pairs={{0,8},{8,0},{16,24},{24,16},{32,40},{40,32},{48,56},{56,48},{64,72... | collective-permute-start | bytes 663560 | tf_op jit(solution)/shard_map/ppermute | solution.py:502
  17.0 1.5 %collective-permute-done.3.halo4_ref = bf16[144,768]{1,0:T(8,128)(2,1)S(1)} collective-permute-done((bf16[144,768]{1,0:T(8,128)(2,1)}, bf16[144,768]{1,0:T(8,128)(2,1)S(1)}, u32[]{:S(2)}, u32[]{:S(2)}) %collective-permute-start.3) | collective-permute-done | bytes 221216 | tf_op jit(solution)/shard_map/ppermute | solution.py:492
  18.5 1.3 %collective-permute-start.4 = (bf16[144,768]{1,0:T(8,128)(2,1)S(1)}, bf16[144,768]{1,0:T(8,128)(2,1)S(1)}, u32[]{:S(2)}, u32[]{:S(2)}) collective-permute-start(bf16[144,768]{1,0:T(8,128)(2,1)S(1)} %collective-permute-done.3.halo4_ref), channel_id=1, source_target_pairs={{8,0},{24,16},{40,32},{56,48},{72,64},{88,80},{104,96},{120,112},{... | collective-permute-start | bytes 663560 | tf_op jit(solution)/shard_map/ppermute | solution.py:497
  19.8 0.1 pad_add_fusion.place_ref
  19.9 2.0 %collective-permute-done.4.cross4_ref = bf16[144,768]{1,0:T(8,128)(2,1)S(1)} collective-permute-done((bf16[144,768]{1,0:T(8,128)(2,1)S(1)}, bf16[144,768]{1,0:T(8,128)(2,1)S(1)}, u32[]{:S(2)}, u32[]{:S(2)}) %collective-permute-start.4) | collective-permute-done | bytes 221216 | tf_op jit(solution)/shard_map/ppermute | solution.py:497
  21.9 5.9 %shard_map.137 = (f32[128,256]{1,0:T(8,128)S(1)}, f32[2,128,8]{2,1,0:T(8,128)S(1)}, bf16[2,5,128,128]{3,2,1,0:T(8,128)(2,1)S(1)}, bf16[2,4,128,128]{3,2,1,0:T(8,...) custom-call(f32[2,128,256]{2,1,0:T(8,128)S(1)} %get-tuple-element.50, ...), custom_call_target="tpu_custom_call" | custom-call | flops 2516582400 | bytes 3023872 | tf_op jit(solution)/shard_map/pallas_call | solution.py:478
  27.9 14.6 %all_to_all.10.sums_ref = f32[8,1,256]{2,1,0:T(1,128)S(1)} all-to-all(f32[8,1,256]{2,1,0:T(1,128)S(1)} %get-tuple-element.55), channel_id=1, replica_groups=mesh['ctx'=64,'head'=8] {'head'}, dimensions={0} | all-to-all | bytes 16384 | tf_op jit(solution)/shard_map/all_to_all | solution.py:506
  42.5 1.5 %shard_map.138 = (bf16[128,256]{1,0:T(8,128)(2,1)}, f32[64,1,256]{2,1,0:T(1,128)}, bf16[128,256]{1,0:T(8,128)(2,1)S(1)}, f32[2,128,8]{2,1,0:T(8,128)S(1)}, bf16[...) custom-call(f32[8,1,256]{2,1,0:T(1,128)S(1)} %all_to_all.10.sums_ref, ...), custom_call_target="tpu_custom_call" | custom-call | flops 125829120 | bytes 2188288 | tf_op jit(solution)/shard_map/pallas_call | solution.py:478
  44.0 1.9 %collective-permute-start.5 = (bf16[128,768]{1,0:T(8,128)(2,1)S(1)}, bf16[128,768]{1,0:T(8,128)(2,1)S(1)}, u32[]{:S(2)}, u32[]{:S(2)}) collective-permute-start(bf16[128,768]{1,0:T(8,128)(2,1)S(1)} %get-tuple-element.64), channel_id=1, source_target_pairs={{24,0},{32,8},{40,16},{48,24},{56,32},{64,40},{72,48},{80,56},{88,... | collective-permute-start | bytes 589832 | tf_op jit(solution)/shard_map/ppermute | solution.py:492
  45.9 2.4 %collective-permute-start.6 = (bf16[128,512]{1,0:T(8,128)(2,1)S(1)}, bf16[128,512]{1,0:T(8,128)(2,1)S(1)}, u32[]{:S(2)}, u32[]{:S(2)}) collective-permute-start(bf16[128,512]{1,0:T(8,128)(2,1)S(1)} %get-tuple-element.65), channel_id=1, source_target_pairs={{32,0},{40,8},{48,16},{56,24},{64,32},{72,40},{80,48},{88,56},{96,... | collective-permute-start | bytes 393224 | tf_op jit(solution)/shard_map/ppermute | solution.py:492
  48.2 18.7 %all-to-all-start.1 = ((f32[64,1,256]{2,1,0:T(1,128)}), f32[64,1,256]{2,1,0:T(1,128)S(1)}, u32[]{:S(2)}, u32[]{:S(2)}) async-start(f32[64,1,256]{2,1,0:T(1,128)} %get-tuple-element.70), calls=%async_computation.1 | async-start | bytes 131072 | tf_op jit(solution)/shard_map/all_to_all | solution.py:506
  67.0 0.9 %shard_map.139 = (bf16[2,128,256]{2,1,0:T(8,128)(2,1)S(1)}, f32[128,256]{1,0:T(8,128)S(1)}, bf16[128,768]{1,0:T(8,128)(2,1)S(1)}, bf16[128,768]{1,0:T(8,128)(2,1)S(1)}) custom-call(bf16[128,256]{1,0:T(8,128)(2,1)S(1)} %get-tuple-element.66.scaled_ref, f32[2,128,8]{2,1,0:T(8,128)S(1)} %get-tuple-element.67.delta_ref, ...), custom_call_target="tpu_custom_call" | custom-call | flops 25165824000 | bytes 2236416 | tf_op jit(solution)/shard_map/pallas_call | solution.py:478
  67.9 2.5 %collective-permute-start.7 = (bf16[128,768]{1,0:T(8,128)(2,1)S(1)}, bf16[128,768]{1,0:T(8,128)(2,1)S(1)}, u32[]{:S(2)}, u32[]{:S(2)}) collective-permute-start(bf16[128,768]{1,0:T(8,128)(2,1)S(1)} %get-tuple-element.74), channel_id=1, source_target_pairs={{8,0},{16,8},{24,16},{32,24},{40,32},{48,40},{56,48},{64,56},{72,6... | collective-permute-start | bytes 589832 | tf_op jit(solution)/shard_map/ppermute | solution.py:492
  70.4 2.5 %collective-permute-start.8 = (bf16[128,768]{1,0:T(8,128)(2,1)S(1)}, bf16[128,768]{1,0:T(8,128)(2,1)S(1)}, u32[]{:S(2)}, u32[]{:S(2)}) collective-permute-start(bf16[128,768]{1,0:T(8,128)(2,1)S(1)} %get-tuple-element.75), channel_id=1, source_target_pairs={{16,0},{24,8},{32,16},{40,24},{48,32},{56,40},{64,48},{72,56},{80,... | collective-permute-start | bytes 589832 | tf_op jit(solution)/shard_map/ppermute | solution.py:492
  72.9 2.1 %all-to-all-done.1.parts_ref = f32[64,1,256]{2,1,0:T(1,128)S(1)} async-done(((f32[64,1,256]{2,1,0:T(1,128)}), f32[64,1,256]{2,1,0:T(1,128)S(1)}, u32[]{:S(2)}, u32[]{:S(2)}) %all-to-all-start.1) | async-done | bytes 65568 | tf_op jit(solution)/shard_map/all_to_all | solution.py:506
  75.0 1.2 %shard_map.140 = (bf16[128,256]{1,0:T(8,128)(2,1)}, f32[2,128,128]{2,1,0:T(8,128)S(1)}, f32[2,128,128]{2,1,0:T(8,128)S(1)}, f32[2,128,256]{2,1,0:T(8,128)S(1)}) custom-call(bf16[2,128,256]{2,1,0:T(8,128)(2,1)S(1)} %get-tuple-element.71.own_ref, bf16[2,128,256]{2,1,0:T(8,128)(2,1)S(1)} %get-tuple-element.72.kw_ref, bf16[128,256]{1,0:T(8,128)(2,1)S(1)} %copy-done.6, ...), custom_call_target="tpu_custom_call" | custom-call | flops 1258291200 | bytes 1048576 | tf_op jit(solution)/shard_map/pallas_call | solution.py:478
  76.2 5.3 %collective-permute-done.8.recv2_ref = bf16[128,768]{1,0:T(8,128)(2,1)S(1)} collective-permute-done((bf16[128,768]{1,0:T(8,128)(2,1)S(1)}, bf16[128,768]{1,0:T(8,128)(2,1)S(1)}, u32[]{:S(2)}, u32[]{:S(2)}) %collective-permute-start.8) | collective-permute-done | bytes 196640 | tf_op jit(solution)/shard_map/ppermute | solution.py:492
  81.5 2.0 %shard_map.141 = (bf16[128,256]{1,0:T(8,128)(2,1)}, bf16[128,256]{1,0:T(8,128)(2,1)}, bf16[128,256]{1,0:T(8,128)(2,1)}, f32[2,128]{1,0:T(2,128)}, f32[1,256]{1,0:T(1,128)}) custom-call(bf16[128,768]{1,0:T(8,128)(2,1)S(1)} %collective-permute-done.7.recv1_ref, bf16[128,768]{1,0:T(8,128)(2,1)S(1)} %collective-permute-done.8.recv2_ref, ...), custom_call_target="tpu_custom_call" | custom-call | flops 167772160 | bytes 1969152 | tf_op jit(solution)/shard_map/pallas_call | solution.py:478
  (21 shorter events, 0.0 us)
Async XLA Ops:
  0.6 12.2 %copy-start.1 = (bf16[128,256]{1,0:T(8,128)(2,1)S(1)}, bf16[128,256]{1,0:T(8,128)(2,1)}, u32[]{:S(2)}) copy-start(bf16[128,256]{1,0:T(8,128)(2,1)} %dir_ref.7) | copy-start | bytes 196612
  0.6 12.2 %copy-start = (bf16[128,256]{1,0:T(8,128)(2,1)S(1)}, bf16[128,256]{1,0:T(8,128)(2,1)}, u32[]{:S(2)}) copy-start(bf16[128,256]{1,0:T(8,128)(2,1)} %key_ref.6) | copy-start | bytes 196612
  0.7 12.2 %copy-start.4 = (f32[2,128]{1,0:T(2,128)S(1)}, f32[2,128]{1,0:T(2,128)}, u32[]{:S(2)}) copy-start(f32[2,128]{1,0:T(2,128)} %rate_ref.5) | copy-start | bytes 3076
  0.7 12.2 %copy-start.6 = (bf16[128,256]{1,0:T(8,128)(2,1)S(1)}, bf16[128,256]{1,0:T(8,128)(2,1)}, u32[]{:S(2)}) copy-start(bf16[128,256]{1,0:T(8,128)(2,1)} %query_ref.3) | copy-start | bytes 196612
  2.4 19.5 %copy-start.2 = (bf16[128,256]{1,0:T(8,128)(2,1)S(1)}, bf16[128,256]{1,0:T(8,128)(2,1)}, u32[]{:S(2)}) copy-start(bf16[128,256]{1,0:T(8,128)(2,1)} %cot_ref.3) | copy-start | bytes 196612
  2.4 19.5 %copy-start.3 = (bf16[128,256]{1,0:T(8,128)(2,1)S(1)}, bf16[128,256]{1,0:T(8,128)(2,1)}, u32[]{:S(2)}) copy-start(bf16[128,256]{1,0:T(8,128)(2,1)} %value_ref.5) | copy-start | bytes 196612
  2.4 10.4 %collective-permute-start.1 = (bf16[144,768]{1,0:T(8,128)(2,1)}, bf16[144,768]{1,0:T(8,128)(2,1)S(1)}, u32[]{:S(2)}, u32[]{:S(2)}) collective-permute-start(bf16[144,768]{1,0:T(8,128)(2,1)} %shard_map.135), channel_id=1, source_target_pairs={{0,8},{16,24},{32,40},{48,56},{64,72},{80,88},{96,104},{112,120},{... | collective-permute-start | bytes 663560 | tf_op jit(solution)/shard_map/ppermute | solution.py:497
  4.3 10.8 %collective-permute-start = (bf16[144,768]{1,0:T(8,128)(2,1)}, bf16[144,768]{1,0:T(8,128)(2,1)S(1)}, u32[]{:S(2)}, u32[]{:S(2)}) collective-permute-start(bf16[144,768]{1,0:T(8,128)(2,1)} %shard_map.135), channel_id=1, source_target_pairs={{0,16},{8,24},{16,32},{24,40},{32,48},{40,56},{48,64},{56,72},{64,... | collective-permute-start | bytes 663560 | tf_op jit(solution)/shard_map/ppermute | solution.py:492
  8.5 10.0 %collective-permute-start.3 = (bf16[144,768]{1,0:T(8,128)(2,1)}, bf16[144,768]{1,0:T(8,128)(2,1)S(1)}, u32[]{:S(2)}, u32[]{:S(2)}) collective-permute-start(bf16[144,768]{1,0:T(8,128)(2,1)} %shard_map.135), channel_id=1, source_target_pairs={{0,32},{8,40},{16,48},{24,56},{32,64},{40,72},{48,80},{56,88},{64,... | collective-permute-start | bytes 663560 | tf_op jit(solution)/shard_map/ppermute | solution.py:492
  15.1 3.4 %collective-permute-start.2 = (bf16[144,768]{1,0:T(8,128)(2,1)S(1)}, bf16[144,768]{1,0:T(8,128)(2,1)S(1)}, u32[]{:S(2)}, u32[]{:S(2)}) collective-permute-start(bf16[144,768]{1,0:T(8,128)(2,1)S(1)} %collective-permute-done.halo2_ref), channel_id=1, source_target_pairs={{0,8},{8,0},{16,24},{24,16},{32,40},{40,32},{48,56},{56,48},{64,72... | collective-permute-start | bytes 663560 | tf_op jit(solution)/shard_map/ppermute | solution.py:502
  18.5 3.4 %collective-permute-start.4 = (bf16[144,768]{1,0:T(8,128)(2,1)S(1)}, bf16[144,768]{1,0:T(8,128)(2,1)S(1)}, u32[]{:S(2)}, u32[]{:S(2)}) collective-permute-start(bf16[144,768]{1,0:T(8,128)(2,1)S(1)} %collective-permute-done.3.halo4_ref), channel_id=1, source_target_pairs={{8,0},{24,16},{40,32},{56,48},{72,64},{88,80},{104,96},{120,112},{... | collective-permute-start | bytes 663560 | tf_op jit(solution)/shard_map/ppermute | solution.py:497
  19.9 2.0 %copy-start.5 = (f32[256]{0:T(256)S(1)}, f32[256]{0:T(256)}, u32[]{:S(2)}) copy-start(f32[256]{0:T(256)} %param.13) | copy-start | bytes 3076
  19.9 2.0 %copy-start.7 = (s32[32]{0:T(128)S(1)}, s32[32]{0:T(128)}, u32[]{:S(2)}) copy-start(s32[32]{0:T(128)} %len_ref.1) | copy-start | bytes 388
  44.0 23.0 %collective-permute-start.5 = (bf16[128,768]{1,0:T(8,128)(2,1)S(1)}, bf16[128,768]{1,0:T(8,128)(2,1)S(1)}, u32[]{:S(2)}, u32[]{:S(2)}) collective-permute-start(bf16[128,768]{1,0:T(8,128)(2,1)S(1)} %get-tuple-element.64), channel_id=1, source_target_pairs={{24,0},{32,8},{40,16},{48,24},{56,32},{64,40},{72,48},{80,56},{88,... | collective-permute-start | bytes 589832 | tf_op jit(solution)/shard_map/ppermute | solution.py:492
  45.9 21.1 %collective-permute-start.6 = (bf16[128,512]{1,0:T(8,128)(2,1)S(1)}, bf16[128,512]{1,0:T(8,128)(2,1)S(1)}, u32[]{:S(2)}, u32[]{:S(2)}) collective-permute-start(bf16[128,512]{1,0:T(8,128)(2,1)S(1)} %get-tuple-element.65), channel_id=1, source_target_pairs={{32,0},{40,8},{48,16},{56,24},{64,32},{72,40},{80,48},{88,56},{96,... | collective-permute-start | bytes 393224 | tf_op jit(solution)/shard_map/ppermute | solution.py:492
  48.2 26.8 %all-to-all-start.1 = ((f32[64,1,256]{2,1,0:T(1,128)}), f32[64,1,256]{2,1,0:T(1,128)S(1)}, u32[]{:S(2)}, u32[]{:S(2)}) async-start(f32[64,1,256]{2,1,0:T(1,128)} %get-tuple-element.70), calls=%async_computation.1 | async-start | bytes 131072 | tf_op jit(solution)/shard_map/all_to_all | solution.py:506
  67.9 8.4 %collective-permute-start.7 = (bf16[128,768]{1,0:T(8,128)(2,1)S(1)}, bf16[128,768]{1,0:T(8,128)(2,1)S(1)}, u32[]{:S(2)}, u32[]{:S(2)}) collective-permute-start(bf16[128,768]{1,0:T(8,128)(2,1)S(1)} %get-tuple-element.74), channel_id=1, source_target_pairs={{8,0},{16,8},{24,16},{32,24},{40,32},{48,40},{56,48},{64,56},{72,6... | collective-permute-start | bytes 589832 | tf_op jit(solution)/shard_map/ppermute | solution.py:492
  70.4 11.1 %collective-permute-start.8 = (bf16[128,768]{1,0:T(8,128)(2,1)S(1)}, bf16[128,768]{1,0:T(8,128)(2,1)S(1)}, u32[]{:S(2)}, u32[]{:S(2)}) collective-permute-start(bf16[128,768]{1,0:T(8,128)(2,1)S(1)} %get-tuple-element.75), channel_id=1, source_target_pairs={{16,0},{24,8},{32,16},{40,24},{48,32},{56,40},{64,48},{72,56},{80,... | collective-permute-start | bytes 589832 | tf_op jit(solution)/shard_map/ppermute | solution.py:492

commit v6 on v5

--- a/solution.py
+++ b/solution.py
@@ -516,19 +516,18 @@
     unit_flops = 2 * size * size * DH
     packed = pack(keys, dirs, values, rates)
     halo2 = passed_along(packed, 2)
-    halo4 = passed_along(packed, 4)
     even = paired(packed, 0, 1)
-    even, own_keys = lax.optimization_barrier((even, keys))
     inverse, coef, raw = call(
         own_kernel,
         [((heads, size, size), BF16), ((heads, size, 2 * DH), BF16), ((heads, size, 2 * DH), F32)],
         heads * 60 * unit_flops,
         query,
-        own_keys,
+        keys,
         dirs,
         rates,
     )
     halo2, raw = lax.optimization_barrier((halo2, raw))
+    halo4 = passed_along(halo2, 2)
     cross2 = swapped(halo2)
     cross2, halo4 = lax.optimization_barrier((cross2, halo4))
     halos = (halo2, halo4, even, cross2, paired(halo4, 1, -1))

time: 84 us -> 87.8 us (1.045)
  starting transfers between devices: 41.6 us -> 44.1 us
  waiting for transfers between devices: 10.9 us -> 12.2 us
    ppermute x6, starting transfers between devices: 17.8 us -> 19.4 us  [passed_along(): lax.ppermute(value, 'ctx', [(source, source + steps) for source in range(...]
    ppermute x6, waiting for transfers between devices: 6.79 us -> 8.11 us  [passed_along(): lax.ppermute(value, 'ctx', [(source, source + steps) for source in range(...]
where the time goes in v6:
time: 87.8 us; the launch traced here: 87.4 us
  starting transfers between devices  44.1 us (50%)
  Pallas kernels  15.5 us (18%)
  blocking collectives  14.6 us (17%)
  waiting for transfers between devices  12.2 us (14%)
  between operations  0.89 us (1%)
    ppermute x6, starting transfers between devices, passed_along(): lax.ppermute(value, 'ctx', [(source, source + steps) for source in range(...  19.4 us
    all_to_all x1, starting transfers between devices, gathered(): lax.all_to_all(value, axis, 0, 0, axis_index_groups=groups, tiled=True)  19 us
    all_to_all x1, blocking collectives, gathered(): lax.all_to_all(value, axis, 0, 0, axis_index_groups=groups, tiled=True)  14.6 us
    pallas_call x6, Pallas kernels, call(): pl.pallas_call(body, out_shape=[jax.ShapeDtypeStruct(s, d) for s, d in ou...  13.8 us
    ppermute x6, waiting for transfers between devices, passed_along(): lax.ppermute(value, 'ctx', [(source, source + steps) for source in range(...  8.11 us
    ppermute x2, starting transfers between devices, paired(): lax.ppermute(value, 'ctx', [(source, source + step) for source in range(f...  3.71 us
    all_to_all x1, waiting for transfers between devices, gathered(): lax.all_to_all(value, axis, 0, 0, axis_index_groups=groups, tiled=True)  2.12 us
    ppermute x2, waiting for transfers between devices, paired(): lax.ppermute(value, 'ctx', [(source, source + step) for source in range(f...  1.99 us
  transfers between devices with their start and end apart: 10, of which 4 were waited for; matrix products, arithmetic and copies ran while one was open for 0% of the time, Pallas kernels for 5%

profile of v6, /device:TPU:6, one launch (start us, length us, event | category | flops | bytes accessed | tf_op | source)
XLA Modules:
  0.0 87.4 jit_solution(15546073015856400503)
XLA Ops:
  0.7 1.7 %shard_map.135 = bf16[144,768]{1,0:T(8,128)(2,1)} custom-call(bf16[128,256]{1,0:T(8,128)(2,1)} %key_ref.7, bf16[128,256]{1,0:T(8,128)(2,1)} %dir_ref.7, bf16[128,256]{1,0:T(8,128)(2,1)} %value_ref.5, f32[2,128]{1,0:T(2,128)} %rate_ref.5), custom_call_target="tpu_custom_call" | custom-call | tf_op jit(solution)/shard_map/pallas_call | solution.py:138
  2.4 0.0 copy-start.3
  2.4 4.3 %collective-permute-start = (bf16[144,768]{1,0:T(8,128)(2,1)}, bf16[144,768]{1,0:T(8,128)(2,1)S(1)}, u32[]{:S(2)}, u32[]{:S(2)}) collective-permute-start(bf16[144,768]{1,0:T(8,128)(2,1)} %shard_map.135), channel_id=1, source_target_pairs={{0,16},{8,24},{16,32},{24,40},{32,48},{40,56},{48,64},{56,72},{64,... | collective-permute-start | bytes 663560 | tf_op jit(solution)/shard_map/ppermute | solution.py:492
  6.8 2.2 %shard_map.136 = (bf16[2,128,128]{2,1,0:T(8,128)(2,1)S(1)}, bf16[2,128,256]{2,1,0:T(8,128)(2,1)S(1)}, f32[2,128,256]{2,1,0:T(8,128)S(1)}) custom-call(bf16[128,256]{1,0:T(8,128)(2,1)S(1)} %copy-done.6, bf16[128,256]{1,0:T(8,128)(2,1)S(1)} %copy-done, bf16[128,256]{1,0:T(8,128)(2,1)S(1)} %copy-done.1, f32[2,128]{1,0:T(2,128)S(1)} %copy-done.4), custom_call_target="tpu_custom_call" | custom-call | flops 503316480 | bytes 656384 | tf_op jit(solution)/shard_map/pallas_call | solution.py:478
  9.0 2.8 %collective-permute-done.halo2_ref = bf16[144,768]{1,0:T(8,128)(2,1)S(1)} collective-permute-done((bf16[144,768]{1,0:T(8,128)(2,1)}, bf16[144,768]{1,0:T(8,128)(2,1)S(1)}, u32[]{:S(2)}, u32[]{:S(2)}) %collective-permute-start) | collective-permute-done | bytes 221216 | tf_op jit(solution)/shard_map/ppermute | solution.py:492
  11.8 6.3 %collective-permute-start.2 = (bf16[144,768]{1,0:T(8,128)(2,1)S(1)}, bf16[144,768]{1,0:T(8,128)(2,1)S(1)}, u32[]{:S(2)}, u32[]{:S(2)}) collective-permute-start(bf16[144,768]{1,0:T(8,128)(2,1)S(1)} %collective-permute-done.halo2_ref), channel_id=1, source_target_pairs={{0,16},{8,24},{16,32},{24,40},{32,48},{40,56},{48,64},{56,72},{64,... | collective-permute-start | bytes 663560 | tf_op jit(solution)/shard_map/ppermute | solution.py:492
  18.1 1.9 %collective-permute-start.1 = (bf16[144,768]{1,0:T(8,128)(2,1)S(1)}, bf16[144,768]{1,0:T(8,128)(2,1)S(1)}, u32[]{:S(2)}, u32[]{:S(2)}) collective-permute-start(bf16[144,768]{1,0:T(8,128)(2,1)S(1)} %collective-permute-done.halo2_ref), channel_id=1, source_target_pairs={{0,8},{8,0},{16,24},{24,16},{32,40},{40,32},{48,56},{56,48},{64,72... | collective-permute-start | bytes 663560 | tf_op jit(solution)/shard_map/ppermute | solution.py:502
  20.1 2.4 %collective-permute-start.3 = (bf16[144,768]{1,0:T(8,128)(2,1)S(1)}, bf16[144,768]{1,0:T(8,128)(2,1)S(1)}, u32[]{:S(2)}, u32[]{:S(2)}) collective-permute-start(bf16[144,768]{1,0:T(8,128)(2,1)S(1)} %copy-done.8), channel_id=1, source_target_pairs={{0,8},{16,24},{32,40},{48,56},{64,72},{80,88},{96,104},{112,120},{... | collective-permute-start | bytes 663560 | tf_op jit(solution)/shard_map/ppermute | solution.py:497
  22.5 1.3 %collective-permute-start.4 = (bf16[144,768]{1,0:T(8,128)(2,1)S(1)}, bf16[144,768]{1,0:T(8,128)(2,1)S(1)}, u32[]{:S(2)}, u32[]{:S(2)}) collective-permute-start(bf16[144,768]{1,0:T(8,128)(2,1)S(1)} %collective-permute-done.2.halo4_ref), channel_id=1, source_target_pairs={{8,0},{24,16},{40,32},{56,48},{72,64},{88,80},{104,96},{120,112},{... | collective-permute-start | bytes 663560 | tf_op jit(solution)/shard_map/ppermute | solution.py:497
  23.8 0.1 pad_add_fusion.place_ref
  23.9 2.0 %collective-permute-done.4.cross4_ref = bf16[144,768]{1,0:T(8,128)(2,1)S(1)} collective-permute-done((bf16[144,768]{1,0:T(8,128)(2,1)S(1)}, bf16[144,768]{1,0:T(8,128)(2,1)S(1)}, u32[]{:S(2)}, u32[]{:S(2)}) %collective-permute-start.4) | collective-permute-done | bytes 221216 | tf_op jit(solution)/shard_map/ppermute | solution.py:497
  25.9 5.9 %shard_map.137 = (f32[128,256]{1,0:T(8,128)S(1)}, f32[2,128,8]{2,1,0:T(8,128)S(1)}, bf16[2,5,128,128]{3,2,1,0:T(8,128)(2,1)S(1)}, bf16[2,4,128,128]{3,2,1,0:T(8,...) custom-call(f32[2,128,256]{2,1,0:T(8,128)S(1)} %get-tuple-element.47, ...), custom_call_target="tpu_custom_call" | custom-call | flops 2516582400 | bytes 3023872 | tf_op jit(solution)/shard_map/pallas_call | solution.py:478
  31.8 14.6 %all_to_all.10.sums_ref = f32[8,1,256]{2,1,0:T(1,128)S(1)} all-to-all(f32[8,1,256]{2,1,0:T(1,128)S(1)} %get-tuple-element.51), channel_id=1, replica_groups=mesh['ctx'=64,'head'=8] {'head'}, dimensions={0} | all-to-all | bytes 16384 | tf_op jit(solution)/shard_map/all_to_all | solution.py:506
  46.5 1.5 %shard_map.138 = (bf16[128,256]{1,0:T(8,128)(2,1)}, f32[64,1,256]{2,1,0:T(1,128)}, bf16[128,256]{1,0:T(8,128)(2,1)S(1)}, f32[2,128,8]{2,1,0:T(8,128)S(1)}, bf16[...) custom-call(f32[8,1,256]{2,1,0:T(1,128)S(1)} %all_to_all.10.sums_ref, ...), custom_call_target="tpu_custom_call" | custom-call | flops 125829120 | bytes 2188288 | tf_op jit(solution)/shard_map/pallas_call | solution.py:478
  47.9 1.9 %collective-permute-start.5 = (bf16[128,768]{1,0:T(8,128)(2,1)S(1)}, bf16[128,768]{1,0:T(8,128)(2,1)S(1)}, u32[]{:S(2)}, u32[]{:S(2)}) collective-permute-start(bf16[128,768]{1,0:T(8,128)(2,1)S(1)} %get-tuple-element.60), channel_id=1, source_target_pairs={{24,0},{32,8},{40,16},{48,24},{56,32},{64,40},{72,48},{80,56},{88,... | collective-permute-start | bytes 589832 | tf_op jit(solution)/shard_map/ppermute | solution.py:492
  49.9 1.9 %collective-permute-start.6 = (bf16[128,512]{1,0:T(8,128)(2,1)S(1)}, bf16[128,512]{1,0:T(8,128)(2,1)S(1)}, u32[]{:S(2)}, u32[]{:S(2)}) collective-permute-start(bf16[128,512]{1,0:T(8,128)(2,1)S(1)} %get-tuple-element.61), channel_id=1, source_target_pairs={{32,0},{40,8},{48,16},{56,24},{64,32},{72,40},{80,48},{88,56},{96,... | collective-permute-start | bytes 393224 | tf_op jit(solution)/shard_map/ppermute | solution.py:492
  51.8 19.0 %all-to-all-start.1 = ((f32[64,1,256]{2,1,0:T(1,128)}), f32[64,1,256]{2,1,0:T(1,128)S(1)}, u32[]{:S(2)}, u32[]{:S(2)}) async-start(f32[64,1,256]{2,1,0:T(1,128)} %get-tuple-element.66), calls=%async_computation.1 | async-start | bytes 131072 | tf_op jit(solution)/shard_map/all_to_all | solution.py:506
  70.8 0.9 %shard_map.139 = (bf16[2,128,256]{2,1,0:T(8,128)(2,1)S(1)}, f32[128,256]{1,0:T(8,128)S(1)}, bf16[128,768]{1,0:T(8,128)(2,1)S(1)}, bf16[128,768]{1,0:T(8,128)(2,1)S(1)}) custom-call(bf16[128,256]{1,0:T(8,128)(2,1)S(1)} %get-tuple-element.62.scaled_ref, f32[2,128,8]{2,1,0:T(8,128)S(1)} %get-tuple-element.63.delta_ref, ...), custom_call_target="tpu_custom_call" | custom-call | flops 25165824000 | bytes 2236416 | tf_op jit(solution)/shard_map/pallas_call | solution.py:478
  71.7 2.5 %collective-permute-start.7 = (bf16[128,768]{1,0:T(8,128)(2,1)S(1)}, bf16[128,768]{1,0:T(8,128)(2,1)S(1)}, u32[]{:S(2)}, u32[]{:S(2)}) collective-permute-start(bf16[128,768]{1,0:T(8,128)(2,1)S(1)} %get-tuple-element.70), channel_id=1, source_target_pairs={{8,0},{16,8},{24,16},{32,24},{40,32},{48,40},{56,48},{64,56},{72,6... | collective-permute-start | bytes 589832 | tf_op jit(solution)/shard_map/ppermute | solution.py:492
  74.2 2.5 %collective-permute-start.8 = (bf16[128,768]{1,0:T(8,128)(2,1)S(1)}, bf16[128,768]{1,0:T(8,128)(2,1)S(1)}, u32[]{:S(2)}, u32[]{:S(2)}) collective-permute-start(bf16[128,768]{1,0:T(8,128)(2,1)S(1)} %get-tuple-element.71), channel_id=1, source_target_pairs={{16,0},{24,8},{32,16},{40,24},{48,32},{56,40},{64,48},{72,56},{80,... | collective-permute-start | bytes 589832 | tf_op jit(solution)/shard_map/ppermute | solution.py:492
  76.7 2.1 %all-to-all-done.1.parts_ref = f32[64,1,256]{2,1,0:T(1,128)S(1)} async-done(((f32[64,1,256]{2,1,0:T(1,128)}), f32[64,1,256]{2,1,0:T(1,128)S(1)}, u32[]{:S(2)}, u32[]{:S(2)}) %all-to-all-start.1) | async-done | bytes 65568 | tf_op jit(solution)/shard_map/all_to_all | solution.py:506
  78.8 1.2 %shard_map.140 = (bf16[128,256]{1,0:T(8,128)(2,1)}, f32[2,128,128]{2,1,0:T(8,128)S(1)}, f32[2,128,128]{2,1,0:T(8,128)S(1)}, f32[2,128,256]{2,1,0:T(8,128)S(1)}) custom-call(bf16[2,128,256]{2,1,0:T(8,128)(2,1)S(1)} %get-tuple-element.67.own_ref, bf16[2,128,256]{2,1,0:T(8,128)(2,1)S(1)} %get-tuple-element.68.kw_ref, bf16[128,256]{1,0:T(8,128)(2,1)S(1)} %copy-done.6, ...), custom_call_target="tpu_custom_call" | custom-call | flops 1258291200 | bytes 1048576 | tf_op jit(solution)/shard_map/pallas_call | solution.py:478
  80.1 5.3 %collective-permute-done.8.recv2_ref = bf16[128,768]{1,0:T(8,128)(2,1)S(1)} collective-permute-done((bf16[128,768]{1,0:T(8,128)(2,1)S(1)}, bf16[128,768]{1,0:T(8,128)(2,1)S(1)}, u32[]{:S(2)}, u32[]{:S(2)}) %collective-permute-start.8) | collective-permute-done | bytes 196640 | tf_op jit(solution)/shard_map/ppermute | solution.py:492
  85.4 2.0 %shard_map.141 = (bf16[128,256]{1,0:T(8,128)(2,1)}, bf16[128,256]{1,0:T(8,128)(2,1)}, bf16[128,256]{1,0:T(8,128)(2,1)}, f32[2,128]{1,0:T(2,128)}, f32[1,256]{1,0:T(1,128)}) custom-call(bf16[128,768]{1,0:T(8,128)(2,1)S(1)} %collective-permute-done.7.recv1_ref, bf16[128,768]{1,0:T(8,128)(2,1)S(1)} %collective-permute-done.8.recv2_ref, ...), custom_call_target="tpu_custom_call" | custom-call | flops 167772160 | bytes 1969152 | tf_op jit(solution)/shard_map/pallas_call | solution.py:478
  (23 shorter events, 0.1 us)
Async XLA Ops:
  0.6 6.1 %copy-start.1 = (bf16[128,256]{1,0:T(8,128)(2,1)S(1)}, bf16[128,256]{1,0:T(8,128)(2,1)}, u32[]{:S(2)}) copy-start(bf16[128,256]{1,0:T(8,128)(2,1)} %dir_ref.7) | copy-start | bytes 196612
  0.6 6.1 %copy-start = (bf16[128,256]{1,0:T(8,128)(2,1)S(1)}, bf16[128,256]{1,0:T(8,128)(2,1)}, u32[]{:S(2)}) copy-start(bf16[128,256]{1,0:T(8,128)(2,1)} %key_ref.7) | copy-start | bytes 196612
  0.7 6.1 %copy-start.4 = (f32[2,128]{1,0:T(2,128)S(1)}, f32[2,128]{1,0:T(2,128)}, u32[]{:S(2)}) copy-start(f32[2,128]{1,0:T(2,128)} %rate_ref.5) | copy-start | bytes 3076
  0.7 6.1 %copy-start.6 = (bf16[128,256]{1,0:T(8,128)(2,1)S(1)}, bf16[128,256]{1,0:T(8,128)(2,1)}, u32[]{:S(2)}) copy-start(bf16[128,256]{1,0:T(8,128)(2,1)} %query_ref.3) | copy-start | bytes 196612
  2.4 17.7 %copy-start.8 = (bf16[144,768]{1,0:T(8,128)(2,1)S(1)}, bf16[144,768]{1,0:T(8,128)(2,1)}, u32[]{:S(2)}) copy-start(bf16[144,768]{1,0:T(8,128)(2,1)} %shard_map.135) | copy-start | bytes 663556
  2.4 23.5 %copy-start.2 = (bf16[128,256]{1,0:T(8,128)(2,1)S(1)}, bf16[128,256]{1,0:T(8,128)(2,1)}, u32[]{:S(2)}) copy-start(bf16[128,256]{1,0:T(8,128)(2,1)} %cot_ref.3) | copy-start | bytes 196612
  2.4 23.5 %copy-start.3 = (bf16[128,256]{1,0:T(8,128)(2,1)S(1)}, bf16[128,256]{1,0:T(8,128)(2,1)}, u32[]{:S(2)}) copy-start(bf16[128,256]{1,0:T(8,128)(2,1)} %value_ref.5) | copy-start | bytes 196612
  2.4 9.4 %collective-permute-start = (bf16[144,768]{1,0:T(8,128)(2,1)}, bf16[144,768]{1,0:T(8,128)(2,1)S(1)}, u32[]{:S(2)}, u32[]{:S(2)}) collective-permute-start(bf16[144,768]{1,0:T(8,128)(2,1)} %shard_map.135), channel_id=1, source_target_pairs={{0,16},{8,24},{16,32},{24,40},{32,48},{40,56},{48,64},{56,72},{64,... | collective-permute-start | bytes 663560 | tf_op jit(solution)/shard_map/ppermute | solution.py:492
  11.8 10.7 %collective-permute-start.2 = (bf16[144,768]{1,0:T(8,128)(2,1)S(1)}, bf16[144,768]{1,0:T(8,128)(2,1)S(1)}, u32[]{:S(2)}, u32[]{:S(2)}) collective-permute-start(bf16[144,768]{1,0:T(8,128)(2,1)S(1)} %collective-permute-done.halo2_ref), channel_id=1, source_target_pairs={{0,16},{8,24},{16,32},{24,40},{32,48},{40,56},{48,64},{56,72},{64,... | collective-permute-start | bytes 663560 | tf_op jit(solution)/shard_map/ppermute | solution.py:492
  18.1 4.4 %collective-permute-start.1 = (bf16[144,768]{1,0:T(8,128)(2,1)S(1)}, bf16[144,768]{1,0:T(8,128)(2,1)S(1)}, u32[]{:S(2)}, u32[]{:S(2)}) collective-permute-start(bf16[144,768]{1,0:T(8,128)(2,1)S(1)} %collective-permute-done.halo2_ref), channel_id=1, source_target_pairs={{0,8},{8,0},{16,24},{24,16},{32,40},{40,32},{48,56},{56,48},{64,72... | collective-permute-start | bytes 663560 | tf_op jit(solution)/shard_map/ppermute | solution.py:502
  20.1 3.8 %collective-permute-start.3 = (bf16[144,768]{1,0:T(8,128)(2,1)S(1)}, bf16[144,768]{1,0:T(8,128)(2,1)S(1)}, u32[]{:S(2)}, u32[]{:S(2)}) collective-permute-start(bf16[144,768]{1,0:T(8,128)(2,1)S(1)} %copy-done.8), channel_id=1, source_target_pairs={{0,8},{16,24},{32,40},{48,56},{64,72},{80,88},{96,104},{112,120},{... | collective-permute-start | bytes 663560 | tf_op jit(solution)/shard_map/ppermute | solution.py:497
  22.5 3.4 %collective-permute-start.4 = (bf16[144,768]{1,0:T(8,128)(2,1)S(1)}, bf16[144,768]{1,0:T(8,128)(2,1)S(1)}, u32[]{:S(2)}, u32[]{:S(2)}) collective-permute-start(bf16[144,768]{1,0:T(8,128)(2,1)S(1)} %collective-permute-done.2.halo4_ref), channel_id=1, source_target_pairs={{8,0},{24,16},{40,32},{56,48},{72,64},{88,80},{104,96},{120,112},{... | collective-permute-start | bytes 663560 | tf_op jit(solution)/shard_map/ppermute | solution.py:497
  23.9 2.0 %copy-start.5 = (f32[256]{0:T(256)S(1)}, f32[256]{0:T(256)}, u32[]{:S(2)}) copy-start(f32[256]{0:T(256)} %param.13) | copy-start | bytes 3076
  23.9 2.0 %copy-start.7 = (s32[32]{0:T(128)S(1)}, s32[32]{0:T(128)}, u32[]{:S(2)}) copy-start(s32[32]{0:T(128)} %len_ref.1) | copy-start | bytes 388
  47.9 22.9 %collective-permute-start.5 = (bf16[128,768]{1,0:T(8,128)(2,1)S(1)}, bf16[128,768]{1,0:T(8,128)(2,1)S(1)}, u32[]{:S(2)}, u32[]{:S(2)}) collective-permute-start(bf16[128,768]{1,0:T(8,128)(2,1)S(1)} %get-tuple-element.60), channel_id=1, source_target_pairs={{24,0},{32,8},{40,16},{48,24},{56,32},{64,40},{72,48},{80,56},{88,... | collective-permute-start | bytes 589832 | tf_op jit(solution)/shard_map/ppermute | solution.py:492
  49.9 20.9 %collective-permute-start.6 = (bf16[128,512]{1,0:T(8,128)(2,1)S(1)}, bf16[128,512]{1,0:T(8,128)(2,1)S(1)}, u32[]{:S(2)}, u32[]{:S(2)}) collective-permute-start(bf16[128,512]{1,0:T(8,128)(2,1)S(1)} %get-tuple-element.61), channel_id=1, source_target_pairs={{32,0},{40,8},{48,16},{56,24},{64,32},{72,40},{80,48},{88,56},{96,... | collective-permute-start | bytes 393224 | tf_op jit(solution)/shard_map/ppermute | solution.py:492
  51.8 27.1 %all-to-all-start.1 = ((f32[64,1,256]{2,1,0:T(1,128)}), f32[64,1,256]{2,1,0:T(1,128)S(1)}, u32[]{:S(2)}, u32[]{:S(2)}) async-start(f32[64,1,256]{2,1,0:T(1,128)} %get-tuple-element.66), calls=%async_computation.1 | async-start | bytes 131072 | tf_op jit(solution)/shard_map/all_to_all | solution.py:506
  71.7 8.4 %collective-permute-start.7 = (bf16[128,768]{1,0:T(8,128)(2,1)S(1)}, bf16[128,768]{1,0:T(8,128)(2,1)S(1)}, u32[]{:S(2)}, u32[]{:S(2)}) collective-permute-start(bf16[128,768]{1,0:T(8,128)(2,1)S(1)} %get-tuple-element.70), channel_id=1, source_target_pairs={{8,0},{16,8},{24,16},{32,24},{40,32},{48,40},{56,48},{64,56},{72,6... | collective-permute-start | bytes 589832 | tf_op jit(solution)/shard_map/ppermute | solution.py:492
  74.2 11.1 %collective-permute-start.8 = (bf16[128,768]{1,0:T(8,128)(2,1)S(1)}, bf16[128,768]{1,0:T(8,128)(2,1)S(1)}, u32[]{:S(2)}, u32[]{:S(2)}) collective-permute-start(bf16[128,768]{1,0:T(8,128)(2,1)S(1)} %get-tuple-element.71), channel_id=1, source_target_pairs={{16,0},{24,8},{32,16},{40,24},{48,32},{56,40},{64,48},{72,56},{80,... | collective-permute-start | bytes 589832 | tf_op jit(solution)/shard_map/ppermute | solution.py:492

commit v7 on v6

--- a/solution.py
+++ b/solution.py
@@ -165,6 +165,32 @@
         kw_ref[h] = coef.astype(BF16)
 
 
+def carries(blocks, heads):
+    shards = []
+    for block in blocks:
+        size, width = block.shape[0] - 16, heads * DH
+        for h in range(heads):
+            lanes = slice(h * DH, (h + 1) * DH)
+            keys = block[0:size, lanes]
+            dirs = block[0:size, width + h * DH : width + (h + 1) * DH]
+            rate = block[size : size + 16, lanes].astype(F32)
+            shards.append((dirs, keys, jnp.sum(rate, axis=0, keepdims=True)))
+    rows, cols = grids(DH)
+    eye = jnp.where(rows == cols, 1.0, 0.0)
+    matrices = []
+    for (dirs, keys, _), (_, coef, (_, norm_col)) in zip(shards, prepare(shards)):
+        base = jnp.concatenate([keys.astype(F32).T, eye], axis=1)
+        high, low = split(coef * norm_col)
+        turned = dirs.astype(F32).T.astype(BF16)
+        matrices.append(base - (mm(turned, high) + mm(turned, low)))
+    return matrices
+
+
+def far_prepare_kernel(heads, halo2_ref, halo4_ref, out_ref):
+    for at, matrix in enumerate(carries((halo2_ref, halo4_ref), heads)):
+        out_ref[at] = matrix
+
+
 def attend_kernel(
     heads,
     raw_ref,
@@ -176,6 +202,7 @@
     even_ref,
     cross2_ref,
     cross4_ref,
+    far_carry_ref,
     len_ref,
     place_ref,
     att_ref,
@@ -206,7 +233,6 @@
         far_ref[s] = halos[s][0:size, 2 * width : 3 * width]
     rows, cols = grids(size)
     eye = rows == cols
-    eye_f = jnp.where(eye, 1.0, 0.0)
     first = place_ref[0]
     pos_row = first + lax.broadcasted_iota(jnp.int32, (1, size), 1)
     start_row = jnp.zeros((1, size), jnp.int32)
@@ -218,20 +244,9 @@
     seen = [(rows >= cols) & (first + cols >= start)]
     for s in range(1, WIN + 1):
         seen.append(first - s * size + cols >= start)
-    shards = []
-    for s in range(WIN):
-        for h in range(heads):
-            keys = halos[s][0:size, h * DH : (h + 1) * DH]
-            dirs = halos[s][0:size, width + h * DH : width + (h + 1) * DH]
-            rate = halos[s][size : size + 16, h * DH : (h + 1) * DH].astype(F32)
-            shards.append((dirs, keys, jnp.sum(rate, axis=0, keepdims=True)))
-    prepared = prepare(shards)
-    carry = []
-    for (dirs, keys, _), (_, coef, (_, norm_col)) in zip(shards, prepared):
-        base = jnp.concatenate([keys.astype(F32).T, eye_f], axis=1)
-        high, low = split(coef * norm_col)
-        turned = dirs.astype(F32).T.astype(BF16)
-        carry.append(base - (mm(turned, high) + mm(turned, low)))
+    near = carries((halo1_ref, halo3_ref), heads)
+    carry = near[0:heads] + [far_carry_ref[h] for h in range(heads)]
+    carry = carry + near[heads : 2 * heads] + [far_carry_ref[heads + h] for h in range(heads)]
     square = jnp.zeros((size, 1), F32)
     inner = jnp.zeros((size, 1), F32)
     for h in range(heads):
@@ -516,7 +531,7 @@
     unit_flops = 2 * size * size * DH
     packed = pack(keys, dirs, values, rates)
     halo2 = passed_along(packed, 2)
-    even = paired(packed, 0, 1)
+    halo4 = passed_along(packed, 4)
     inverse, coef, raw = call(
         own_kernel,
         [((heads, size, size), BF16), ((heads, size, 2 * DH), BF16), ((heads, size, 2 * DH), F32)],
@@ -526,11 +541,19 @@
         dirs,
         rates,
     )
+    own_packed, raw = lax.optimization_barrier((packed, raw))
+    even = paired(own_packed, 0, 1)
     halo2, raw = lax.optimization_barrier((halo2, raw))
-    halo4 = passed_along(halo2, 2)
     cross2 = swapped(halo2)
     cross2, halo4 = lax.optimization_barrier((cross2, halo4))
-    halos = (halo2, halo4, even, cross2, paired(halo4, 1, -1))
+    (far_carry,) = call(
+        functools.partial(far_prepare_kernel, heads),
+        [((2 * heads, DH, 2 * DH), F32)],
+        heads * 150 * unit_flops,
+        halo2,
+        halo4,
+    )
+    halos = (halo2, halo4, even, cross2, paired(halo4, 1, -1), far_carry)
     att, total, prob, frame, carry, sums, far = call(
         functools.partial(attend_kernel, heads),
         [

time: 87.8 us -> 83.5 us (0.951)
  waiting for transfers between devices: 12.2 us -> 7.43 us
  starting transfers between devices: 44.1 us -> 42.8 us
  Pallas kernels: 15.5 us -> 16.5 us
    ppermute x6, waiting for transfers between devices: 8.11 us -> 5.29 us  [passed_along(): lax.ppermute(value, 'ctx', [(source, source + steps) for source in range(...]
    ppermute x2, waiting for transfers between devices: 1.99 us -> 0.01 us  [paired(): lax.ppermute(value, 'ctx', [(source, source + step) for source in range(f...]
    ppermute x6, starting transfers between devices: 19.4 us -> 18 us  [passed_along(): lax.ppermute(value, 'ctx', [(source, source + steps) for source in range(...]
    pallas_call x6 -> x7, Pallas kernels: 13.8 us -> 14.8 us  [call(): pl.pallas_call(body, out_shape=[jax.ShapeDtypeStruct(s, d) for s, d in ou...]
  transfers between devices with their start and end apart: 10 -> 10, of which waited for: 4 -> 2; matrix products, arithmetic and copies ran while one was open for 0% -> 0% of each run, Pallas kernels for 5% -> 8%
where the time goes in v7:
time: 83.5 us; the launch traced here: 83.1 us
  starting transfers between devices  42.8 us (51%)
  Pallas kernels  16.5 us (20%)
  blocking collectives  14.6 us (17%)
  waiting for transfers between devices  7.43 us (9%)
  between operations  0.92 us (1%)
    all_to_all x1, starting transfers between devices, gathered(): lax.all_to_all(value, axis, 0, 0, axis_index_groups=groups, tiled=True)  19.2 us
    ppermute x6, starting transfers between devices, passed_along(): lax.ppermute(value, 'ctx', [(source, source + steps) for source in range(...  18 us
    pallas_call x7, Pallas kernels, call(): pl.pallas_call(body, out_shape=[jax.ShapeDtypeStruct(s, d) for s, d in ou...  14.8 us
    all_to_all x1, blocking collectives, gathered(): lax.all_to_all(value, axis, 0, 0, axis_index_groups=groups, tiled=True)  14.6 us
    ppermute x6, waiting for transfers between devices, passed_along(): lax.ppermute(value, 'ctx', [(source, source + steps) for source in range(...  5.29 us
    ppermute x2, starting transfers between devices, paired(): lax.ppermute(value, 'ctx', [(source, source + step) for source in range(f...  3.71 us
    all_to_all x1, waiting for transfers between devices, gathered(): lax.all_to_all(value, axis, 0, 0, axis_index_groups=groups, tiled=True)  2.12 us
    ppermute x1, starting transfers between devices, swapped(): lax.ppermute(value, 'ctx', [(source, source ^ 1) for source in range(coun...  1.92 us
  transfers between devices with their start and end apart: 10, of which 2 were waited for; matrix products, arithmetic and copies ran while one was open for 0% of the time, Pallas kernels for 8%

profile of v7, /device:TPU:6, one launch (start us, length us, event | category | flops | bytes accessed | tf_op | source)
XLA Modules:
  0.0 83.1 jit_solution(4985163947274287670)
XLA Ops:
  0.7 1.7 %shard_map.135 = bf16[144,768]{1,0:T(8,128)(2,1)} custom-call(bf16[128,256]{1,0:T(8,128)(2,1)} %key_ref.7, bf16[128,256]{1,0:T(8,128)(2,1)} %dir_ref.7, bf16[128,256]{1,0:T(8,128)(2,1)} %value_ref.5, f32[2,128]{1,0:T(2,128)} %rate_ref.5), custom_call_target="tpu_custom_call" | custom-call | tf_op jit(solution)/shard_map/pallas_call | solution.py:138
  2.4 4.3 %collective-permute-start = (bf16[144,768]{1,0:T(8,128)(2,1)}, bf16[144,768]{1,0:T(8,128)(2,1)S(1)}, u32[]{:S(2)}, u32[]{:S(2)}) collective-permute-start(bf16[144,768]{1,0:T(8,128)(2,1)} %shard_map.135), channel_id=1, source_target_pairs={{0,16},{8,24},{16,32},{24,40},{32,48},{40,56},{48,64},{56,72},{64,... | collective-permute-start | bytes 663560 | tf_op jit(solution)/shard_map/ppermute | solution.py:507
  6.7 4.3 %collective-permute-start.2 = (bf16[144,768]{1,0:T(8,128)(2,1)}, bf16[144,768]{1,0:T(8,128)(2,1)S(1)}, u32[]{:S(2)}, u32[]{:S(2)}) collective-permute-start(bf16[144,768]{1,0:T(8,128)(2,1)} %shard_map.135), channel_id=1, source_target_pairs={{0,32},{8,40},{16,48},{24,56},{32,64},{40,72},{48,80},{56,88},{64,... | collective-permute-start | bytes 663560 | tf_op jit(solution)/shard_map/ppermute | solution.py:507
  11.1 2.2 %shard_map.136 = (bf16[2,128,128]{2,1,0:T(8,128)(2,1)S(1)}, bf16[2,128,256]{2,1,0:T(8,128)(2,1)S(1)}, f32[2,128,256]{2,1,0:T(8,128)S(1)}) custom-call(bf16[128,256]{1,0:T(8,128)(2,1)S(1)} %copy-done.6, bf16[128,256]{1,0:T(8,128)(2,1)S(1)} %copy-done, bf16[128,256]{1,0:T(8,128)(2,1)S(1)} %copy-done.1, f32[2,128]{1,0:T(2,128)S(1)} %copy-done.4), custom_call_target="tpu_custom_call" | custom-call | flops 503316480 | bytes 656384 | tf_op jit(solution)/shard_map/pallas_call | solution.py:493
  13.3 1.9 %collective-permute-start.1 = (bf16[144,768]{1,0:T(8,128)(2,1)S(1)}, bf16[144,768]{1,0:T(8,128)(2,1)S(1)}, u32[]{:S(2)}, u32[]{:S(2)}) collective-permute-start(bf16[144,768]{1,0:T(8,128)(2,1)S(1)} %collective-permute-done.halo2_ref), channel_id=1, source_target_pairs={{0,8},{8,0},{16,24},{24,16},{32,40},{40,32},{48,56},{56,48},{64,72... | collective-permute-start | bytes 663560 | tf_op jit(solution)/shard_map/ppermute | solution.py:517
  15.3 2.4 %collective-permute-start.3 = (bf16[144,768]{1,0:T(8,128)(2,1)S(1)}, bf16[144,768]{1,0:T(8,128)(2,1)S(1)}, u32[]{:S(2)}, u32[]{:S(2)}) collective-permute-start(bf16[144,768]{1,0:T(8,128)(2,1)S(1)} %copy-done.8), channel_id=1, source_target_pairs={{0,8},{16,24},{32,40},{48,56},{64,72},{80,88},{96,104},{112,120},{... | collective-permute-start | bytes 663560 | tf_op jit(solution)/shard_map/ppermute | solution.py:512
  17.7 1.3 %collective-permute-start.4 = (bf16[144,768]{1,0:T(8,128)(2,1)S(1)}, bf16[144,768]{1,0:T(8,128)(2,1)S(1)}, u32[]{:S(2)}, u32[]{:S(2)}) collective-permute-start(bf16[144,768]{1,0:T(8,128)(2,1)S(1)} %collective-permute-done.2.halo4_ref), channel_id=1, source_target_pairs={{8,0},{24,16},{40,32},{56,48},{72,64},{88,80},{104,96},{120,112},{... | collective-permute-start | bytes 663560 | tf_op jit(solution)/shard_map/ppermute | solution.py:512
  19.0 0.1 pad_add_fusion.place_ref
  19.1 2.5 %shard_map.137.far_carry_ref = f32[4,128,256]{2,1,0:T(8,128)S(1)} custom-call(bf16[144,768]{1,0:T(8,128)(2,1)S(1)} %collective-permute-done.halo2_ref, bf16[144,768]{1,0:T(8,128)(2,1)S(1)} %collective-permute-done.2.halo4_ref), custom_call_target="tpu_custom_call" | custom-call | flops 1258291200 | bytes 966656 | tf_op jit(solution)/shard_map/pallas_call | solution.py:493
  21.6 0.0 copy-start.7
  21.6 0.6 copy-done.5
  22.2 4.6 %shard_map.138 = (f32[128,256]{1,0:T(8,128)S(1)}, f32[2,128,8]{2,1,0:T(8,128)S(1)}, bf16[2,5,128,128]{3,2,1,0:T(8,128)(2,1)S(1)}, bf16[2,4,128,128]{3,2,1,0:T(8,...) custom-call(f32[2,128,256]{2,1,0:T(8,128)S(1)} %get-tuple-element.50, ...), custom_call_target="tpu_custom_call" | custom-call | flops 2516582400 | bytes 3548160 | tf_op jit(solution)/shard_map/pallas_call | solution.py:493
  26.8 14.6 %all_to_all.10.sums_ref = f32[8,1,256]{2,1,0:T(1,128)S(1)} all-to-all(f32[8,1,256]{2,1,0:T(1,128)S(1)} %get-tuple-element.55), channel_id=1, replica_groups=mesh['ctx'=64,'head'=8] {'head'}, dimensions={0} | all-to-all | bytes 16384 | tf_op jit(solution)/shard_map/all_to_all | solution.py:521
  41.5 1.5 %shard_map.139 = (bf16[128,256]{1,0:T(8,128)(2,1)}, f32[64,1,256]{2,1,0:T(1,128)}, bf16[128,256]{1,0:T(8,128)(2,1)S(1)}, f32[2,128,8]{2,1,0:T(8,128)S(1)}, bf16[...) custom-call(f32[8,1,256]{2,1,0:T(1,128)S(1)} %all_to_all.10.sums_ref, ...), custom_call_target="tpu_custom_call" | custom-call | flops 125829120 | bytes 2188288 | tf_op jit(solution)/shard_map/pallas_call | solution.py:493
  42.9 2.3 %collective-permute-start.5 = (bf16[128,768]{1,0:T(8,128)(2,1)S(1)}, bf16[128,768]{1,0:T(8,128)(2,1)S(1)}, u32[]{:S(2)}, u32[]{:S(2)}) collective-permute-start(bf16[128,768]{1,0:T(8,128)(2,1)S(1)} %get-tuple-element.64), channel_id=1, source_target_pairs={{24,0},{32,8},{40,16},{48,24},{56,32},{64,40},{72,48},{80,56},{88,... | collective-permute-start | bytes 589832 | tf_op jit(solution)/shard_map/ppermute | solution.py:507
  45.2 2.0 %collective-permute-start.6 = (bf16[128,512]{1,0:T(8,128)(2,1)S(1)}, bf16[128,512]{1,0:T(8,128)(2,1)S(1)}, u32[]{:S(2)}, u32[]{:S(2)}) collective-permute-start(bf16[128,512]{1,0:T(8,128)(2,1)S(1)} %get-tuple-element.65), channel_id=1, source_target_pairs={{32,0},{40,8},{48,16},{56,24},{64,32},{72,40},{80,48},{88,56},{96,... | collective-permute-start | bytes 393224 | tf_op jit(solution)/shard_map/ppermute | solution.py:507
  47.3 19.2 %all-to-all-start.1 = ((f32[64,1,256]{2,1,0:T(1,128)}), f32[64,1,256]{2,1,0:T(1,128)S(1)}, u32[]{:S(2)}, u32[]{:S(2)}) async-start(f32[64,1,256]{2,1,0:T(1,128)} %get-tuple-element.70), calls=%async_computation.1 | async-start | bytes 131072 | tf_op jit(solution)/shard_map/all_to_all | solution.py:521
  66.5 0.9 %shard_map.140 = (bf16[2,128,256]{2,1,0:T(8,128)(2,1)S(1)}, f32[128,256]{1,0:T(8,128)S(1)}, bf16[128,768]{1,0:T(8,128)(2,1)S(1)}, bf16[128,768]{1,0:T(8,128)(2,1)S(1)}) custom-call(bf16[128,256]{1,0:T(8,128)(2,1)S(1)} %get-tuple-element.66.scaled_ref, f32[2,128,8]{2,1,0:T(8,128)S(1)} %get-tuple-element.67.delta_ref, ...), custom_call_target="tpu_custom_call" | custom-call | flops 25165824000 | bytes 2236416 | tf_op jit(solution)/shard_map/pallas_call | solution.py:493
  67.4 2.5 %collective-permute-start.7 = (bf16[128,768]{1,0:T(8,128)(2,1)S(1)}, bf16[128,768]{1,0:T(8,128)(2,1)S(1)}, u32[]{:S(2)}, u32[]{:S(2)}) collective-permute-start(bf16[128,768]{1,0:T(8,128)(2,1)S(1)} %get-tuple-element.74), channel_id=1, source_target_pairs={{8,0},{16,8},{24,16},{32,24},{40,32},{48,40},{56,48},{64,56},{72,6... | collective-permute-start | bytes 589832 | tf_op jit(solution)/shard_map/ppermute | solution.py:507
  69.9 2.5 %collective-permute-start.8 = (bf16[128,768]{1,0:T(8,128)(2,1)S(1)}, bf16[128,768]{1,0:T(8,128)(2,1)S(1)}, u32[]{:S(2)}, u32[]{:S(2)}) collective-permute-start(bf16[128,768]{1,0:T(8,128)(2,1)S(1)} %get-tuple-element.75), channel_id=1, source_target_pairs={{16,0},{24,8},{32,16},{40,24},{48,32},{56,40},{64,48},{72,56},{80,... | collective-permute-start | bytes 589832 | tf_op jit(solution)/shard_map/ppermute | solution.py:507
  72.4 2.1 %all-to-all-done.1.parts_ref = f32[64,1,256]{2,1,0:T(1,128)S(1)} async-done(((f32[64,1,256]{2,1,0:T(1,128)}), f32[64,1,256]{2,1,0:T(1,128)S(1)}, u32[]{:S(2)}, u32[]{:S(2)}) %all-to-all-start.1) | async-done | bytes 65568 | tf_op jit(solution)/shard_map/all_to_all | solution.py:521
  74.5 1.2 %shard_map.141 = (bf16[128,256]{1,0:T(8,128)(2,1)}, f32[2,128,128]{2,1,0:T(8,128)S(1)}, f32[2,128,128]{2,1,0:T(8,128)S(1)}, f32[2,128,256]{2,1,0:T(8,128)S(1)}) custom-call(bf16[2,128,256]{2,1,0:T(8,128)(2,1)S(1)} %get-tuple-element.71.own_ref, bf16[2,128,256]{2,1,0:T(8,128)(2,1)S(1)} %get-tuple-element.72.kw_ref, bf16[128,256]{1,0:T(8,128)(2,1)S(1)} %copy-done.6, ...), custom_call_target="tpu_custom_call" | custom-call | flops 1258291200 | bytes 1048576 | tf_op jit(solution)/shard_map/pallas_call | solution.py:493
  75.7 5.3 %collective-permute-done.8.recv2_ref = bf16[128,768]{1,0:T(8,128)(2,1)S(1)} collective-permute-done((bf16[128,768]{1,0:T(8,128)(2,1)S(1)}, bf16[128,768]{1,0:T(8,128)(2,1)S(1)}, u32[]{:S(2)}, u32[]{:S(2)}) %collective-permute-start.8) | collective-permute-done | bytes 196640 | tf_op jit(solution)/shard_map/ppermute | solution.py:507
  81.0 2.0 %shard_map.142 = (bf16[128,256]{1,0:T(8,128)(2,1)}, bf16[128,256]{1,0:T(8,128)(2,1)}, bf16[128,256]{1,0:T(8,128)(2,1)}, f32[2,128]{1,0:T(2,128)}, f32[1,256]{1,0:T(1,128)}) custom-call(bf16[128,768]{1,0:T(8,128)(2,1)S(1)} %collective-permute-done.7.recv1_ref, bf16[128,768]{1,0:T(8,128)(2,1)S(1)} %collective-permute-done.8.recv2_ref, ...), custom_call_target="tpu_custom_call" | custom-call | flops 167772160 | bytes 1969152 | tf_op jit(solution)/shard_map/pallas_call | solution.py:493
  (24 shorter events, 0.1 us)
Async XLA Ops:
  0.6 10.4 %copy-start.1 = (bf16[128,256]{1,0:T(8,128)(2,1)S(1)}, bf16[128,256]{1,0:T(8,128)(2,1)}, u32[]{:S(2)}) copy-start(bf16[128,256]{1,0:T(8,128)(2,1)} %dir_ref.7) | copy-start | bytes 196612
  0.6 10.4 %copy-start = (bf16[128,256]{1,0:T(8,128)(2,1)S(1)}, bf16[128,256]{1,0:T(8,128)(2,1)}, u32[]{:S(2)}) copy-start(bf16[128,256]{1,0:T(8,128)(2,1)} %key_ref.7) | copy-start | bytes 196612
  0.7 10.4 %copy-start.4 = (f32[2,128]{1,0:T(2,128)S(1)}, f32[2,128]{1,0:T(2,128)}, u32[]{:S(2)}) copy-start(f32[2,128]{1,0:T(2,128)} %rate_ref.5) | copy-start | bytes 3076
  0.7 10.4 %copy-start.6 = (bf16[128,256]{1,0:T(8,128)(2,1)S(1)}, bf16[128,256]{1,0:T(8,128)(2,1)}, u32[]{:S(2)}) copy-start(bf16[128,256]{1,0:T(8,128)(2,1)} %query_ref.3) | copy-start | bytes 196612
  2.4 12.9 %copy-start.8 = (bf16[144,768]{1,0:T(8,128)(2,1)S(1)}, bf16[144,768]{1,0:T(8,128)(2,1)}, u32[]{:S(2)}) copy-start(bf16[144,768]{1,0:T(8,128)(2,1)} %shard_map.135) | copy-start | bytes 663556
  2.4 10.9 %collective-permute-start = (bf16[144,768]{1,0:T(8,128)(2,1)}, bf16[144,768]{1,0:T(8,128)(2,1)S(1)}, u32[]{:S(2)}, u32[]{:S(2)}) collective-permute-start(bf16[144,768]{1,0:T(8,128)(2,1)} %shard_map.135), channel_id=1, source_target_pairs={{0,16},{8,24},{16,32},{24,40},{32,48},{40,56},{48,64},{56,72},{64,... | collective-permute-start | bytes 663560 | tf_op jit(solution)/shard_map/ppermute | solution.py:507
  6.7 11.0 %collective-permute-start.2 = (bf16[144,768]{1,0:T(8,128)(2,1)}, bf16[144,768]{1,0:T(8,128)(2,1)S(1)}, u32[]{:S(2)}, u32[]{:S(2)}) collective-permute-start(bf16[144,768]{1,0:T(8,128)(2,1)} %shard_map.135), channel_id=1, source_target_pairs={{0,32},{8,40},{16,48},{24,56},{32,64},{40,72},{48,80},{56,88},{64,... | collective-permute-start | bytes 663560 | tf_op jit(solution)/shard_map/ppermute | solution.py:507
  13.3 4.4 %collective-permute-start.1 = (bf16[144,768]{1,0:T(8,128)(2,1)S(1)}, bf16[144,768]{1,0:T(8,128)(2,1)S(1)}, u32[]{:S(2)}, u32[]{:S(2)}) collective-permute-start(bf16[144,768]{1,0:T(8,128)(2,1)S(1)} %collective-permute-done.halo2_ref), channel_id=1, source_target_pairs={{0,8},{8,0},{16,24},{24,16},{32,40},{40,32},{48,56},{56,48},{64,72... | collective-permute-start | bytes 663560 | tf_op jit(solution)/shard_map/ppermute | solution.py:517
  15.3 6.3 %collective-permute-start.3 = (bf16[144,768]{1,0:T(8,128)(2,1)S(1)}, bf16[144,768]{1,0:T(8,128)(2,1)S(1)}, u32[]{:S(2)}, u32[]{:S(2)}) collective-permute-start(bf16[144,768]{1,0:T(8,128)(2,1)S(1)} %copy-done.8), channel_id=1, source_target_pairs={{0,8},{16,24},{32,40},{48,56},{64,72},{80,88},{96,104},{112,120},{... | collective-permute-start | bytes 663560 | tf_op jit(solution)/shard_map/ppermute | solution.py:512
  17.7 3.9 %collective-permute-start.4 = (bf16[144,768]{1,0:T(8,128)(2,1)S(1)}, bf16[144,768]{1,0:T(8,128)(2,1)S(1)}, u32[]{:S(2)}, u32[]{:S(2)}) collective-permute-start(bf16[144,768]{1,0:T(8,128)(2,1)S(1)} %collective-permute-done.2.halo4_ref), channel_id=1, source_target_pairs={{8,0},{24,16},{40,32},{56,48},{72,64},{88,80},{104,96},{120,112},{... | collective-permute-start | bytes 663560 | tf_op jit(solution)/shard_map/ppermute | solution.py:512
  19.1 2.5 %copy-start.2 = (bf16[128,256]{1,0:T(8,128)(2,1)S(1)}, bf16[128,256]{1,0:T(8,128)(2,1)}, u32[]{:S(2)}) copy-start(bf16[128,256]{1,0:T(8,128)(2,1)} %cot_ref.3) | copy-start | bytes 196612
  19.1 2.5 %copy-start.3 = (bf16[128,256]{1,0:T(8,128)(2,1)S(1)}, bf16[128,256]{1,0:T(8,128)(2,1)}, u32[]{:S(2)}) copy-start(bf16[128,256]{1,0:T(8,128)(2,1)} %value_ref.5) | copy-start | bytes 196612
  21.6 0.7 copy-start.5
  21.6 0.7 copy-start.7
  42.9 23.6 %collective-permute-start.5 = (bf16[128,768]{1,0:T(8,128)(2,1)S(1)}, bf16[128,768]{1,0:T(8,128)(2,1)S(1)}, u32[]{:S(2)}, u32[]{:S(2)}) collective-permute-start(bf16[128,768]{1,0:T(8,128)(2,1)S(1)} %get-tuple-element.64), channel_id=1, source_target_pairs={{24,0},{32,8},{40,16},{48,24},{56,32},{64,40},{72,48},{80,56},{88,... | collective-permute-start | bytes 589832 | tf_op jit(solution)/shard_map/ppermute | solution.py:507
  45.2 21.2 %collective-permute-start.6 = (bf16[128,512]{1,0:T(8,128)(2,1)S(1)}, bf16[128,512]{1,0:T(8,128)(2,1)S(1)}, u32[]{:S(2)}, u32[]{:S(2)}) collective-permute-start(bf16[128,512]{1,0:T(8,128)(2,1)S(1)} %get-tuple-element.65), channel_id=1, source_target_pairs={{32,0},{40,8},{48,16},{56,24},{64,32},{72,40},{80,48},{88,56},{96,... | collective-permute-start | bytes 393224 | tf_op jit(solution)/shard_map/ppermute | solution.py:507
  47.3 27.3 %all-to-all-start.1 = ((f32[64,1,256]{2,1,0:T(1,128)}), f32[64,1,256]{2,1,0:T(1,128)S(1)}, u32[]{:S(2)}, u32[]{:S(2)}) async-start(f32[64,1,256]{2,1,0:T(1,128)} %get-tuple-element.70), calls=%async_computation.1 | async-start | bytes 131072 | tf_op jit(solution)/shard_map/all_to_all | solution.py:521
  67.4 8.4 %collective-permute-start.7 = (bf16[128,768]{1,0:T(8,128)(2,1)S(1)}, bf16[128,768]{1,0:T(8,128)(2,1)S(1)}, u32[]{:S(2)}, u32[]{:S(2)}) collective-permute-start(bf16[128,768]{1,0:T(8,128)(2,1)S(1)} %get-tuple-element.74), channel_id=1, source_target_pairs={{8,0},{16,8},{24,16},{32,24},{40,32},{48,40},{56,48},{64,56},{72,6... | collective-permute-start | bytes 589832 | tf_op jit(solution)/shard_map/ppermute | solution.py:507
  69.9 11.1 %collective-permute-start.8 = (bf16[128,768]{1,0:T(8,128)(2,1)S(1)}, bf16[128,768]{1,0:T(8,128)(2,1)S(1)}, u32[]{:S(2)}, u32[]{:S(2)}) collective-permute-start(bf16[128,768]{1,0:T(8,128)(2,1)S(1)} %get-tuple-element.75), channel_id=1, source_target_pairs={{16,0},{24,8},{32,16},{40,24},{48,32},{56,40},{64,48},{72,56},{80,... | collective-permute-start | bytes 589832 | tf_op jit(solution)/shard_map/ppermute | solution.py:507

commit v8 on v7

--- a/solution.py
+++ b/solution.py
@@ -144,10 +144,20 @@
     )(keys, dirs, values, rates)
 
 
-def own_kernel(query_ref, key_ref, dir_ref, rate_ref, inv_ref, kw_ref, raw_ref):
+def own_kernel(
+    query_ref, key_ref, dir_ref, rate_ref, gain_ref, len_ref, place_ref, inv_ref, kw_ref, raw_ref, gain_out_ref, start_ref
+):
     size = query_ref.shape[0]
     heads = rate_ref.shape[0]
     rows, cols = grids(size)
+    gain_out_ref[...] = gain_ref[...]
+    pos_row = place_ref[0] + lax.broadcasted_iota(jnp.int32, (1, size), 1)
+    start_row = jnp.zeros((1, size), jnp.int32)
+    end = jnp.int32(0)
+    for d in range(len_ref.shape[0]):
+        end = end + len_ref[d]
+        start_row = jnp.where(end <= pos_row, end, start_row)
+    start_ref[...] = start_row.astype(F32)
     shards = []
     for h in range(heads):
         lanes = slice(h * DH, (h + 1) * DH)
@@ -203,7 +213,7 @@
     cross2_ref,
     cross4_ref,
     far_carry_ref,
-    len_ref,
+    start_ref,
     place_ref,
     att_ref,
     tot_ref,
@@ -234,13 +244,7 @@
     rows, cols = grids(size)
     eye = rows == cols
     first = place_ref[0]
-    pos_row = first + lax.broadcasted_iota(jnp.int32, (1, size), 1)
-    start_row = jnp.zeros((1, size), jnp.int32)
-    end = jnp.int32(0)
-    for d in range(len_ref.shape[0]):
-        end = end + len_ref[d]
-        start_row = jnp.where(end <= pos_row, end, start_row)
-    start = to_col(start_row.astype(F32), eye).astype(jnp.int32)
+    start = to_col(start_ref[...], eye).astype(jnp.int32)
     seen = [(rows >= cols) & (first + cols >= start)]
     for s in range(1, WIN + 1):
         seen.append(first - s * size + cols >= start)
@@ -532,14 +536,16 @@
     packed = pack(keys, dirs, values, rates)
     halo2 = passed_along(packed, 2)
     halo4 = passed_along(packed, 4)
-    inverse, coef, raw = call(
+    inverse, coef, raw, gain_row, start_row = call(
         own_kernel,
-        [((heads, size, size), BF16), ((heads, size, 2 * DH), BF16), ((heads, size, 2 * DH), F32)],
+        [((heads, size, size), BF16), ((heads, size, 2 * DH), BF16), ((heads, size, 2 * DH), F32), ((1, width), F32), ((1, size), F32)],
         heads * 60 * unit_flops,
         query,
         keys,
         dirs,
         rates,
+        gain_row,
+        scalars=(doc_lengths, place),
     )
     own_packed, raw = lax.optimization_barrier((packed, raw))
     even = paired(own_packed, 0, 1)
@@ -553,7 +559,7 @@
         halo2,
         halo4,
     )
-    halos = (halo2, halo4, even, cross2, paired(halo4, 1, -1), far_carry)
+    halos = (halo2, halo4, even, cross2, paired(halo4, 1, -1), far_carry, start_row)
     att, total, prob, frame, carry, sums, far = call(
         functools.partial(attend_kernel, heads),
         [
@@ -571,7 +577,7 @@
         cotangent,
         gain_row,
         *halos,
-        scalars=(doc_lengths, place),
+        scalars=(place,),
         scratch=[pltpu.VMEM((size + 16, 3 * width), BF16)] * 2,
     )
     sums = gathered(sums, "head")
@@ -621,7 +627,8 @@
         far,
     )
     own, parts = lax.optimization_barrier((own, parts))
-    recvs = (passed_along(send1, -1), passed_along(send2, -2), recv3, recv4)
+    recv2 = passed_along(send2, -2)
+    recvs = (passed_along(send1, -1), recv2, recv3, recv4)
     dquery, dkey_part, ddir_part, pulled = call(
         functools.partial(local_kernel, heads),
         [

time: 83.5 us -> 82.7 us (level)
  starting transfers between devices: 42.8 us -> 41.4 us
    all_to_all x1, starting transfers between devices: 19.2 us -> 17.8 us  [gathered(): lax.all_to_all(value, axis, 0, 0, axis_index_groups=groups, tiled=True)]
  transfers between devices with their start and end apart: 10 -> 10, of which waited for: 2 -> 2; matrix products, arithmetic and copies ran while one was open for 0% -> 0% of each run, Pallas kernels for 8% -> 9%
where the time goes in v8:
time: 82.7 us; the launch traced here: 82.2 us
  starting transfers between devices  41.4 us (50%)
  Pallas kernels  17.1 us (21%)
  blocking collectives  14.7 us (18%)
  waiting for transfers between devices  7.43 us (9%)
  between operations  0.89 us (1%)
    ppermute x6, starting transfers between devices, passed_along(): lax.ppermute(value, 'ctx', [(source, source + steps) for source in range(...  17.8 us
    all_to_all x1, starting transfers between devices, gathered(): lax.all_to_all(value, axis, 0, 0, axis_index_groups=groups, tiled=True)  17.8 us
    pallas_call x7, Pallas kernels, call(): pl.pallas_call(body, out_shape=[jax.ShapeDtypeStruct(s, d) for s, d in ou...  15.4 us
    all_to_all x1, blocking collectives, gathered(): lax.all_to_all(value, axis, 0, 0, axis_index_groups=groups, tiled=True)  14.7 us
    ppermute x6, waiting for transfers between devices, passed_along(): lax.ppermute(value, 'ctx', [(source, source + steps) for source in range(...  5.29 us
    ppermute x2, starting transfers between devices, paired(): lax.ppermute(value, 'ctx', [(source, source + step) for source in range(f...  3.71 us
    all_to_all x1, waiting for transfers between devices, gathered(): lax.all_to_all(value, axis, 0, 0, axis_index_groups=groups, tiled=True)  2.13 us
    ppermute x1, starting transfers between devices, swapped(): lax.ppermute(value, 'ctx', [(source, source ^ 1) for source in range(coun...  2.05 us
  transfers between devices with their start and end apart: 10, of which 2 were waited for; matrix products, arithmetic and copies ran while one was open for 0% of the time, Pallas kernels for 9%

profile of v8, /device:TPU:6, one launch (start us, length us, event | category | flops | bytes accessed | tf_op | source)
XLA Modules:
  0.0 82.2 jit_solution(5083384901778175324)
XLA Ops:
  0.7 1.7 %shard_map.135 = bf16[144,768]{1,0:T(8,128)(2,1)} custom-call(bf16[128,256]{1,0:T(8,128)(2,1)} %key_ref.7, bf16[128,256]{1,0:T(8,128)(2,1)} %dir_ref.7, bf16[128,256]{1,0:T(8,128)(2,1)} %value_ref.5, f32[2,128]{1,0:T(2,128)} %rate_ref.5), custom_call_target="tpu_custom_call" | custom-call | tf_op jit(solution)/shard_map/pallas_call | solution.py:138
  2.4 4.2 %collective-permute-start = (bf16[144,768]{1,0:T(8,128)(2,1)}, bf16[144,768]{1,0:T(8,128)(2,1)S(1)}, u32[]{:S(2)}, u32[]{:S(2)}) collective-permute-start(bf16[144,768]{1,0:T(8,128)(2,1)} %shard_map.135), channel_id=1, source_target_pairs={{0,16},{8,24},{16,32},{24,40},{32,48},{40,56},{48,64},{56,72},{64,... | collective-permute-start | bytes 663560 | tf_op jit(solution)/shard_map/ppermute | solution.py:511
  6.6 4.3 %collective-permute-start.2 = (bf16[144,768]{1,0:T(8,128)(2,1)}, bf16[144,768]{1,0:T(8,128)(2,1)S(1)}, u32[]{:S(2)}, u32[]{:S(2)}) collective-permute-start(bf16[144,768]{1,0:T(8,128)(2,1)} %shard_map.135), channel_id=1, source_target_pairs={{0,32},{8,40},{16,48},{24,56},{32,64},{40,72},{48,80},{56,88},{64,... | collective-permute-start | bytes 663560 | tf_op jit(solution)/shard_map/ppermute | solution.py:511
  10.9 0.1 pad_add_fusion.place_ref
  11.0 0.6 copy-done.6
  11.6 0.1 copy-done.4
  11.7 2.7 %shard_map.136 = (bf16[2,128,128]{2,1,0:T(8,128)(2,1)S(1)}, bf16[2,128,256]{2,1,0:T(8,128)(2,1)S(1)}, f32[2,128,256]{2,1,0:T(8,128)S(1)}, f32[1,256]{1,0:T(1,128)S(1)}, f32[1,128]{1,0:T(1,128)S(1)}) custom-call(bf16[128,256]{1,0:T(8,128)(2,1)S(1)} %copy-done.5, bf16[128,256]{1,0:T(8,128)(2,1)S(1)} %copy-done, bf16[128,256]{1,0:T(8,128)(2,1)S(1)} %copy-done.1, ...), custom_call_target="tpu_custom_call" | custom-call | flops 503316480 | bytes 658944 | tf_op jit(solution)/shard_map/pallas_call | solution.py:497
  14.5 2.1 %collective-permute-start.1 = (bf16[144,768]{1,0:T(8,128)(2,1)S(1)}, bf16[144,768]{1,0:T(8,128)(2,1)S(1)}, u32[]{:S(2)}, u32[]{:S(2)}) collective-permute-start(bf16[144,768]{1,0:T(8,128)(2,1)S(1)} %collective-permute-done.halo2_ref), channel_id=1, source_target_pairs={{0,8},{8,0},{16,24},{24,16},{32,40},{40,32},{48,56},{56,48},{64,72... | collective-permute-start | bytes 663560 | tf_op jit(solution)/shard_map/ppermute | solution.py:521
  16.5 2.4 %collective-permute-start.3 = (bf16[144,768]{1,0:T(8,128)(2,1)S(1)}, bf16[144,768]{1,0:T(8,128)(2,1)S(1)}, u32[]{:S(2)}, u32[]{:S(2)}) collective-permute-start(bf16[144,768]{1,0:T(8,128)(2,1)S(1)} %copy-done.8), channel_id=1, source_target_pairs={{0,8},{16,24},{32,40},{48,56},{64,72},{80,88},{96,104},{112,120},{... | collective-permute-start | bytes 663560 | tf_op jit(solution)/shard_map/ppermute | solution.py:516
  19.0 1.3 %collective-permute-start.4 = (bf16[144,768]{1,0:T(8,128)(2,1)S(1)}, bf16[144,768]{1,0:T(8,128)(2,1)S(1)}, u32[]{:S(2)}, u32[]{:S(2)}) collective-permute-start(bf16[144,768]{1,0:T(8,128)(2,1)S(1)} %collective-permute-done.2.halo4_ref), channel_id=1, source_target_pairs={{8,0},{24,16},{40,32},{56,48},{72,64},{88,80},{104,96},{120,112},{... | collective-permute-start | bytes 663560 | tf_op jit(solution)/shard_map/ppermute | solution.py:516
  20.3 2.5 %shard_map.137.far_carry_ref = f32[4,128,256]{2,1,0:T(8,128)S(1)} custom-call(bf16[144,768]{1,0:T(8,128)(2,1)S(1)} %collective-permute-done.halo2_ref, bf16[144,768]{1,0:T(8,128)(2,1)S(1)} %collective-permute-done.2.halo4_ref), custom_call_target="tpu_custom_call" | custom-call | flops 1258291200 | bytes 966656 | tf_op jit(solution)/shard_map/pallas_call | solution.py:497
  22.8 4.6 %shard_map.138 = (f32[128,256]{1,0:T(8,128)S(1)}, f32[2,128,8]{2,1,0:T(8,128)S(1)}, bf16[2,5,128,128]{3,2,1,0:T(8,128)(2,1)S(1)}, bf16[2,4,128,128]{3,2,1,0:T(8,...) custom-call(f32[2,128,256]{2,1,0:T(8,128)S(1)} %get-tuple-element.52, ...), custom_call_target="tpu_custom_call" | custom-call | flops 2516582400 | bytes 3548672 | tf_op jit(solution)/shard_map/pallas_call | solution.py:497
  27.3 14.7 %all_to_all.10.sums_ref = f32[8,1,256]{2,1,0:T(1,128)S(1)} all-to-all(f32[8,1,256]{2,1,0:T(1,128)S(1)} %get-tuple-element.59), channel_id=1, replica_groups=mesh['ctx'=64,'head'=8] {'head'}, dimensions={0} | all-to-all | bytes 16384 | tf_op jit(solution)/shard_map/all_to_all | solution.py:525
  42.0 1.5 %shard_map.139 = (bf16[128,256]{1,0:T(8,128)(2,1)}, f32[64,1,256]{2,1,0:T(1,128)}, bf16[128,256]{1,0:T(8,128)(2,1)S(1)}, f32[2,128,8]{2,1,0:T(8,128)S(1)}, bf16[...) custom-call(f32[8,1,256]{2,1,0:T(1,128)S(1)} %all_to_all.10.sums_ref, ...), custom_call_target="tpu_custom_call" | custom-call | flops 125829120 | bytes 2188288 | tf_op jit(solution)/shard_map/pallas_call | solution.py:497
  43.5 2.3 %collective-permute-start.5 = (bf16[128,768]{1,0:T(8,128)(2,1)S(1)}, bf16[128,768]{1,0:T(8,128)(2,1)S(1)}, u32[]{:S(2)}, u32[]{:S(2)}) collective-permute-start(bf16[128,768]{1,0:T(8,128)(2,1)S(1)} %get-tuple-element.68), channel_id=1, source_target_pairs={{24,0},{32,8},{40,16},{48,24},{56,32},{64,40},{72,48},{80,56},{88,... | collective-permute-start | bytes 589832 | tf_op jit(solution)/shard_map/ppermute | solution.py:511
  45.8 2.0 %collective-permute-start.6 = (bf16[128,512]{1,0:T(8,128)(2,1)S(1)}, bf16[128,512]{1,0:T(8,128)(2,1)S(1)}, u32[]{:S(2)}, u32[]{:S(2)}) collective-permute-start(bf16[128,512]{1,0:T(8,128)(2,1)S(1)} %get-tuple-element.69), channel_id=1, source_target_pairs={{32,0},{40,8},{48,16},{56,24},{64,32},{72,40},{80,48},{88,56},{96,... | collective-permute-start | bytes 393224 | tf_op jit(solution)/shard_map/ppermute | solution.py:511
  47.8 17.8 %all-to-all-start.1 = ((f32[64,1,256]{2,1,0:T(1,128)}), f32[64,1,256]{2,1,0:T(1,128)S(1)}, u32[]{:S(2)}, u32[]{:S(2)}) async-start(f32[64,1,256]{2,1,0:T(1,128)} %get-tuple-element.74), calls=%async_computation.1 | async-start | bytes 131072 | tf_op jit(solution)/shard_map/all_to_all | solution.py:525
  65.6 0.9 %shard_map.140 = (bf16[2,128,256]{2,1,0:T(8,128)(2,1)S(1)}, f32[128,256]{1,0:T(8,128)S(1)}, bf16[128,768]{1,0:T(8,128)(2,1)S(1)}, bf16[128,768]{1,0:T(8,128)(2,1)S(1)}) custom-call(bf16[128,256]{1,0:T(8,128)(2,1)S(1)} %get-tuple-element.70.scaled_ref, f32[2,128,8]{2,1,0:T(8,128)S(1)} %get-tuple-element.71.delta_ref, ...), custom_call_target="tpu_custom_call" | custom-call | flops 25165824000 | bytes 2236416 | tf_op jit(solution)/shard_map/pallas_call | solution.py:497
  66.5 2.5 %collective-permute-start.7 = (bf16[128,768]{1,0:T(8,128)(2,1)S(1)}, bf16[128,768]{1,0:T(8,128)(2,1)S(1)}, u32[]{:S(2)}, u32[]{:S(2)}) collective-permute-start(bf16[128,768]{1,0:T(8,128)(2,1)S(1)} %get-tuple-element.78), channel_id=1, source_target_pairs={{8,0},{16,8},{24,16},{32,24},{40,32},{48,40},{56,48},{64,56},{72,6... | collective-permute-start | bytes 589832 | tf_op jit(solution)/shard_map/ppermute | solution.py:511
  69.0 2.5 %collective-permute-start.8 = (bf16[128,768]{1,0:T(8,128)(2,1)S(1)}, bf16[128,768]{1,0:T(8,128)(2,1)S(1)}, u32[]{:S(2)}, u32[]{:S(2)}) collective-permute-start(bf16[128,768]{1,0:T(8,128)(2,1)S(1)} %get-tuple-element.79), channel_id=1, source_target_pairs={{16,0},{24,8},{32,16},{40,24},{48,32},{56,40},{64,48},{72,56},{80,... | collective-permute-start | bytes 589832 | tf_op jit(solution)/shard_map/ppermute | solution.py:511
  71.5 2.1 %all-to-all-done.1.parts_ref = f32[64,1,256]{2,1,0:T(1,128)S(1)} async-done(((f32[64,1,256]{2,1,0:T(1,128)}), f32[64,1,256]{2,1,0:T(1,128)S(1)}, u32[]{:S(2)}, u32[]{:S(2)}) %all-to-all-start.1) | async-done | bytes 65568 | tf_op jit(solution)/shard_map/all_to_all | solution.py:525
  73.6 1.2 %shard_map.141 = (bf16[128,256]{1,0:T(8,128)(2,1)}, f32[2,128,128]{2,1,0:T(8,128)S(1)}, f32[2,128,128]{2,1,0:T(8,128)S(1)}, f32[2,128,256]{2,1,0:T(8,128)S(1)}) custom-call(bf16[2,128,256]{2,1,0:T(8,128)(2,1)S(1)} %get-tuple-element.75.own_ref, bf16[2,128,256]{2,1,0:T(8,128)(2,1)S(1)} %get-tuple-element.76.kw_ref, bf16[128,256]{1,0:T(8,128)(2,1)S(1)} %copy-done.5, ...), custom_call_target="tpu_custom_call" | custom-call | flops 1258291200 | bytes 1048576 | tf_op jit(solution)/shard_map/pallas_call | solution.py:497
  74.9 5.3 %collective-permute-done.8.recv2_ref = bf16[128,768]{1,0:T(8,128)(2,1)S(1)} collective-permute-done((bf16[128,768]{1,0:T(8,128)(2,1)S(1)}, bf16[128,768]{1,0:T(8,128)(2,1)S(1)}, u32[]{:S(2)}, u32[]{:S(2)}) %collective-permute-start.8) | collective-permute-done | bytes 196640 | tf_op jit(solution)/shard_map/ppermute | solution.py:511
  80.1 2.0 %shard_map.142 = (bf16[128,256]{1,0:T(8,128)(2,1)}, bf16[128,256]{1,0:T(8,128)(2,1)}, bf16[128,256]{1,0:T(8,128)(2,1)}, f32[2,128]{1,0:T(2,128)}, f32[1,256]{1,0:T(1,128)}) custom-call(bf16[128,768]{1,0:T(8,128)(2,1)S(1)} %collective-permute-done.7.recv1_ref, bf16[128,768]{1,0:T(8,128)(2,1)S(1)} %collective-permute-done.8.recv2_ref, ...), custom_call_target="tpu_custom_call" | custom-call | flops 167772160 | bytes 1969152 | tf_op jit(solution)/shard_map/pallas_call | solution.py:497
  (24 shorter events, 0.1 us)
Async XLA Ops:
  0.6 10.4 %copy-start.1 = (bf16[128,256]{1,0:T(8,128)(2,1)S(1)}, bf16[128,256]{1,0:T(8,128)(2,1)}, u32[]{:S(2)}) copy-start(bf16[128,256]{1,0:T(8,128)(2,1)} %dir_ref.7) | copy-start | bytes 196612
  0.6 10.3 %copy-start = (bf16[128,256]{1,0:T(8,128)(2,1)S(1)}, bf16[128,256]{1,0:T(8,128)(2,1)}, u32[]{:S(2)}) copy-start(bf16[128,256]{1,0:T(8,128)(2,1)} %key_ref.7) | copy-start | bytes 196612
  0.7 10.3 %copy-start.5 = (bf16[128,256]{1,0:T(8,128)(2,1)S(1)}, bf16[128,256]{1,0:T(8,128)(2,1)}, u32[]{:S(2)}) copy-start(bf16[128,256]{1,0:T(8,128)(2,1)} %query_ref.3) | copy-start | bytes 196612
  2.4 12.1 %collective-permute-start = (bf16[144,768]{1,0:T(8,128)(2,1)}, bf16[144,768]{1,0:T(8,128)(2,1)S(1)}, u32[]{:S(2)}, u32[]{:S(2)}) collective-permute-start(bf16[144,768]{1,0:T(8,128)(2,1)} %shard_map.135), channel_id=1, source_target_pairs={{0,16},{8,24},{16,32},{24,40},{32,48},{40,56},{48,64},{56,72},{64,... | collective-permute-start | bytes 663560 | tf_op jit(solution)/shard_map/ppermute | solution.py:511
  6.6 12.4 %collective-permute-start.2 = (bf16[144,768]{1,0:T(8,128)(2,1)}, bf16[144,768]{1,0:T(8,128)(2,1)S(1)}, u32[]{:S(2)}, u32[]{:S(2)}) collective-permute-start(bf16[144,768]{1,0:T(8,128)(2,1)} %shard_map.135), channel_id=1, source_target_pairs={{0,32},{8,40},{16,48},{24,56},{32,64},{40,72},{48,80},{56,88},{64,... | collective-permute-start | bytes 663560 | tf_op jit(solution)/shard_map/ppermute | solution.py:511
  10.9 0.7 copy-start.6
  11.0 0.7 copy-start.4
  11.0 0.7 copy-start.7
  11.7 4.8 %copy-start.8 = (bf16[144,768]{1,0:T(8,128)(2,1)S(1)}, bf16[144,768]{1,0:T(8,128)(2,1)}, u32[]{:S(2)}) copy-start(bf16[144,768]{1,0:T(8,128)(2,1)} %shard_map.135) | copy-start | bytes 663556
  14.4 8.3 %copy-start.2 = (bf16[128,256]{1,0:T(8,128)(2,1)S(1)}, bf16[128,256]{1,0:T(8,128)(2,1)}, u32[]{:S(2)}) copy-start(bf16[128,256]{1,0:T(8,128)(2,1)} %cot_ref.3) | copy-start | bytes 196612
  14.4 8.3 %copy-start.3 = (bf16[128,256]{1,0:T(8,128)(2,1)S(1)}, bf16[128,256]{1,0:T(8,128)(2,1)}, u32[]{:S(2)}) copy-start(bf16[128,256]{1,0:T(8,128)(2,1)} %value_ref.5) | copy-start | bytes 196612
  14.5 4.5 %collective-permute-start.1 = (bf16[144,768]{1,0:T(8,128)(2,1)S(1)}, bf16[144,768]{1,0:T(8,128)(2,1)S(1)}, u32[]{:S(2)}, u32[]{:S(2)}) collective-permute-start(bf16[144,768]{1,0:T(8,128)(2,1)S(1)} %collective-permute-done.halo2_ref), channel_id=1, source_target_pairs={{0,8},{8,0},{16,24},{24,16},{32,40},{40,32},{48,56},{56,48},{64,72... | collective-permute-start | bytes 663560 | tf_op jit(solution)/shard_map/ppermute | solution.py:521
  16.5 6.2 %collective-permute-start.3 = (bf16[144,768]{1,0:T(8,128)(2,1)S(1)}, bf16[144,768]{1,0:T(8,128)(2,1)S(1)}, u32[]{:S(2)}, u32[]{:S(2)}) collective-permute-start(bf16[144,768]{1,0:T(8,128)(2,1)S(1)} %copy-done.8), channel_id=1, source_target_pairs={{0,8},{16,24},{32,40},{48,56},{64,72},{80,88},{96,104},{112,120},{... | collective-permute-start | bytes 663560 | tf_op jit(solution)/shard_map/ppermute | solution.py:516
  19.0 3.8 %collective-permute-start.4 = (bf16[144,768]{1,0:T(8,128)(2,1)S(1)}, bf16[144,768]{1,0:T(8,128)(2,1)S(1)}, u32[]{:S(2)}, u32[]{:S(2)}) collective-permute-start(bf16[144,768]{1,0:T(8,128)(2,1)S(1)} %collective-permute-done.2.halo4_ref), channel_id=1, source_target_pairs={{8,0},{24,16},{40,32},{56,48},{72,64},{88,80},{104,96},{120,112},{... | collective-permute-start | bytes 663560 | tf_op jit(solution)/shard_map/ppermute | solution.py:516
  43.5 22.1 %collective-permute-start.5 = (bf16[128,768]{1,0:T(8,128)(2,1)S(1)}, bf16[128,768]{1,0:T(8,128)(2,1)S(1)}, u32[]{:S(2)}, u32[]{:S(2)}) collective-permute-start(bf16[128,768]{1,0:T(8,128)(2,1)S(1)} %get-tuple-element.68), channel_id=1, source_target_pairs={{24,0},{32,8},{40,16},{48,24},{56,32},{64,40},{72,48},{80,56},{88,... | collective-permute-start | bytes 589832 | tf_op jit(solution)/shard_map/ppermute | solution.py:511
  45.8 19.8 %collective-permute-start.6 = (bf16[128,512]{1,0:T(8,128)(2,1)S(1)}, bf16[128,512]{1,0:T(8,128)(2,1)S(1)}, u32[]{:S(2)}, u32[]{:S(2)}) collective-permute-start(bf16[128,512]{1,0:T(8,128)(2,1)S(1)} %get-tuple-element.69), channel_id=1, source_target_pairs={{32,0},{40,8},{48,16},{56,24},{64,32},{72,40},{80,48},{88,56},{96,... | collective-permute-start | bytes 393224 | tf_op jit(solution)/shard_map/ppermute | solution.py:511
  47.8 25.8 %all-to-all-start.1 = ((f32[64,1,256]{2,1,0:T(1,128)}), f32[64,1,256]{2,1,0:T(1,128)S(1)}, u32[]{:S(2)}, u32[]{:S(2)}) async-start(f32[64,1,256]{2,1,0:T(1,128)} %get-tuple-element.74), calls=%async_computation.1 | async-start | bytes 131072 | tf_op jit(solution)/shard_map/all_to_all | solution.py:525
  66.5 8.4 %collective-permute-start.7 = (bf16[128,768]{1,0:T(8,128)(2,1)S(1)}, bf16[128,768]{1,0:T(8,128)(2,1)S(1)}, u32[]{:S(2)}, u32[]{:S(2)}) collective-permute-start(bf16[128,768]{1,0:T(8,128)(2,1)S(1)} %get-tuple-element.78), channel_id=1, source_target_pairs={{8,0},{16,8},{24,16},{32,24},{40,32},{48,40},{56,48},{64,56},{72,6... | collective-permute-start | bytes 589832 | tf_op jit(solution)/shard_map/ppermute | solution.py:511
  69.0 11.1 %collective-permute-start.8 = (bf16[128,768]{1,0:T(8,128)(2,1)S(1)}, bf16[128,768]{1,0:T(8,128)(2,1)S(1)}, u32[]{:S(2)}, u32[]{:S(2)}) collective-permute-start(bf16[128,768]{1,0:T(8,128)(2,1)S(1)} %get-tuple-element.79), channel_id=1, source_target_pairs={{16,0},{24,8},{32,16},{40,24},{48,32},{56,40},{64,48},{72,56},{80,... | collective-permute-start | bytes 589832 | tf_op jit(solution)/shard_map/ppermute | solution.py:511
